TPU v7x, 512 devices: a whole 4x4x16 slice. The times are simulated.
512 devices in a mesh: tm: 32 (over z_lo, y), mp: 16 (over x, z_hi, core).
Axes of the slice: x: 4, y: 4, z: 16 (z_hi: 2, z_lo: 8; z = z_hi * 8 + z_lo), core: 2. Of those that a mesh axis runs over, the one named last changes fastest.
Arguments:
- queries: bfloat16 [6144, 4096], P('tm', 'mp'), may hold values from -8 to 8
- d_queries: bfloat16 [6144, 4096], P('tm', 'mp'), may hold values from -6 to 6
- key_rows: bfloat16 [6144, 4096], P('tm', 'mp'), may hold values from -8 to 8
- value_rows: bfloat16 [6144, 4096], P('tm', 'mp'), may hold values from -6 to 6
- d_key_rows: bfloat16 [6144, 4096], P('tm', 'mp'), may hold values from -6 to 6
- d_value_rows: bfloat16 [6144, 4096], P('tm', 'mp'), may hold values from -6 to 6
- live_flags: int32 [6144], P('tm'), may hold values from 0 to 1, as said below
- out_weight: bfloat16 [4096, 5120], P('mp'), may hold values from -1 to 1
- gate_scale: float32 [5120], P('mp'), may hold values from 0.25 to 1.75
- tokens: bfloat16 [6144, 5120], P('tm', 'mp'), may hold values from -6 to 6
- d_tokens: bfloat16 [6144, 5120], P('tm', 'mp'), may hold values from -6 to 6
Outputs:
- result: bfloat16 [6144, 5120], P('tm', 'mp')
- d_result: bfloat16 [6144, 5120], P('tm', 'mp')
Inputs may be any that keep to these rules, and one draw needn't show every extreme that they name: live_flags are equal within each aligned run of 32 tokens.
All inputs are finite; a program needn't handle non-finite values.
Results may differ from a plain program's by a relative error of at most 0.019.
Values may be sent and summed in bfloat16 or wider, within the bound.
No kernel may reach another device: no remote copies, remote signals or barrier semaphores. Data moves between devices by JAX's collectives and lax.ppermute only.
A program may use at most 128 MiB of HBM per device.

v0:
```python
import math

import jax
import jax.numpy as jnp
from jax import lax
from jax.sharding import PartitionSpec as P

HD = 128


def side_by_side(arrays, axis, dim, along):
    ends, at = ([], 0)
    for a in arrays[:-1]:
        at += a.shape[along]
        ends.append(at)
    both = jnp.concatenate(arrays, axis=along)
    return tuple(jnp.split(lax.all_gather(both, axis, axis=dim, tiled=True), ends, axis=along))


def in_one_piece(arrays, axis, dim, along):
    ends, at = ([], 0)
    for a in arrays[:-1]:
        at += a.shape[along]
        ends.append(at)
    both = jnp.concatenate(arrays, axis=along)
    return tuple(
        jnp.split(lax.psum_scatter(both, axis, scatter_dimension=dim, tiled=True), ends, axis=along)
    )


def by_heads(matrix):
    return matrix.reshape(matrix.shape[0], matrix.shape[1] // HD, HD)


def attend(running, pieces, queries_h, tangent_h):
    keys_h, values_h, dkeys_h, dvalues_h = [by_heads(matrix) for matrix in pieces]
    factor = 1.0 / math.sqrt(HD)
    scores = (
        jnp.einsum("qhd,khd->qhk", queries_h, keys_h, preferred_element_type=jnp.float32) * factor
    )
    d_scores = (
        jnp.einsum("qhd,khd->qhk", tangent_h, keys_h, preferred_element_type=jnp.float32)
        + jnp.einsum("qhd,khd->qhk", queries_h, dkeys_h, preferred_element_type=jnp.float32)
    ) * factor
    peak_old, totals, slopes, primal, tangent = running
    peak_new = jnp.max(scores, axis=2)
    rescale = jnp.exp(peak_old - peak_new)
    weights = jnp.exp(scores - peak_new[:, :, None])
    product = weights * d_scores
    weights_b = weights.astype(jnp.bfloat16)
    product_b = product.astype(jnp.bfloat16)
    totals = totals * rescale + jnp.sum(weights, axis=2)
    slopes = slopes * rescale + jnp.sum(product, axis=2)
    primal = primal * rescale[:, :, None] + jnp.einsum(
        "qhk,khd->qhd", weights_b, values_h, preferred_element_type=jnp.float32
    )
    tangent = (
        tangent * rescale[:, :, None]
        + jnp.einsum("qhk,khd->qhd", product_b, values_h, preferred_element_type=jnp.float32)
        + jnp.einsum("qhk,khd->qhd", weights_b, dvalues_h, preferred_element_type=jnp.float32)
    )
    return (peak_new, totals, slopes, primal, tangent)


def per_device(
    queries,
    d_queries,
    key_rows,
    value_rows,
    d_key_rows,
    d_value_rows,
    live_flags,
    out_weight,
    gate_scale,
    tokens,
    d_tokens,
):
    live_rows = live_flags[:, None] > 0

    def masked(matrix):
        return jnp.where(live_rows, matrix, jnp.zeros_like(matrix))

    tangent_q = masked(d_queries)
    tangent_k = masked(d_key_rows)
    tangent_v = masked(d_value_rows)
    tangent_x = masked(d_tokens)
    queries_h = by_heads(queries)
    tangent_h = by_heads(tangent_q)
    row_count = queries.shape[0]
    head_count = queries.shape[1] // HD
    initial = (
        jnp.full((row_count, head_count), -jnp.inf, jnp.float32),
        jnp.zeros((row_count, head_count), jnp.float32),
        jnp.zeros((row_count, head_count), jnp.float32),
        jnp.zeros((row_count, head_count, HD), jnp.float32),
        jnp.zeros((row_count, head_count, HD), jnp.float32),
    )
    finished = attend(
        initial,
        side_by_side((key_rows, value_rows, tangent_k, tangent_v), "tm", 0, 1),
        queries_h,
        tangent_h,
    )
    peak_new, totals, slopes, primal, tangent = finished
    outputs = primal / totals[:, :, None]
    d_outputs = tangent / totals[:, :, None] - (slopes / totals)[:, :, None] * outputs
    outputs_b = outputs.astype(jnp.bfloat16).reshape(row_count, head_count * HD)
    d_outputs_b = d_outputs.astype(jnp.bfloat16).reshape(row_count, head_count * HD)
    partial_y = jnp.dot(outputs_b, out_weight, preferred_element_type=jnp.float32)
    partial_dy = jnp.dot(d_outputs_b, out_weight, preferred_element_type=jnp.float32)
    summed, d_summed = tuple(
        (
            part.astype(jnp.float32)
            for part in in_one_piece(
                (partial_y.astype(jnp.bfloat16), partial_dy.astype(jnp.bfloat16)), "mp", 1, 0
            )
        )
    )
    result = (tokens.astype(jnp.float32) + gate_scale * summed).astype(jnp.bfloat16)
    d_result = (tangent_x.astype(jnp.float32) + gate_scale * d_summed).astype(jnp.bfloat16)
    return (result, d_result)


def solution(mesh):
    placed = (
        P("tm", "mp"),
        P("tm", "mp"),
        P("tm", "mp"),
        P("tm", "mp"),
        P("tm", "mp"),
        P("tm", "mp"),
        P("tm"),
        P("mp", None),
        P("mp"),
        P("tm", "mp"),
        P("tm", "mp"),
    )
    return jax.shard_map(
        per_device,
        mesh=mesh,
        in_specs=placed,
        out_specs=(P("tm", "mp"), P("tm", "mp")),
        check_vma=False,
    )
```

profile of v0, /device:TPU:1, one launch (start us, length us, event | category | flops | bytes accessed | tf_op | source)
XLA Modules:
  0.0 487.5 jit_solution(500588568889247541)
XLA Ops:
  7.2 0.0 copy-start
  7.2 0.0 all-gather.2.cloned.1.call-start
  7.2 0.8 broadcast_compare_fusion
  8.1 1.1 select_bitcast_fusion
  9.1 1.8 pad_maximum_fusion.1
  10.9 0.0 all-gather.2.cloned.1.call-update
  10.9 0.0 reduce-scatter.4.cloned.1.call-start
  11.0 232.9 %all-gather.2.cloned.1.call-done = bf16[6144,1024]{1,0:T(8,128)(2,1)} async-done(((bf16[192,1024]{1,0:T(8,128)(2,1)}), bf16[6144,1024]{1,0:T(8,128)(2,1)}) %all-gather.2.cloned.1.call-update) | async-done | bytes 12582928 | tf_op jit(solution)/shard_map/all_gather | solution.py:17
  243.9 9.5 %fusion.54 = (bf16[6144,256]{1,0:T(8,128)(2,1)}, bf16[6144,256]{1,0:T(8,128)(2,1)}, bf16[6144,256]{1,0:T(8,128)(2,1)}, bf16[6144,256]{1,0:T(8,128)(2,1)}) fusion(bf16[6144,1024]{1,0:T(8,128)(2,1)} %all-gather.2.cloned.1.call-done), kind=kLoop, calls=%fused_computation.47 | loop fusion | bytes 25165824 | tf_op jit(solution)/shard_map/split | solution.py:17
  253.4 4.7 copy.58
  258.1 4.7 copy.55
  262.8 3.4 bitcast_reduce_fusion
  266.2 1.5 fusion.1
  267.7 2.8 copy-done.1
  270.5 0.0 copy-done.3
  270.5 1.6 fusion.12
  272.0 4.7 copy.56
  276.7 6.9 %fusion.46 = f32[2,6144,192]{1,2,0:T(8,128)} fusion(bf16[6144,2,128]{0,2,1:T(8,128)(2,1)} %bitcast.96, bf16[24,2,8,128]{3,2,1,0:T(8,128)(2,1)S(1)} %get-tuple-element.13), kind=kOutput, calls=%fused_computation.32 | convolution fusion | flops 603979776 | bytes 12681216 | tf_op jit(solution)/shard_map/qhd,khd->qhk/dot_general | solution.py:42
  283.7 4.7 copy.57
  288.3 10.6 %fusion.56 = (f32[192,2]{0,1:T(2,128)S(1)}, bf16[192,2,6144]{2,0,1:T(8,128)(2,1)S(1)}) fusion(f32[2,6144,192]{1,2,0:T(8,128)} %fusion.46, bf16[6144,2,128]{0,2,1:T(8,128)(2,1)} %bitcast.99, f32[192,2]{0,1:T(2,128)S(1)} %get-tuple-element.16, f32[2,6144,192]{1,2,0:T(8,128)} %copy-done.1, bf16[192,256]{1,0:T(8,128)(2,1)S(1)} %copy-done.4), kind=kOutput, calls=%fused_computation.49 | convolution fusion | flops 618135168 | bytes 26840064 | tf_op jit(solution)/shard_map/qhd,khd->qhk/dot_general | solution.py:43
  298.9 5.5 %fusion.39 = f32[192,2,128]{2,0,1:T(8,128)S(1)} fusion(bf16[6144,2,128]{0,2,1:T(8,128)(2,1)S(1)} %bitcast.93, f32[2,6144,192]{1,2,0:T(8,128)} %copy-done.1, f32[192,2]{0,1:T(2,128)S(1)} %get-tuple-element.16, f32[192,2]{0,1:T(2,128)S(1)} %get-tuple-element.9, f32[192,2]{0,1:T(2,128)S(1)} %get-tuple-element.12), kind=kOutput, calls=%fused_computation.24 | convolution fusion | flops 608796672 | bytes 12784128 | tf_op jit(solution)/shard_map/qhk,khd->qhd/dot_general | solution.py:54
  304.4 0.7 convolution_convert_fusion.1
  305.1 1.4 fusion.36
  306.5 0.7 convolution_convert_fusion
  307.2 2.1 pad_maximum_fusion
  309.4 6.3 %copy.53 = bf16[384,5120]{0,1:T(8,128)(2,1)} copy(bf16[384,5120]{1,0:T(8,128)(2,1)} %pad_maximum_fusion) | data formatting | bytes 7864320
  315.7 0.0 reduce-scatter.4.cloned.1.call-update
  315.7 162.7 %reduce-scatter.4.cloned.1.call-done = bf16[320,384]{1,0:T(8,128)(2,1)} async-done(((bf16[5120,384]{1,0:T(8,128)(2,1)}), bf16[320,384]{1,0:T(8,128)(2,1)}) %reduce-scatter.4.cloned.1.call-update) | async-done | bytes 245776
  478.4 1.1 fusion.55
  479.5 0.1 copy.60
  479.7 0.1 copy.59
  479.9 0.8 add_convert_fusion
  (14 shorter events, 0.0 us)
Async XLA Ops:
  7.2 297.2 %copy-start = (bf16[256,5120]{1,0:T(8,128)(2,1)S(1)}, bf16[256,5120]{1,0:T(8,128)(2,1)}, u32[]{:S(2)}) copy-start(bf16[256,5120]{1,0:T(8,128)(2,1)} %param.18) | copy-start | bytes 7864324
  7.2 236.7 %all-gather.2.cloned.1.call-start = ((), (), s32[]{:S(2)}) async-start(), calls=%async_computation.1 | async-start | bytes 12976128 | tf_op jit(solution)/shard_map/all_gather | solution.py:17
  10.9 467.5 %reduce-scatter.4.cloned.1.call-start = ((), (), s32[]{:S(2)}) async-start(), calls=%async_computation.2 | async-start | bytes 4177920
  258.1 4.7 copy-start.4
  266.2 4.3 copy-start.1
  266.2 4.3 copy-start.3
  288.3 10.6 %copy-start.2 = (bf16[6144,256]{0,1:T(8,128)(2,1)S(1)}, bf16[6144,256]{0,1:T(8,128)(2,1)}, u32[]{:S(2)}) copy-start(bf16[6144,256]{0,1:T(8,128)(2,1)} %copy.56) | copy-start | bytes 9437188
  315.7 164.2 %copy-start.5 = (bf16[192,320]{1,0:T(8,128)(2,1)S(1)}, bf16[192,320]{1,0:T(8,128)(2,1)}, u32[]{:S(2)}) copy-start(bf16[192,320]{1,0:T(8,128)(2,1)} %param.21) | copy-start | bytes 368644
  315.7 164.2 %copy-start.6 = (bf16[192,320]{1,0:T(8,128)(2,1)S(1)}, bf16[192,320]{1,0:T(8,128)(2,1)}, u32[]{:S(2)}) copy-start(bf16[192,320]{1,0:T(8,128)(2,1)} %param.20) | copy-start | bytes 368644
  315.7 164.2 %copy-start.7 = (f32[320]{0:T(512)S(1)}, f32[320]{0:T(512)}, u32[]{:S(2)}) copy-start(f32[320]{0:T(512)} %param.19) | copy-start | bytes 3844
Sparse Core Ops, SparseCore 0:
  11.1 232.7 all-gather.1
  315.8 162.5 reduce-scatter.3
where the time goes:
time: 489 us; the launch traced here: 488 us
  waiting for transfers between devices  396 us (81%)
  local copies, waits for them, and re-layouts  38.8 us (8%)
  matrix products  30.7 us (6%)
  between operations  14.2 us (3%)
  other arithmetic  8.09 us (2%)
    all_gather x1, waiting for transfers between devices, side_by_side(): lax.all_gather(both, axis, axis=dim, tiled=True)  233 us
    unnamed x3, waiting for transfers between devices  163 us
    unnamed x23, local copies, waits for them, and re-layouts  28.2 us
    dot_general x1, matrix products, attend(): jnp.einsum('qhd,khd->qhk', queries_h, dkeys_h, preferred_element_type=jnp...  10.6 us
  transfers between devices with their start and end apart: 2, of which 2 were waited for; matrix products, arithmetic and copies ran while one was open for 0% of the time, Pallas kernels for 0%

commit v1 on v0

v1 whole, which is shorter than its diff:
```python
import functools
import math

import jax
import jax.numpy as jnp
from jax import lax
from jax.experimental import pallas as pl
from jax.experimental.pallas import tpu as pltpu
from jax.sharding import PartitionSpec as P

HD = 128
FRAME = 32
NZ, NY, NX = 8, 4, 4
FACTOR = 1.0 / math.sqrt(HD)
LOG2E = math.log2(math.e)
STAT_ROWS = 16
BF = jnp.bfloat16
F32 = jnp.float32
VMEM_LIMIT = 44 * 1024 * 1024


def params():
    return pltpu.CompilerParams(vmem_limit_bytes=VMEM_LIMIT)


SMEM_SPEC = pl.BlockSpec(memory_space=pltpu.SMEM)
VMEM_SPEC = pl.BlockSpec(memory_space=pltpu.VMEM)
ANY_SPEC = pl.BlockSpec(memory_space=pl.ANY)


def over_z(k):
    return [(z * NY + y, (z ^ k) * NY + y) for z in range(NZ) for y in range(NY)]


def over_y(k):
    return [(z * NY + y, z * NY + (y + k) % NY) for z in range(NZ) for y in range(NY)]


def over_x(k):
    return [(x * 4 + r, (x + k) % NX * 4 + r) for x in range(NX) for r in range(4)]


def over_half():
    return [(i, i ^ 2) for i in range(4 * NX)]


def over_core():
    return [(i, i ^ 1) for i in range(4 * NX)]


def pack_kernel(odd, flags, q, dq, k, v, dk, dv, qd_own, qd_other, kv_own, kv_other):
    is_odd = odd[0] > 0
    for f in range(q.shape[0] // FRAME):
        rows = pl.ds(f * FRAME, FRAME)
        live = flags[f * FRAME] > 0

        def masked(ref):
            block = ref[rows, :]
            return jnp.where(live, block, jnp.zeros_like(block))

        blocks = (masked(dq), q[rows, :], k[rows, :], masked(dk), v[rows, :], masked(dv))
        for i, block in enumerate(blocks):
            first, second = block[:, :HD], block[:, HD:]
            own = jnp.where(is_odd, second, first)
            other = jnp.where(is_odd, first, second)
            if i < 2:
                at = slice(i * HD, (i + 1) * HD)
                qd_own[rows, at] = own
                qd_other[rows, at] = other
            else:
                at = slice((i - 2) * HD, (i - 1) * HD)
                kv_own[rows, at] = own
                kv_other[rows, at] = other


def in_three(value):
    high = value.astype(BF).astype(F32)
    middle = (value - high).astype(BF).astype(F32)
    low = (value - high - middle).astype(BF).astype(F32)
    return high, middle, low


def attend_kernel(pieces, *refs):
    kv_in, qd_in, outs = refs[:8], refs[8:16], refs[16:24]
    kv, qd, held, sems = refs[24:]
    rows = qd_in[0].shape[0]
    copies = []
    for i in range(8):
        at = pl.ds(i * rows, rows)
        copies.append(pltpu.make_async_copy(kv_in[i], kv.at[at], sems.at[i]))
        copies.append(pltpu.make_async_copy(qd_in[i], qd.at[at], sems.at[8 + i]))
    for copy in copies:
        copy.start()
    for copy in copies:
        copy.wait()
    count = rows * pieces
    contract = (((1,), (1,)), ((), ()))

    def step(j, carry):
        at = pl.ds(pl.multiple_of(j * count, count), count)
        both = qd[at, :]
        scores = lax.dot_general(both[:, HD:], kv[:, :HD], contract, preferred_element_type=F32)
        slopes = lax.dot_general(both, kv[:, : 2 * HD], contract, preferred_element_type=F32)
        scores = scores * (FACTOR * LOG2E)
        peak = jnp.max(scores, axis=1, keepdims=True)
        weights = jnp.exp2(scores - peak)
        total = jnp.sum(weights, axis=1, keepdims=True)
        product = weights * slopes
        slope = jnp.sum(product, axis=1, keepdims=True)
        weighted = jnp.dot(weights.astype(BF), kv[:, 2 * HD :], preferred_element_type=F32)
        tangent = jnp.dot(product.astype(BF), kv[:, 2 * HD : 3 * HD], preferred_element_type=F32)
        inverse = 1.0 / total
        mean = slope * (inverse * FACTOR)
        primal = weighted[:, :HD] * inverse
        tangent = (tangent * FACTOR + weighted[:, HD:]) * inverse - mean * primal
        lanes = lax.broadcasted_iota(jnp.int32, (count, HD), 1)
        stats = jnp.zeros((count, HD), F32)
        for i, part in enumerate(in_three(peak + jnp.log2(total)) + in_three(mean)):
            stats = jnp.where(lanes == i, part, stats)
        for p in range(pieces):
            mine = slice(p * rows, (p + 1) * rows)
            held[j * pieces + p, :rows, :HD] = primal[mine].astype(BF)
            held[j * pieces + p, :rows, HD:] = tangent[mine].astype(BF)
            tile = jnp.concatenate([stats[mine], jnp.zeros((2 * HD - rows, HD), F32)], axis=0)
            held[j * pieces + p, rows:, :] = tile.T[:STAT_ROWS].astype(BF)
        return carry

    lax.fori_loop(0, 8 // pieces, step, 0)
    back = [pltpu.make_async_copy(held.at[i], outs[i], sems.at[i]) for i in range(8)]
    for copy in back:
        copy.start()
    for copy in back:
        copy.wait()


def merge_kernel(place, *refs):
    parts, (keep, send) = refs[:8], refs[8:]
    rows = keep.shape[0]
    stats = jnp.concatenate([part[rows:, :] for part in parts], axis=0).astype(F32).T[:rows]

    def value(i, first):
        at = i * STAT_ROWS + first
        return stats[:, at : at + 1] + stats[:, at + 1 : at + 2] + stats[:, at + 2 : at + 3]

    merged = []
    for parity in range(2):
        group = range(parity, 8, 2)
        sizes = [value(i, 0) for i in group]
        means = [value(i, 3) for i in group]
        peak = functools.reduce(jnp.maximum, sizes)
        sizes = [jnp.exp2(size - peak) for size in sizes]
        inverse = 1.0 / sum(sizes)
        sizes = [size * inverse for size in sizes]
        mean = sum(size * m for size, m in zip(sizes, means))
        primal = jnp.zeros((rows, HD), F32)
        tangent = jnp.zeros((rows, HD), F32)
        for i, size, m in zip(group, sizes, means):
            a = parts[i][:rows, :HD].astype(F32)
            primal += size * a
            tangent += size * parts[i][:rows, HD:].astype(F32) + (size * (m - mean)) * a
        merged.append((primal.astype(BF), tangent.astype(BF)))
    odd = place[0] > 0
    core = place[1] > 0
    (own_p, own_t), (other_p, other_t) = merged
    for h, (p, t) in enumerate(
        (
            (jnp.where(odd, other_p, own_p), jnp.where(odd, other_t, own_t)),
            (jnp.where(odd, own_p, other_p), jnp.where(odd, own_t, other_t)),
        )
    ):
        at = slice(h * HD, (h + 1) * HD)
        keep[:, at] = jnp.where(core, t, p)
        send[:, at] = jnp.where(core, p, t)


def project_kernel(half, *refs):
    acts, w_own, w_other, (mine, theirs) = refs[:4], refs[4:8], refs[8:12], refs[12:]
    width = mine.shape[1]
    depth = w_own[0].shape[0]
    for second in range(2):
        at = slice(second * width, (second + 1) * width)
        total = jnp.zeros(mine.shape, F32)
        for i in range(4):
            total += jnp.dot(acts[i][:, :depth], w_own[i][:, at], preferred_element_type=F32)
            total += jnp.dot(acts[i][:, depth:], w_other[i][:, at], preferred_element_type=F32)

        @pl.when(half[0] == second)
        def _():
            mine[...] = total

        @pl.when(half[0] != second)
        def _():
            theirs[...] = total.astype(BF)


def add_kernel(core, mine, theirs, keep, send):
    total = (mine[...] + theirs[...].astype(F32)).astype(BF)
    width = keep.shape[1]
    first, second = total[:, :width], total[:, width:]
    is_second = core[0] > 0
    keep[...] = jnp.where(is_second, second, first)
    send[...] = jnp.where(is_second, first, second)


def finish_kernel(core, flags, keep, got, gate, tokens, d_tokens, result, d_result):
    is_second = core[0] > 0
    scale = gate[...]
    for f in range(tokens.shape[0] // FRAME):
        rows = pl.ds(f * FRAME, FRAME)
        live = flags[f * FRAME] > 0
        kept, other = keep[rows, :].astype(F32), got[rows, :].astype(F32)
        primal = jnp.where(is_second, other, kept)
        tangent = jnp.where(is_second, kept, other)
        base = tokens[rows, :].astype(F32)
        d_base = d_tokens[rows, :].astype(F32)
        d_base = jnp.where(live, d_base, jnp.zeros_like(d_base))
        result[rows, :] = (base + scale * primal).astype(BF)
        d_result[rows, :] = (d_base + scale * tangent).astype(BF)


def per_device(
    queries,
    d_queries,
    key_rows,
    value_rows,
    d_key_rows,
    d_value_rows,
    live_flags,
    out_weight,
    gate_scale,
    tokens,
    d_tokens,
):
    rows, width = queries.shape
    columns = tokens.shape[1]
    t, m = lax.axis_index("tm"), lax.axis_index("mp")
    odd = (t // NY % 2).astype(jnp.int32).reshape(1)
    core = (m % 2).astype(jnp.int32).reshape(1)
    half = (m // 2 % 2).astype(jnp.int32).reshape(1)
    x = m // 4

    def shape(r, c, dtype=BF):
        return jax.ShapeDtypeStruct((r, c), dtype)

    qd_own, qd_other, kv_own, kv_other = pl.pallas_call(
        pack_kernel,
        out_shape=[shape(rows, 2 * HD)] * 2 + [shape(rows, 4 * HD)] * 2,
        in_specs=[SMEM_SPEC] * 2 + [VMEM_SPEC] * 6,
        out_specs=[VMEM_SPEC] * 4,
        compiler_params=params(),
        name="pack",
    )(odd, live_flags, queries, d_queries, key_rows, value_rows, d_key_rows, d_value_rows)

    def z(a, k):
        return lax.ppermute(a, "tm", over_z(k))

    def y(a, k):
        return lax.ppermute(a, "tm", over_y(k))

    kv_got = z(kv_other, 1)
    kv = [kv_own] + [y(kv_own, k) for k in (1, 3, 2)]
    kv += [kv_got] + [y(kv_got, k) for k in (1, 3, 2)]
    qd = [qd_own] + [z(qd_other if k % 2 else qd_own, k) for k in range(1, 8)]

    part = shape(rows + STAT_ROWS, 2 * HD)
    parts = pl.pallas_call(
        functools.partial(attend_kernel, 2),
        out_shape=[part] * 8,
        in_specs=[ANY_SPEC] * 16,
        out_specs=[ANY_SPEC] * 8,
        scratch_shapes=[
            pltpu.VMEM((8 * rows, 4 * HD), BF),
            pltpu.VMEM((8 * rows, 2 * HD), BF),
            pltpu.VMEM((8, rows + STAT_ROWS, 2 * HD), BF),
            pltpu.SemaphoreType.DMA((16,)),
        ],
        compiler_params=params(),
        name="attend",
    )(*kv, *qd)
    parts = [parts[0]] + [z(parts[k], k) for k in range(1, 8)]

    group = 4 * columns
    w_own = []
    for k in range(4):
        piece = lax.dynamic_slice(out_weight, (0, (x + k) % NX * group), (width, group))
        w_own.append(lax.ppermute(piece, "mp", over_x(k)) if k else piece)
    w_other = [lax.ppermute(piece, "mp", over_core()) for piece in w_own]

    keep, send = pl.pallas_call(
        merge_kernel,
        out_shape=[shape(rows, 2 * HD)] * 2,
        in_specs=[SMEM_SPEC] + [VMEM_SPEC] * 8,
        out_specs=[VMEM_SPEC] * 2,
        compiler_params=params(),
        name="merge",
    )(jnp.concatenate([odd, core]), *parts)
    act = jnp.concatenate([keep, lax.ppermute(send, "mp", over_core())], axis=1)
    acts = [act] + [lax.ppermute(act, "mp", over_x(k)) for k in (1, 2, 3)]

    mine, theirs = pl.pallas_call(
        project_kernel,
        out_shape=[shape(rows, 2 * columns, F32), shape(rows, 2 * columns)],
        in_specs=[SMEM_SPEC] + [VMEM_SPEC] * 12,
        out_specs=[VMEM_SPEC] * 2,
        compiler_params=params(),
        name="project",
    )(half, *acts, *w_own, *w_other)
    theirs = lax.ppermute(theirs, "mp", over_half())

    keep, send = pl.pallas_call(
        add_kernel,
        out_shape=[shape(rows, columns)] * 2,
        in_specs=[SMEM_SPEC] + [VMEM_SPEC] * 2,
        out_specs=[VMEM_SPEC] * 2,
        compiler_params=params(),
        name="add",
    )(core, mine, theirs)
    got = lax.ppermute(send, "mp", over_core())

    result, d_result = pl.pallas_call(
        finish_kernel,
        out_shape=[shape(rows, columns)] * 2,
        in_specs=[SMEM_SPEC] * 2 + [VMEM_SPEC] * 5,
        out_specs=[VMEM_SPEC] * 2,
        compiler_params=params(),
        name="finish",
    )(core, live_flags, keep, got, gate_scale.reshape(1, columns), tokens, d_tokens)
    return (result, d_result)


def solution(mesh):
    placed = (
        P("tm", "mp"),
        P("tm", "mp"),
        P("tm", "mp"),
        P("tm", "mp"),
        P("tm", "mp"),
        P("tm", "mp"),
        P("tm"),
        P("mp", None),
        P("mp"),
        P("tm", "mp"),
        P("tm", "mp"),
    )
    return jax.shard_map(
        per_device,
        mesh=mesh,
        in_specs=placed,
        out_specs=(P("tm", "mp"), P("tm", "mp")),
        check_vma=False,
    )
```

time: 489 us -> 248 us (0.51)
  waiting for transfers between devices: 396 us -> 56.3 us
  starting transfers between devices: 0.08 us -> 148 us
  matrix products: 30.7 us -> 0 us
  Pallas kernels: 0 us -> 20.8 us
  local copies, waits for them, and re-layouts: 38.8 us -> 19.6 us
  between operations: 14.2 us -> 1.43 us
  other arithmetic: 8.09 us -> 0.08 us
    all_gather x1 -> x0, waiting for transfers between devices: 233 us -> none  [side_by_side(): lax.all_gather(both, axis, axis=dim, tiled=True)]
    unnamed x3 -> x0, waiting for transfers between devices: 163 us -> none
    ppermute x0 -> x34, starting transfers between devices: none -> 148 us  [the longest x15 68.2 us: z(): return lax.ppermute(a, 'tm', over_z(k))]
    ppermute x0 -> x34, waiting for transfers between devices: none -> 56.3 us  [the longest x1 19.4 us: per_device(): theirs = lax.ppermute(theirs, 'mp', over_half())]
    dot_general x8 -> x0, matrix products: 30.7 us -> none  [the longest x1 10.6 us: attend(): jnp.einsum('qhd,khd->qhk', queries_h, dkeys_h, preferred_element_type=jnp...]
    pallas_call x0 -> x6, Pallas kernels: none -> 20.8 us  [the longest x1 12.7 us: per_device(): pl.pallas_call(functools.partial(attend_kernel, 2), out_shape=[part] * 8,...]
    unnamed x23 -> x61, local copies, waits for them, and re-layouts: 28.2 us -> 16.6 us
    split x2 -> x0, local copies, waits for them, and re-layouts: 10.6 us -> none  [the longest x1 9.48 us: side_by_side(): jnp.split(lax.all_gather(both, axis, axis=dim, tiled=True), ends, axis=al...]
  transfers between devices with their start and end apart: 2 -> 34, of which waited for: 2 -> 11; matrix products, arithmetic and copies ran while one was open for 0% -> 1% of each run, Pallas kernels for 0% -> 6%
where the time goes in v1:
time: 248 us; the launch traced here: 246 us
  starting transfers between devices  148 us (60%)
  waiting for transfers between devices  56.3 us (23%)
  Pallas kernels  20.8 us (8%)
  local copies, waits for them, and re-layouts  19.6 us (8%)
    ppermute x15, starting transfers between devices, z(): return lax.ppermute(a, 'tm', over_z(k))  68.2 us
    ppermute x4, starting transfers between devices, per_device(): w_other = [lax.ppermute(piece, 'mp', over_core()) for piece in w_own]  25.7 us
    ppermute x6, starting transfers between devices, y(): return lax.ppermute(a, 'tm', over_y(k))  21.3 us
    ppermute x1, waiting for transfers between devices, per_device(): theirs = lax.ppermute(theirs, 'mp', over_half())  19.4 us
    ppermute x15, waiting for transfers between devices, z(): return lax.ppermute(a, 'tm', over_z(k))  16.7 us
    unnamed x61, local copies, waits for them, and re-layouts  16.6 us
    ppermute x3, waiting for transfers between devices, per_device(): acts = [act] + [lax.ppermute(act, 'mp', over_x(k)) for k in (1, 2, 3)]  13.8 us
    pallas_call x1, Pallas kernels, per_device(): pl.pallas_call(functools.partial(attend_kernel, 2), out_shape=[part] * 8,...  12.7 us
  transfers between devices with their start and end apart: 34, of which 11 were waited for; matrix products, arithmetic and copies ran while one was open for 1% of the time, Pallas kernels for 6%

profile of v1, /device:TPU:1, one launch (start us, length us, event | category | flops | bytes accessed | tf_op | source)
XLA Modules:
  0.0 246.0 jit_solution(3311189381648361334)
XLA Ops:
  7.3 4.4 %collective-permute-start.7 = (bf16[192,256]{1,0:T(8,128)(2,1)S(1)}, bf16[192,256]{1,0:T(8,128)(2,1)S(1)}, u32[]{:S(2)}, u32[]{:S(2)}) collective-permute-start(bf16[192,256]{1,0:T(8,128)(2,1)S(1)} %get-tuple-element.23), channel_id=1, source_target_pairs={{0,64},{16,80},{32,96},{48,112},{64,0},{80,16},{96,32},{112,48},{1... | collective-permute-start | bytes 294920 | tf_op jit(solution)/shard_map/ppermute | solution.py:255
  11.7 4.9 %collective-permute-start.8 = (bf16[192,256]{1,0:T(8,128)(2,1)S(1)}, bf16[192,256]{1,0:T(8,128)(2,1)S(1)}, u32[]{:S(2)}, u32[]{:S(2)}) collective-permute-start(bf16[192,256]{1,0:T(8,128)(2,1)S(1)} %get-tuple-element.22.refs_8_), channel_id=1, source_target_pairs={{0,128},{16,144},{32,160},{48,176},{64,192},{80,208},{96,224},{112... | collective-permute-start | bytes 294920 | tf_op jit(solution)/shard_map/ppermute | solution.py:255
  18.6 3.1 %collective-permute-start.9 = (bf16[192,256]{1,0:T(8,128)(2,1)S(1)}, bf16[192,256]{1,0:T(8,128)(2,1)S(1)}, u32[]{:S(2)}, u32[]{:S(2)}) collective-permute-start(bf16[192,256]{1,0:T(8,128)(2,1)S(1)} %get-tuple-element.23), channel_id=1, source_target_pairs={{0,192},{16,208},{32,224},{48,240},{64,128},{80,144},{96,160},{112... | collective-permute-start | bytes 294920 | tf_op jit(solution)/shard_map/ppermute | solution.py:255
  21.7 8.8 %collective-permute-start.10 = (bf16[192,256]{1,0:T(8,128)(2,1)S(1)}, bf16[192,256]{1,0:T(8,128)(2,1)S(1)}, u32[]{:S(2)}, u32[]{:S(2)}) collective-permute-start(bf16[192,256]{1,0:T(8,128)(2,1)S(1)} %get-tuple-element.22.refs_8_), channel_id=1, source_target_pairs={{0,256},{16,272},{32,288},{48,304},{64,320},{80,336},{96,352},{112... | collective-permute-start | bytes 294920 | tf_op jit(solution)/shard_map/ppermute | solution.py:255
  32.4 8.2 %collective-permute-start.12 = (bf16[192,256]{1,0:T(8,128)(2,1)S(1)}, bf16[192,256]{1,0:T(8,128)(2,1)S(1)}, u32[]{:S(2)}, u32[]{:S(2)}) collective-permute-start(bf16[192,256]{1,0:T(8,128)(2,1)S(1)} %get-tuple-element.22.refs_8_), channel_id=1, source_target_pairs={{0,384},{16,400},{32,416},{48,432},{64,448},{80,464},{96,480},{112... | collective-permute-start | bytes 294920 | tf_op jit(solution)/shard_map/ppermute | solution.py:255
  40.7 3.2 %collective-permute-start = (bf16[192,512]{1,0:T(8,128)(2,1)S(1)}, bf16[192,512]{1,0:T(8,128)(2,1)S(1)}, u32[]{:S(2)}, u32[]{:S(2)}) collective-permute-start(bf16[192,512]{1,0:T(8,128)(2,1)S(1)} %get-tuple-element.20.refs_0_), channel_id=1, source_target_pairs={{0,16},{16,32},{32,48},{48,0},{64,80},{80,96},{96,112},{112,64},{1... | collective-permute-start | bytes 589832 | tf_op jit(solution)/shard_map/ppermute | solution.py:258
  44.6 3.3 %collective-permute-start.1 = (bf16[192,512]{1,0:T(8,128)(2,1)S(1)}, bf16[192,512]{1,0:T(8,128)(2,1)S(1)}, u32[]{:S(2)}, u32[]{:S(2)}) collective-permute-start(bf16[192,512]{1,0:T(8,128)(2,1)S(1)} %get-tuple-element.20.refs_0_), channel_id=1, source_target_pairs={{0,48},{16,0},{32,16},{48,32},{64,112},{80,64},{96,80},{112,96},{1... | collective-permute-start | bytes 589832 | tf_op jit(solution)/shard_map/ppermute | solution.py:258
  51.0 4.8 %collective-permute-start.2 = (bf16[192,512]{1,0:T(8,128)(2,1)S(1)}, bf16[192,512]{1,0:T(8,128)(2,1)S(1)}, u32[]{:S(2)}, u32[]{:S(2)}) collective-permute-start(bf16[192,512]{1,0:T(8,128)(2,1)S(1)} %get-tuple-element.20.refs_0_), channel_id=1, source_target_pairs={{0,32},{16,48},{32,0},{48,16},{64,96},{80,112},{96,64},{112,80},{1... | collective-permute-start | bytes 589832 | tf_op jit(solution)/shard_map/ppermute | solution.py:258
  56.5 14.1 %collective-permute-start.13 = (bf16[192,256]{1,0:T(8,128)(2,1)S(1)}, bf16[192,256]{1,0:T(8,128)(2,1)S(1)}, u32[]{:S(2)}, u32[]{:S(2)}) collective-permute-start(bf16[192,256]{1,0:T(8,128)(2,1)S(1)} %get-tuple-element.23), channel_id=1, source_target_pairs={{0,448},{16,464},{32,480},{48,496},{64,384},{80,400},{96,416},{112... | collective-permute-start | bytes 294920 | tf_op jit(solution)/shard_map/ppermute | solution.py:255
  70.6 2.7 %collective-permute-start.4 = (bf16[192,512]{1,0:T(8,128)(2,1)S(1)}, bf16[192,512]{1,0:T(8,128)(2,1)S(1)}, u32[]{:S(2)}, u32[]{:S(2)}) collective-permute-start(bf16[192,512]{1,0:T(8,128)(2,1)S(1)} %collective-permute-done.3.refs_4_), channel_id=1, source_target_pairs={{0,16},{16,32},{32,48},{48,0},{64,80},{80,96},{96,112},{112,64},{1... | collective-permute-start | bytes 589832 | tf_op jit(solution)/shard_map/ppermute | solution.py:258
  73.4 3.1 %constant_dynamic-slice_fusion = (bf16[256,1280]{1,0:T(8,128)(2,1)}, bf16[256,1280]{1,0:T(8,128)(2,1)}, bf16[256,1280]{1,0:T(8,128)(2,1)S(1)}, bf16[256,1280]{1,0:T(8,128)(2,1)}) fusion(bf16[256,5120]{1,0:T(8,128)(2,1)} %param.18, s32[]{:T(128)S(6)} %select_n.66, s32[]{:T(128)S(6)} %select_n.62, s32[]{:T(128)S(6)} %select_n.60, s32[]{:T(128)S(6)} %select_n.64), kind=kLoop, calls=%fused_computation.2 | loop fusion | bytes 5242896 | tf_op jit(solution)/shard_map/dynamic_slice | solution.py:285
  76.4 3.1 %collective-permute-start.25 = (bf16[256,1280]{1,0:T(8,128)(2,1)}, bf16[256,1280]{1,0:T(8,128)(2,1)S(1)}, u32[]{:S(2)}, u32[]{:S(2)}) collective-permute-start(bf16[256,1280]{1,0:T(8,128)(2,1)} %get-tuple-element.39), channel_id=1, source_target_pairs={{0,4},{1,5},{2,6},{3,7},{4,8},{5,9},{6,10},{7,11},{8,12},{9,13},{1... | collective-permute-start | bytes 1966088 | tf_op jit(solution)/shard_map/ppermute | solution.py:286
  79.6 4.4 %collective-permute-start.26 = (bf16[256,1280]{1,0:T(8,128)(2,1)}, bf16[256,1280]{1,0:T(8,128)(2,1)S(1)}, u32[]{:S(2)}, u32[]{:S(2)}) collective-permute-start(bf16[256,1280]{1,0:T(8,128)(2,1)} %get-tuple-element.41), channel_id=1, source_target_pairs={{0,8},{1,9},{2,10},{3,11},{4,12},{5,13},{6,14},{7,15},{8,0},{9,1},... | collective-permute-start | bytes 1966088 | tf_op jit(solution)/shard_map/ppermute | solution.py:286
  83.9 3.1 %collective-permute-start.27 = (bf16[256,1280]{1,0:T(8,128)(2,1)}, bf16[256,1280]{1,0:T(8,128)(2,1)S(1)}, u32[]{:S(2)}, u32[]{:S(2)}) collective-permute-start(bf16[256,1280]{1,0:T(8,128)(2,1)} %get-tuple-element.38), channel_id=1, source_target_pairs={{0,12},{1,13},{2,14},{3,15},{4,0},{5,1},{6,2},{7,3},{8,4},{9,5},{1... | collective-permute-start | bytes 1966088 | tf_op jit(solution)/shard_map/ppermute | solution.py:286
  87.0 3.9 %collective-permute-start.5 = (bf16[192,512]{1,0:T(8,128)(2,1)S(1)}, bf16[192,512]{1,0:T(8,128)(2,1)S(1)}, u32[]{:S(2)}, u32[]{:S(2)}) collective-permute-start(bf16[192,512]{1,0:T(8,128)(2,1)S(1)} %collective-permute-done.3.refs_4_), channel_id=1, source_target_pairs={{0,48},{16,0},{32,16},{48,32},{64,112},{80,64},{96,80},{112,96},{1... | collective-permute-start | bytes 589832 | tf_op jit(solution)/shard_map/ppermute | solution.py:258
  90.9 3.3 %collective-permute-start.6 = (bf16[192,512]{1,0:T(8,128)(2,1)S(1)}, bf16[192,512]{1,0:T(8,128)(2,1)S(1)}, u32[]{:S(2)}, u32[]{:S(2)}) collective-permute-start(bf16[192,512]{1,0:T(8,128)(2,1)S(1)} %collective-permute-done.3.refs_4_), channel_id=1, source_target_pairs={{0,32},{16,48},{32,0},{48,16},{64,96},{80,112},{96,64},{112,80},{1... | collective-permute-start | bytes 589832 | tf_op jit(solution)/shard_map/ppermute | solution.py:258
  94.3 4.6 %collective-permute-done.6.refs_7_ = bf16[192,512]{1,0:T(8,128)(2,1)S(1)} collective-permute-done((bf16[192,512]{1,0:T(8,128)(2,1)S(1)}, bf16[192,512]{1,0:T(8,128)(2,1)S(1)}, u32[]{:S(2)}, u32[]{:S(2)}) %collective-permute-start.6) | collective-permute-done | bytes 196640 | tf_op jit(solution)/shard_map/ppermute | solution.py:258
  99.7 12.7 %attend.1 = (bf16[208,256]{1,0:T(8,128)(2,1)S(1)}, bf16[208,256]{1,0:T(8,128)(2,1)S(1)}, bf16[208,256]{1,0:T(8,128)(2,1)S(1)}, bf16[208,256]{1,0:T(8,128)(2,1)S(...) custom-call(bf16[192,512]{1,0:T(8,128)(2,1)S(1)} %get-tuple-element., ...), custom_call_target="tpu_custom_call" | custom-call | tf_op jit(solution)/shard_map/attend/pallas_call | solution.py:266
  117.9 3.8 %collective-permute-start.16 = (bf16[208,256]{1,0:T(8,128)(2,1)S(1)}, bf16[208,256]{1,0:T(8,128)(2,1)S(1)}, u32[]{:S(2)}, u32[]{:S(2)}) collective-permute-start(bf16[208,256]{1,0:T(8,128)(2,1)S(1)} %get-tuple-element.27), channel_id=1, source_target_pairs={{0,192},{16,208},{32,224},{48,240},{64,128},{80,144},{96,160},{112... | collective-permute-start | bytes 319496 | tf_op jit(solution)/shard_map/ppermute | solution.py:255
  122.4 3.2 %collective-permute-start.17 = (bf16[208,256]{1,0:T(8,128)(2,1)S(1)}, bf16[208,256]{1,0:T(8,128)(2,1)S(1)}, u32[]{:S(2)}, u32[]{:S(2)}) collective-permute-start(bf16[208,256]{1,0:T(8,128)(2,1)S(1)} %get-tuple-element.28), channel_id=1, source_target_pairs={{0,256},{16,272},{32,288},{48,304},{64,320},{80,336},{96,352},{112... | collective-permute-start | bytes 319496 | tf_op jit(solution)/shard_map/ppermute | solution.py:255
  126.3 6.1 %collective-permute-start.18 = (bf16[208,256]{1,0:T(8,128)(2,1)S(1)}, bf16[208,256]{1,0:T(8,128)(2,1)S(1)}, u32[]{:S(2)}, u32[]{:S(2)}) collective-permute-start(bf16[208,256]{1,0:T(8,128)(2,1)S(1)} %get-tuple-element.29), channel_id=1, source_target_pairs={{0,320},{16,336},{32,352},{48,368},{64,256},{80,272},{96,288},{112... | collective-permute-start | bytes 319496 | tf_op jit(solution)/shard_map/ppermute | solution.py:255
  134.0 16.5 %collective-permute-start.28 = (bf16[256,1280]{1,0:T(8,128)(2,1)S(1)}, bf16[256,1280]{1,0:T(8,128)(2,1)S(1)}, u32[]{:S(2)}, u32[]{:S(2)}) collective-permute-start(bf16[256,1280]{1,0:T(8,128)(2,1)S(1)} %get-tuple-element.40.refs_4_), channel_id=1, source_target_pairs={{0,1},{1,0},{2,3},{3,2},{4,5},{5,4},{6,7},{7,6},{8,9},{9,8},{10,11... | collective-permute-start | bytes 1966088 | tf_op jit(solution)/shard_map/ppermute | solution.py:287
  153.0 10.9 %collective-permute-done.19.refs_6_ = bf16[208,256]{1,0:T(8,128)(2,1)} collective-permute-done((bf16[208,256]{1,0:T(8,128)(2,1)}, bf16[208,256]{1,0:T(8,128)(2,1)}, u32[]{:S(2)}, u32[]{:S(2)}) %collective-permute-start.19) | collective-permute-done | bytes 106528 | tf_op jit(solution)/shard_map/ppermute | solution.py:255
  166.0 4.9 %collective-permute-start.29 = (bf16[256,1280]{1,0:T(8,128)(2,1)S(1)}, bf16[256,1280]{1,0:T(8,128)(2,1)}, u32[]{:S(2)}, u32[]{:S(2)}) collective-permute-start(bf16[256,1280]{1,0:T(8,128)(2,1)S(1)} %collective-permute-done.25.refs_5_), channel_id=1, source_target_pairs={{0,1},{1,0},{2,3},{3,2},{4,5},{5,4},{6,7},{7,6},{8,9},{9,8},{10,11... | collective-permute-start | bytes 1966088 | tf_op jit(solution)/shard_map/ppermute | solution.py:287
  179.7 2.6 %merge.1 = (bf16[192,256]{1,0:T(8,128)(2,1)S(1)}, bf16[192,256]{1,0:T(8,128)(2,1)S(1)}) custom-call(s32[2]{0:T(128)S(1)} %pad_add_fusion.place, bf16[208,256]{1,0:T(8,128)(2,1)S(1)} %get-tuple-element.24.refs_0_, bf16[208,256]{1,0:T(8,128)(2,1)S(1)} %collective-permute-done.14.refs_1_, bf16[208,256]{1,0:T(8,128)(2,1)S(1)} %copy-done.5, ...), custom_call_target="tpu_custom_call" | custom-call | tf_op jit(solution)/shard_map/merge/pallas_call | solution.py:289
  182.3 3.7 %collective-permute-start.21 = (bf16[192,256]{1,0:T(8,128)(2,1)S(1)}, bf16[192,256]{1,0:T(8,128)(2,1)S(1)}, u32[]{:S(2)}, u32[]{:S(2)}) collective-permute-start(bf16[192,256]{1,0:T(8,128)(2,1)S(1)} %get-tuple-element.33), channel_id=1, source_target_pairs={{0,1},{1,0},{2,3},{3,2},{4,5},{5,4},{6,7},{7,6},{8,9},{9,8},{10,11... | collective-permute-start | bytes 294920 | tf_op jit(solution)/shard_map/ppermute | solution.py:297
  189.2 2.7 %collective-permute-start.23 = (bf16[192,512]{1,0:T(8,128)(2,1)S(1)}, bf16[192,512]{1,0:T(8,128)(2,1)}, u32[]{:S(2)}, u32[]{:S(2)}) collective-permute-start(bf16[192,512]{1,0:T(8,128)(2,1)S(1)} %constant_dynamic-update-slice_fusion.refs_0_), channel_id=1, source_target_pairs={{0,8},{1,9},{2,10},{3,11},{4,12},{5,13},{6,14},{7,15},{8,0},{9,1},... | collective-permute-start | bytes 589832 | tf_op jit(solution)/shard_map/ppermute | solution.py:298
  191.9 8.5 %collective-permute-done.22.refs_1_ = bf16[192,512]{1,0:T(8,128)(2,1)S(1)} collective-permute-done((bf16[192,512]{1,0:T(8,128)(2,1)S(1)}, bf16[192,512]{1,0:T(8,128)(2,1)S(1)}, u32[]{:S(2)}, u32[]{:S(2)}) %collective-permute-start.22) | collective-permute-done | bytes 196640 | tf_op jit(solution)/shard_map/ppermute | solution.py:298
  203.0 5.2 %collective-permute-done.24.refs_3_ = bf16[192,512]{1,0:T(8,128)(2,1)} collective-permute-done((bf16[192,512]{1,0:T(8,128)(2,1)S(1)}, bf16[192,512]{1,0:T(8,128)(2,1)}, u32[]{:S(2)}, u32[]{:S(2)}) %collective-permute-start.24) | collective-permute-done | bytes 196640 | tf_op jit(solution)/shard_map/ppermute | solution.py:298
  209.2 3.3 %project.1 = (f32[192,640]{1,0:T(8,128)S(1)}, bf16[192,640]{1,0:T(8,128)(2,1)S(1)}) custom-call(s32[1]{0:T(128)} %bitcast.1.half, bf16[192,512]{1,0:T(8,128)(2,1)S(1)} %constant_dynamic-update-slice_fusion.refs_0_, bf16[192,512]{1,0:T(8,128)(2,1)S(1)} %copy-done.1, bf16[192,512]{1,0:T(8,128)(2,1)} %collective-permute-done.23.refs_2_, ...), custom_call_target="tpu_custom_call" | custom-call | tf_op jit(solution)/shard_map/project/pallas_call | solution.py:300
  212.5 9.0 %collective-permute-start.32 = (bf16[192,640]{1,0:T(8,128)(2,1)S(1)}, bf16[192,640]{1,0:T(8,128)(2,1)S(1)}, u32[]{:S(2)}, u32[]{:S(2)}) collective-permute-start(bf16[192,640]{1,0:T(8,128)(2,1)S(1)} %get-tuple-element.35), channel_id=1, source_target_pairs={{0,2},{1,3},{2,0},{3,1},{4,6},{5,7},{6,4},{7,5},{8,10},{9,11},{10,... | collective-permute-start | bytes 737288 | tf_op jit(solution)/shard_map/ppermute | solution.py:308
  221.6 19.4 %collective-permute-done.32.theirs = bf16[192,640]{1,0:T(8,128)(2,1)S(1)} collective-permute-done((bf16[192,640]{1,0:T(8,128)(2,1)S(1)}, bf16[192,640]{1,0:T(8,128)(2,1)S(1)}, u32[]{:S(2)}, u32[]{:S(2)}) %collective-permute-start.32) | collective-permute-done | bytes 245792 | tf_op jit(solution)/shard_map/ppermute | solution.py:308
  (107 shorter events, 49.1 us)
Async XLA Ops:
  7.3 23.1 %collective-permute-start.7 = (bf16[192,256]{1,0:T(8,128)(2,1)S(1)}, bf16[192,256]{1,0:T(8,128)(2,1)S(1)}, u32[]{:S(2)}, u32[]{:S(2)}) collective-permute-start(bf16[192,256]{1,0:T(8,128)(2,1)S(1)} %get-tuple-element.23), channel_id=1, source_target_pairs={{0,64},{16,80},{32,96},{48,112},{64,0},{80,16},{96,32},{112,48},{1... | collective-permute-start | bytes 294920 | tf_op jit(solution)/shard_map/ppermute | solution.py:255
  11.7 20.7 %collective-permute-start.8 = (bf16[192,256]{1,0:T(8,128)(2,1)S(1)}, bf16[192,256]{1,0:T(8,128)(2,1)S(1)}, u32[]{:S(2)}, u32[]{:S(2)}) collective-permute-start(bf16[192,256]{1,0:T(8,128)(2,1)S(1)} %get-tuple-element.22.refs_8_), channel_id=1, source_target_pairs={{0,128},{16,144},{32,160},{48,176},{64,192},{80,208},{96,224},{112... | collective-permute-start | bytes 294920 | tf_op jit(solution)/shard_map/ppermute | solution.py:255
  16.6 54.0 %collective-permute-start.3 = (bf16[192,512]{1,0:T(8,128)(2,1)S(1)}, bf16[192,512]{1,0:T(8,128)(2,1)S(1)}, u32[]{:S(2)}, u32[]{:S(2)}) collective-permute-start(bf16[192,512]{1,0:T(8,128)(2,1)S(1)} %get-tuple-element.21), channel_id=1, source_target_pairs={{0,64},{16,80},{32,96},{48,112},{64,0},{80,16},{96,32},{112,48},{1... | collective-permute-start | bytes 589832 | tf_op jit(solution)/shard_map/ppermute | solution.py:255
  18.6 22.1 %collective-permute-start.9 = (bf16[192,256]{1,0:T(8,128)(2,1)S(1)}, bf16[192,256]{1,0:T(8,128)(2,1)S(1)}, u32[]{:S(2)}, u32[]{:S(2)}) collective-permute-start(bf16[192,256]{1,0:T(8,128)(2,1)S(1)} %get-tuple-element.23), channel_id=1, source_target_pairs={{0,192},{16,208},{32,224},{48,240},{64,128},{80,144},{96,160},{112... | collective-permute-start | bytes 294920 | tf_op jit(solution)/shard_map/ppermute | solution.py:255
  21.7 22.3 %collective-permute-start.10 = (bf16[192,256]{1,0:T(8,128)(2,1)S(1)}, bf16[192,256]{1,0:T(8,128)(2,1)S(1)}, u32[]{:S(2)}, u32[]{:S(2)}) collective-permute-start(bf16[192,256]{1,0:T(8,128)(2,1)S(1)} %get-tuple-element.22.refs_8_), channel_id=1, source_target_pairs={{0,256},{16,272},{32,288},{48,304},{64,320},{80,336},{96,352},{112... | collective-permute-start | bytes 294920 | tf_op jit(solution)/shard_map/ppermute | solution.py:255
  30.5 19.9 %collective-permute-start.11 = (bf16[192,256]{1,0:T(8,128)(2,1)S(1)}, bf16[192,256]{1,0:T(8,128)(2,1)S(1)}, u32[]{:S(2)}, u32[]{:S(2)}) collective-permute-start(bf16[192,256]{1,0:T(8,128)(2,1)S(1)} %get-tuple-element.23), channel_id=1, source_target_pairs={{0,320},{16,336},{32,352},{48,368},{64,256},{80,272},{96,288},{112... | collective-permute-start | bytes 294920 | tf_op jit(solution)/shard_map/ppermute | solution.py:255
  32.4 23.4 %collective-permute-start.12 = (bf16[192,256]{1,0:T(8,128)(2,1)S(1)}, bf16[192,256]{1,0:T(8,128)(2,1)S(1)}, u32[]{:S(2)}, u32[]{:S(2)}) collective-permute-start(bf16[192,256]{1,0:T(8,128)(2,1)S(1)} %get-tuple-element.22.refs_8_), channel_id=1, source_target_pairs={{0,384},{16,400},{32,416},{48,432},{64,448},{80,464},{96,480},{112... | collective-permute-start | bytes 294920 | tf_op jit(solution)/shard_map/ppermute | solution.py:255
  40.7 38.8 %collective-permute-start = (bf16[192,512]{1,0:T(8,128)(2,1)S(1)}, bf16[192,512]{1,0:T(8,128)(2,1)S(1)}, u32[]{:S(2)}, u32[]{:S(2)}) collective-permute-start(bf16[192,512]{1,0:T(8,128)(2,1)S(1)} %get-tuple-element.20.refs_0_), channel_id=1, source_target_pairs={{0,16},{16,32},{32,48},{48,0},{64,80},{80,96},{96,112},{112,64},{1... | collective-permute-start | bytes 589832 | tf_op jit(solution)/shard_map/ppermute | solution.py:258
  44.6 39.3 %collective-permute-start.1 = (bf16[192,512]{1,0:T(8,128)(2,1)S(1)}, bf16[192,512]{1,0:T(8,128)(2,1)S(1)}, u32[]{:S(2)}, u32[]{:S(2)}) collective-permute-start(bf16[192,512]{1,0:T(8,128)(2,1)S(1)} %get-tuple-element.20.refs_0_), channel_id=1, source_target_pairs={{0,48},{16,0},{32,16},{48,32},{64,112},{80,64},{96,80},{112,96},{1... | collective-permute-start | bytes 589832 | tf_op jit(solution)/shard_map/ppermute | solution.py:258
  51.0 36.0 %collective-permute-start.2 = (bf16[192,512]{1,0:T(8,128)(2,1)S(1)}, bf16[192,512]{1,0:T(8,128)(2,1)S(1)}, u32[]{:S(2)}, u32[]{:S(2)}) collective-permute-start(bf16[192,512]{1,0:T(8,128)(2,1)S(1)} %get-tuple-element.20.refs_0_), channel_id=1, source_target_pairs={{0,32},{16,48},{32,0},{48,16},{64,96},{80,112},{96,64},{112,80},{1... | collective-permute-start | bytes 589832 | tf_op jit(solution)/shard_map/ppermute | solution.py:258
  56.5 19.9 %collective-permute-start.13 = (bf16[192,256]{1,0:T(8,128)(2,1)S(1)}, bf16[192,256]{1,0:T(8,128)(2,1)S(1)}, u32[]{:S(2)}, u32[]{:S(2)}) collective-permute-start(bf16[192,256]{1,0:T(8,128)(2,1)S(1)} %get-tuple-element.23), channel_id=1, source_target_pairs={{0,448},{16,464},{32,480},{48,496},{64,384},{80,400},{96,416},{112... | collective-permute-start | bytes 294920 | tf_op jit(solution)/shard_map/ppermute | solution.py:255
  70.6 20.3 %collective-permute-start.4 = (bf16[192,512]{1,0:T(8,128)(2,1)S(1)}, bf16[192,512]{1,0:T(8,128)(2,1)S(1)}, u32[]{:S(2)}, u32[]{:S(2)}) collective-permute-start(bf16[192,512]{1,0:T(8,128)(2,1)S(1)} %collective-permute-done.3.refs_4_), channel_id=1, source_target_pairs={{0,16},{16,32},{32,48},{48,0},{64,80},{80,96},{96,112},{112,64},{1... | collective-permute-start | bytes 589832 | tf_op jit(solution)/shard_map/ppermute | solution.py:258
  76.4 89.5 %collective-permute-start.25 = (bf16[256,1280]{1,0:T(8,128)(2,1)}, bf16[256,1280]{1,0:T(8,128)(2,1)S(1)}, u32[]{:S(2)}, u32[]{:S(2)}) collective-permute-start(bf16[256,1280]{1,0:T(8,128)(2,1)} %get-tuple-element.39), channel_id=1, source_target_pairs={{0,4},{1,5},{2,6},{3,7},{4,8},{5,9},{6,10},{7,11},{8,12},{9,13},{1... | collective-permute-start | bytes 1966088 | tf_op jit(solution)/shard_map/ppermute | solution.py:286
  79.6 91.3 %collective-permute-start.26 = (bf16[256,1280]{1,0:T(8,128)(2,1)}, bf16[256,1280]{1,0:T(8,128)(2,1)S(1)}, u32[]{:S(2)}, u32[]{:S(2)}) collective-permute-start(bf16[256,1280]{1,0:T(8,128)(2,1)} %get-tuple-element.41), channel_id=1, source_target_pairs={{0,8},{1,9},{2,10},{3,11},{4,12},{5,13},{6,14},{7,15},{8,0},{9,1},... | collective-permute-start | bytes 1966088 | tf_op jit(solution)/shard_map/ppermute | solution.py:286
  83.9 88.9 %collective-permute-start.27 = (bf16[256,1280]{1,0:T(8,128)(2,1)}, bf16[256,1280]{1,0:T(8,128)(2,1)S(1)}, u32[]{:S(2)}, u32[]{:S(2)}) collective-permute-start(bf16[256,1280]{1,0:T(8,128)(2,1)} %get-tuple-element.38), channel_id=1, source_target_pairs={{0,12},{1,13},{2,14},{3,15},{4,0},{5,1},{6,2},{7,3},{8,4},{9,5},{1... | collective-permute-start | bytes 1966088 | tf_op jit(solution)/shard_map/ppermute | solution.py:286
  87.0 7.2 %collective-permute-start.5 = (bf16[192,512]{1,0:T(8,128)(2,1)S(1)}, bf16[192,512]{1,0:T(8,128)(2,1)S(1)}, u32[]{:S(2)}, u32[]{:S(2)}) collective-permute-start(bf16[192,512]{1,0:T(8,128)(2,1)S(1)} %collective-permute-done.3.refs_4_), channel_id=1, source_target_pairs={{0,48},{16,0},{32,16},{48,32},{64,112},{80,64},{96,80},{112,96},{1... | collective-permute-start | bytes 589832 | tf_op jit(solution)/shard_map/ppermute | solution.py:258
  90.9 7.9 %collective-permute-start.6 = (bf16[192,512]{1,0:T(8,128)(2,1)S(1)}, bf16[192,512]{1,0:T(8,128)(2,1)S(1)}, u32[]{:S(2)}, u32[]{:S(2)}) collective-permute-start(bf16[192,512]{1,0:T(8,128)(2,1)S(1)} %collective-permute-done.3.refs_4_), channel_id=1, source_target_pairs={{0,32},{16,48},{32,0},{48,16},{64,96},{80,112},{96,64},{112,80},{1... | collective-permute-start | bytes 589832 | tf_op jit(solution)/shard_map/ppermute | solution.py:258
  112.5 5.4 %collective-permute-start.14 = (bf16[208,256]{1,0:T(8,128)(2,1)S(1)}, bf16[208,256]{1,0:T(8,128)(2,1)S(1)}, u32[]{:S(2)}, u32[]{:S(2)}) collective-permute-start(bf16[208,256]{1,0:T(8,128)(2,1)S(1)} %get-tuple-element.25), channel_id=1, source_target_pairs={{0,64},{16,80},{32,96},{48,112},{64,0},{80,16},{96,32},{112,48},{1... | collective-permute-start | bytes 319496 | tf_op jit(solution)/shard_map/ppermute | solution.py:255
  114.4 7.4 %collective-permute-start.15 = (bf16[208,256]{1,0:T(8,128)(2,1)S(1)}, bf16[208,256]{1,0:T(8,128)(2,1)S(1)}, u32[]{:S(2)}, u32[]{:S(2)}) collective-permute-start(bf16[208,256]{1,0:T(8,128)(2,1)S(1)} %get-tuple-element.26), channel_id=1, source_target_pairs={{0,128},{16,144},{32,160},{48,176},{64,192},{80,208},{96,224},{112... | collective-permute-start | bytes 319496 | tf_op jit(solution)/shard_map/ppermute | solution.py:255
  117.9 7.8 %collective-permute-start.16 = (bf16[208,256]{1,0:T(8,128)(2,1)S(1)}, bf16[208,256]{1,0:T(8,128)(2,1)S(1)}, u32[]{:S(2)}, u32[]{:S(2)}) collective-permute-start(bf16[208,256]{1,0:T(8,128)(2,1)S(1)} %get-tuple-element.27), channel_id=1, source_target_pairs={{0,192},{16,208},{32,224},{48,240},{64,128},{80,144},{96,160},{112... | collective-permute-start | bytes 319496 | tf_op jit(solution)/shard_map/ppermute | solution.py:255
  122.4 10.9 %collective-permute-start.17 = (bf16[208,256]{1,0:T(8,128)(2,1)S(1)}, bf16[208,256]{1,0:T(8,128)(2,1)S(1)}, u32[]{:S(2)}, u32[]{:S(2)}) collective-permute-start(bf16[208,256]{1,0:T(8,128)(2,1)S(1)} %get-tuple-element.28), channel_id=1, source_target_pairs={{0,256},{16,272},{32,288},{48,304},{64,320},{80,336},{96,352},{112... | collective-permute-start | bytes 319496 | tf_op jit(solution)/shard_map/ppermute | solution.py:255
  126.3 24.1 %collective-permute-start.18 = (bf16[208,256]{1,0:T(8,128)(2,1)S(1)}, bf16[208,256]{1,0:T(8,128)(2,1)S(1)}, u32[]{:S(2)}, u32[]{:S(2)}) collective-permute-start(bf16[208,256]{1,0:T(8,128)(2,1)S(1)} %get-tuple-element.29), channel_id=1, source_target_pairs={{0,320},{16,336},{32,352},{48,368},{64,256},{80,272},{96,288},{112... | collective-permute-start | bytes 319496 | tf_op jit(solution)/shard_map/ppermute | solution.py:255
  134.0 55.2 %collective-permute-start.28 = (bf16[256,1280]{1,0:T(8,128)(2,1)S(1)}, bf16[256,1280]{1,0:T(8,128)(2,1)S(1)}, u32[]{:S(2)}, u32[]{:S(2)}) collective-permute-start(bf16[256,1280]{1,0:T(8,128)(2,1)S(1)} %get-tuple-element.40.refs_4_), channel_id=1, source_target_pairs={{0,1},{1,0},{2,3},{3,2},{4,5},{5,4},{6,7},{7,6},{8,9},{9,8},{10,11... | collective-permute-start | bytes 1966088 | tf_op jit(solution)/shard_map/ppermute | solution.py:287
  151.1 12.8 %collective-permute-start.19 = (bf16[208,256]{1,0:T(8,128)(2,1)}, bf16[208,256]{1,0:T(8,128)(2,1)}, u32[]{:S(2)}, u32[]{:S(2)}) collective-permute-start(bf16[208,256]{1,0:T(8,128)(2,1)} %get-tuple-element.30), channel_id=1, source_target_pairs={{0,384},{16,400},{32,416},{48,432},{64,448},{80,464},{96,480},{112... | collective-permute-start | bytes 319496 | tf_op jit(solution)/shard_map/ppermute | solution.py:255
  163.9 12.3 %collective-permute-start.20 = (bf16[208,256]{1,0:T(8,128)(2,1)}, bf16[208,256]{1,0:T(8,128)(2,1)S(1)}, u32[]{:S(2)}, u32[]{:S(2)}) collective-permute-start(bf16[208,256]{1,0:T(8,128)(2,1)} %copy-done.28), channel_id=1, source_target_pairs={{0,448},{16,464},{32,480},{48,496},{64,384},{80,400},{96,416},{112... | collective-permute-start | bytes 319496 | tf_op jit(solution)/shard_map/ppermute | solution.py:255
  166.0 42.3 %collective-permute-start.29 = (bf16[256,1280]{1,0:T(8,128)(2,1)S(1)}, bf16[256,1280]{1,0:T(8,128)(2,1)}, u32[]{:S(2)}, u32[]{:S(2)}) collective-permute-start(bf16[256,1280]{1,0:T(8,128)(2,1)S(1)} %collective-permute-done.25.refs_5_), channel_id=1, source_target_pairs={{0,1},{1,0},{2,3},{3,2},{4,5},{5,4},{6,7},{7,6},{8,9},{9,8},{10,11... | collective-permute-start | bytes 1966088 | tf_op jit(solution)/shard_map/ppermute | solution.py:287
  170.9 37.4 %collective-permute-start.30 = (bf16[256,1280]{1,0:T(8,128)(2,1)S(1)}, bf16[256,1280]{1,0:T(8,128)(2,1)}, u32[]{:S(2)}, u32[]{:S(2)}) collective-permute-start(bf16[256,1280]{1,0:T(8,128)(2,1)S(1)} %collective-permute-done.26.refs_6_), channel_id=1, source_target_pairs={{0,1},{1,0},{2,3},{3,2},{4,5},{5,4},{6,7},{7,6},{8,9},{9,8},{10,11... | collective-permute-start | bytes 1966088 | tf_op jit(solution)/shard_map/ppermute | solution.py:287
  172.8 35.5 %collective-permute-start.31 = (bf16[256,1280]{1,0:T(8,128)(2,1)S(1)}, bf16[256,1280]{1,0:T(8,128)(2,1)}, u32[]{:S(2)}, u32[]{:S(2)}) collective-permute-start(bf16[256,1280]{1,0:T(8,128)(2,1)S(1)} %collective-permute-done.27.refs_7_), channel_id=1, source_target_pairs={{0,1},{1,0},{2,3},{3,2},{4,5},{5,4},{6,7},{7,6},{8,9},{9,8},{10,11... | collective-permute-start | bytes 1966088 | tf_op jit(solution)/shard_map/ppermute | solution.py:287
  187.0 13.4 %collective-permute-start.22 = (bf16[192,512]{1,0:T(8,128)(2,1)S(1)}, bf16[192,512]{1,0:T(8,128)(2,1)S(1)}, u32[]{:S(2)}, u32[]{:S(2)}) collective-permute-start(bf16[192,512]{1,0:T(8,128)(2,1)S(1)} %constant_dynamic-update-slice_fusion.refs_0_), channel_id=1, source_target_pairs={{0,4},{1,5},{2,6},{3,7},{4,8},{5,9},{6,10},{7,11},{8,12},{9,13},{1... | collective-permute-start | bytes 589832 | tf_op jit(solution)/shard_map/ppermute | solution.py:298
  189.2 13.8 %collective-permute-start.23 = (bf16[192,512]{1,0:T(8,128)(2,1)S(1)}, bf16[192,512]{1,0:T(8,128)(2,1)}, u32[]{:S(2)}, u32[]{:S(2)}) collective-permute-start(bf16[192,512]{1,0:T(8,128)(2,1)S(1)} %constant_dynamic-update-slice_fusion.refs_0_), channel_id=1, source_target_pairs={{0,8},{1,9},{2,10},{3,11},{4,12},{5,13},{6,14},{7,15},{8,0},{9,1},... | collective-permute-start | bytes 589832 | tf_op jit(solution)/shard_map/ppermute | solution.py:298
  201.1 7.2 %collective-permute-start.24 = (bf16[192,512]{1,0:T(8,128)(2,1)S(1)}, bf16[192,512]{1,0:T(8,128)(2,1)}, u32[]{:S(2)}, u32[]{:S(2)}) collective-permute-start(bf16[192,512]{1,0:T(8,128)(2,1)S(1)} %constant_dynamic-update-slice_fusion.refs_0_), channel_id=1, source_target_pairs={{0,12},{1,13},{2,14},{3,15},{4,0},{5,1},{6,2},{7,3},{8,4},{9,5},{1... | collective-permute-start | bytes 589832 | tf_op jit(solution)/shard_map/ppermute | solution.py:298
  212.5 28.4 %collective-permute-start.32 = (bf16[192,640]{1,0:T(8,128)(2,1)S(1)}, bf16[192,640]{1,0:T(8,128)(2,1)S(1)}, u32[]{:S(2)}, u32[]{:S(2)}) collective-permute-start(bf16[192,640]{1,0:T(8,128)(2,1)S(1)} %get-tuple-element.35), channel_id=1, source_target_pairs={{0,2},{1,3},{2,0},{3,1},{4,6},{5,7},{6,4},{7,5},{8,10},{9,11},{10,... | collective-permute-start | bytes 737288 | tf_op jit(solution)/shard_map/ppermute | solution.py:308
  (32 other events, 361.2 us)

commit v2 on v1

v2 whole, which is shorter than its diff:
```python
import functools
import math

import jax
import jax.numpy as jnp
from jax import lax
from jax.experimental import pallas as pl
from jax.experimental.pallas import tpu as pltpu
from jax.sharding import PartitionSpec as P

HD = 128
FRAME = 32
NZ, NY, NX = 8, 4, 4
FACTOR = 1.0 / math.sqrt(HD)
LOG2E = math.log2(math.e)
STAT_ROWS = 16
BF = jnp.bfloat16
F32 = jnp.float32
def params(mib):
    return pltpu.CompilerParams(vmem_limit_bytes=mib * 1024 * 1024)


SMEM_SPEC = pl.BlockSpec(memory_space=pltpu.SMEM)
VMEM_SPEC = pl.BlockSpec(memory_space=pltpu.VMEM)
HBM_SPEC = pl.BlockSpec(memory_space=pltpu.HBM)


def over_z(k):
    return [(z * NY + y, (z ^ k) * NY + y) for z in range(NZ) for y in range(NY)]


def over_y(k):
    return [(z * NY + y, z * NY + (y + k) % NY) for z in range(NZ) for y in range(NY)]


def over_x(k):
    return [(x * 4 + r, (x + k) % NX * 4 + r) for x in range(NX) for r in range(4)]


def flip(bits):
    return [(i, i ^ bits) for i in range(4 * NX)]


def same_y():
    return [[z * NY + y for z in range(NZ)] for y in range(NY)]


def pack_kernel(odd, flags, *refs):
    sources, (qd_out, kv_own, kv_other) = refs[:6], refs[6:9]
    held, qd, kv, other, sems = refs[9:15], refs[15:17], refs[17], refs[18], refs[19]
    rows_all = other.shape[0]
    copies = [pltpu.make_async_copy(sources[i], held[i], sems.at[i]) for i in range(6)]
    for copy in copies:
        copy.start()
    for copy in copies:
        copy.wait()
    q, dq, k, v, dk, dv = held
    is_odd = odd[0] > 0
    for f in range(rows_all // FRAME):
        rows = pl.ds(f * FRAME, FRAME)
        live = flags[f * FRAME] > 0

        def masked(ref):
            block = ref[rows, :]
            return jnp.where(live, block, jnp.zeros_like(block))

        for i, block in enumerate((masked(dq), q[rows, :])):
            for h in range(2):
                qd[h][rows, i * HD : (i + 1) * HD] = block[:, h * HD : (h + 1) * HD]
        for i, block in enumerate((k[rows, :], masked(dk), v[rows, :], masked(dv))):
            first, second = block[:, :HD], block[:, HD:]
            kv[rows, i * HD : (i + 1) * HD] = jnp.where(is_odd, second, first)
            other[rows, i * HD : (i + 1) * HD] = jnp.where(is_odd, first, second)
    copies = [
        pltpu.make_async_copy(other, kv_other, sems.at[0]),
        pltpu.make_async_copy(kv, kv_own.at[pl.ds(0, rows_all)], sems.at[1]),
    ]
    for i in range(NZ):
        at = pl.ds(i * rows_all, rows_all)
        copies.append(pltpu.make_async_copy(qd[i % 2], qd_out.at[at], sems.at[2 + i]))
    for copy in copies:
        copy.start()
    for copy in copies:
        copy.wait()


def join_kernel(at, got, own_in, own, sem):
    del own_in
    rows, width = got.shape
    copy = pltpu.make_async_copy(
        got, own.at[pl.ds(at * rows, rows), pl.ds((1 - at) * width, width)], sem
    )
    copy.start()
    copy.wait()


def in_three(value):
    high = value.astype(BF).astype(F32)
    middle = (value - high).astype(BF).astype(F32)
    low = (value - high - middle).astype(BF).astype(F32)
    return high, middle, low


def attend_kernel(*refs):
    kv_in, qd_in, out = refs[:4], refs[4], refs[5]
    kv, qd, held, sems = refs[6:]
    rows = kv_in[0].shape[0]
    half = rows // 2
    copies = [pltpu.make_async_copy(qd_in, qd, sems.at[4])]
    for i in range(4):
        copies.append(pltpu.make_async_copy(kv_in[i], kv.at[pl.ds(i * rows, rows)], sems.at[i]))
    for copy in copies:
        copy.start()
    for copy in copies:
        copy.wait()
    contract = (((1,), (1,)), ((), ()))

    def step(j, carry):
        both = qd[pl.ds(pl.multiple_of(j * rows, rows), rows), :]
        scores = lax.dot_general(both[:, HD:], kv[:, :HD], contract, preferred_element_type=F32)
        slopes = lax.dot_general(both, kv[:, : 2 * HD], contract, preferred_element_type=F32)
        scores = scores * (FACTOR * LOG2E)
        peak = jnp.max(scores, axis=1, keepdims=True)
        weights = jnp.exp2(scores - peak)
        total = jnp.sum(weights, axis=1, keepdims=True)
        product = weights * slopes
        slope = jnp.sum(product, axis=1, keepdims=True)
        weighted = jnp.dot(weights.astype(BF), kv[:, 2 * HD :], preferred_element_type=F32)
        tangent = jnp.dot(product.astype(BF), kv[:, 2 * HD : 3 * HD], preferred_element_type=F32)
        inverse = 1.0 / total
        mean = slope * (inverse * FACTOR)
        primal = weighted[:, :HD] * inverse
        tangent = (tangent * FACTOR + weighted[:, HD:]) * inverse - mean * primal
        lanes = lax.broadcasted_iota(jnp.int32, (rows, HD), 1)
        stats = jnp.zeros((rows, HD), F32)
        for i, part in enumerate(in_three(peak + jnp.log2(total)) + in_three(mean)):
            stats = jnp.where(lanes == i, part, stats)
        for p in range(2):
            mine = slice(p * half, (p + 1) * half)
            at = p * (half + STAT_ROWS)
            held[j, at : at + half, :HD] = primal[mine].astype(BF)
            held[j, at : at + half, HD:] = tangent[mine].astype(BF)
            tile = jnp.concatenate([stats[mine], jnp.zeros((2 * HD - half, HD), F32)], axis=0)
            held[j, at + half : at + half + STAT_ROWS, :] = tile.T[:STAT_ROWS].astype(BF)
        return carry

    lax.fori_loop(0, 4, step, 0)
    count = held.shape[1]
    back = [
        pltpu.make_async_copy(held.at[i], out.at[pl.ds(i * count, count)], sems.at[i])
        for i in range(4)
    ]
    for copy in back:
        copy.start()
    for copy in back:
        copy.wait()


def merge_kernel(core, parts, keep_all, send, keep, sem):
    rows = send.shape[0]
    step = rows + STAT_ROWS
    is_second = core[0] > 0
    tiles = [parts[i * step + rows : (i + 1) * step, :].astype(F32) for i in range(NZ)]
    stats = jnp.concatenate(tiles, axis=0).T[:rows]

    def value(i, first):
        lane = i * STAT_ROWS + first
        return sum(stats[:, lane + j : lane + j + 1] for j in range(3))

    for h in range(2):
        group = range(h, NZ, 2)
        sizes = [value(i, 0) for i in group]
        means = [value(i, 3) for i in group]
        peak = functools.reduce(jnp.maximum, sizes)
        sizes = [jnp.exp2(size - peak) for size in sizes]
        inverse = 1.0 / sum(sizes)
        sizes = [size * inverse for size in sizes]
        mean = sum(size * m for size, m in zip(sizes, means))
        primal = jnp.zeros((rows, HD), F32)
        tangent = jnp.zeros((rows, HD), F32)
        for i, size, m in zip(group, sizes, means):
            at = i * step
            a = parts[at : at + rows, :HD].astype(F32)
            primal += size * a
            tangent += size * parts[at : at + rows, HD:].astype(F32) + (size * (m - mean)) * a
        primal, tangent = primal.astype(BF), tangent.astype(BF)
        at = slice(h * HD, (h + 1) * HD)
        keep[:, at] = jnp.where(is_second, tangent, primal)
        send[:, at] = jnp.where(is_second, primal, tangent)
    copy = pltpu.make_async_copy(keep, keep_all.at[:, pl.ds(0, 2 * HD)], sem)
    copy.start()
    copy.wait()


def project_kernel(place, *refs):
    acts, w_own, w_other, (mine, others) = refs[:4], refs[4], refs[5], refs[6:]
    width = mine.shape[1]
    depth = w_own.shape[0] // 4
    is_second = place[1] > 0
    for half in range(2):

        @pl.when(place[0] == half)
        def _():
            at = slice(2 * half * width, 2 * (half + 1) * width)
            total = jnp.zeros((mine.shape[0], 2 * width), F32)
            for i in range(4):
                down = slice(i * depth, (i + 1) * depth)
                total += jnp.dot(acts[i][:, :depth], w_own[down, at], preferred_element_type=F32)
                total += jnp.dot(acts[i][:, depth:], w_other[down, at], preferred_element_type=F32)
            first, second = total[:, :width], total[:, width:]
            mine[...] = jnp.where(is_second, second, first).astype(mine.dtype)
            others[...] = jnp.where(is_second, first, second).astype(others.dtype)


def stack_kernel(*refs):
    pieces, out, sems = refs[:4], refs[4], refs[5]
    rows = pieces[0].shape[0]
    copies = [
        pltpu.make_async_copy(pieces[i], out.at[pl.ds(i * rows, rows)], sems.at[i])
        for i in range(4)
    ]
    for copy in copies:
        copy.start()
    for copy in copies:
        copy.wait()


def finish_kernel(
    core, flags, mine, z_got, core_got, both_got, gate, tokens, d_tokens, result, d_result
):
    is_second = core[0] > 0
    scale = gate[...]
    for f in range(tokens.shape[0] // FRAME):
        rows = pl.ds(f * FRAME, FRAME)
        live = flags[f * FRAME] > 0
        kept = mine[rows, :] + z_got[rows, :].astype(F32)
        other = core_got[rows, :].astype(F32) + both_got[rows, :].astype(F32)
        primal = jnp.where(is_second, other, kept)
        tangent = jnp.where(is_second, kept, other)
        base = tokens[rows, :].astype(F32)
        d_base = d_tokens[rows, :].astype(F32)
        d_base = jnp.where(live, d_base, jnp.zeros_like(d_base))
        result[rows, :] = (base + scale * primal).astype(BF)
        d_result[rows, :] = (d_base + scale * tangent).astype(BF)


def per_device(
    queries,
    d_queries,
    key_rows,
    value_rows,
    d_key_rows,
    d_value_rows,
    live_flags,
    out_weight,
    gate_scale,
    tokens,
    d_tokens,
):
    rows, width = queries.shape
    columns = tokens.shape[1]
    t, m = lax.axis_index("tm"), lax.axis_index("mp")
    odd = (t // NY % 2).astype(jnp.int32).reshape(1)
    core = (m % 2).astype(jnp.int32).reshape(1)
    half = (m // 2 % 2).astype(jnp.int32).reshape(1)
    x = m // 4

    def shape(r, c, dtype=BF):
        return jax.ShapeDtypeStruct((r, c), dtype)

    qd, kv, kv_other = pl.pallas_call(
        pack_kernel,
        out_shape=[shape(NZ * rows, 2 * HD), shape(2 * rows, 4 * HD), shape(rows, 4 * HD)],
        in_specs=[SMEM_SPEC] * 2 + [HBM_SPEC] * 6,
        out_specs=[HBM_SPEC] * 3,
        scratch_shapes=[pltpu.VMEM((rows, width), BF)] * 6
        + [pltpu.VMEM((rows, 2 * HD), BF)] * 2
        + [pltpu.VMEM((rows, 4 * HD), BF)] * 2
        + [pltpu.SemaphoreType.DMA((2 + NZ,))],
        compiler_params=params(60),
        name="pack",
    )(odd, live_flags, queries, d_queries, key_rows, value_rows, d_key_rows, d_value_rows)

    def join(got, own, at):
        return pl.pallas_call(
            functools.partial(join_kernel, at),
            out_shape=jax.ShapeDtypeStruct(own.shape, BF),
            in_specs=[HBM_SPEC] * 2,
            out_specs=HBM_SPEC,
            scratch_shapes=[pltpu.SemaphoreType.DMA],
            input_output_aliases={1: 0},
            compiler_params=params(8),
            name="join",
        )(got, own)

    def y(a, k):
        return lax.ppermute(a, "tm", over_y(k))

    def exchange(a):
        return lax.all_to_all(a, "tm", 0, 0, axis_index_groups=same_y(), tiled=True)

    group = 4 * columns
    qd, out_weight = lax.optimization_barrier((qd, out_weight))
    w_own = [
        lax.dynamic_slice(out_weight, (0, (x + k) % NX * group), (width, group)) for k in range(4)
    ]
    kv_got = lax.ppermute(kv_other, "tm", over_z(1))
    w_one, w_three = (lax.ppermute(w_own[k], "mp", over_x(k)) for k in (1, 3))
    qd, kv_got = lax.optimization_barrier((qd, kv_got))
    kv = join(kv_got, kv, 1)
    kv = [kv] + [y(kv, k) for k in (1, 3, 2)]
    w_two, kv[1] = lax.optimization_barrier((w_own[2], kv[1]))
    w_two = lax.ppermute(w_two, "mp", over_x(2))
    qd = exchange(qd)

    parts = pl.pallas_call(
        attend_kernel,
        out_shape=shape(NZ * (rows + STAT_ROWS), 2 * HD),
        in_specs=[HBM_SPEC] * 5,
        out_specs=HBM_SPEC,
        scratch_shapes=[
            pltpu.VMEM((NZ * rows, 4 * HD), BF),
            pltpu.VMEM((NZ * rows, 2 * HD), BF),
            pltpu.VMEM((4, 2 * (rows + STAT_ROWS), 2 * HD), BF),
            pltpu.SemaphoreType.DMA((5,)),
        ],
        compiler_params=params(24),
        name="attend",
    )(*kv, qd)
    w_own = [w_own[0], w_one, w_two, w_three]
    w_own, parts = lax.optimization_barrier((w_own, parts))
    parts = exchange(parts)

    act, send = pl.pallas_call(
        merge_kernel,
        out_shape=[shape(rows, 4 * HD), shape(rows, 2 * HD)],
        in_specs=[SMEM_SPEC, VMEM_SPEC],
        out_specs=[HBM_SPEC, VMEM_SPEC],
        scratch_shapes=[pltpu.VMEM((rows, 2 * HD), BF), pltpu.SemaphoreType.DMA],
        compiler_params=params(8),
        name="merge",
    )(core, parts)
    w_own = pl.pallas_call(
        stack_kernel,
        out_shape=shape(4 * width, group),
        in_specs=[HBM_SPEC] * 4,
        out_specs=HBM_SPEC,
        scratch_shapes=[pltpu.SemaphoreType.DMA((4,))],
        compiler_params=params(8),
        name="stack",
    )(*w_own)
    w_other = lax.ppermute(w_own, "mp", flip(1))
    act = join(lax.ppermute(send, "mp", flip(1)), act, 0)
    acts = [act] + [lax.ppermute(act, "mp", over_x(k)) for k in (1, 2, 3)]

    def project(which, dtype):
        return pl.pallas_call(
            project_kernel,
            out_shape=[shape(rows, columns, dtype), shape(rows, columns)],
            in_specs=[SMEM_SPEC] + [VMEM_SPEC] * 6,
            out_specs=[VMEM_SPEC] * 2,
            compiler_params=params(20),
            name="project",
        )(jnp.concatenate([which, core]), *acts, w_own, w_other)

    z_send, both_send = project(1 - half, BF)
    mine, core_send = project(half, F32)
    z_got = lax.ppermute(z_send, "mp", flip(2))
    both_got = lax.ppermute(both_send, "mp", flip(3))
    core_got = lax.ppermute(core_send, "mp", flip(1))

    result, d_result = pl.pallas_call(
        finish_kernel,
        out_shape=[shape(rows, columns)] * 2,
        in_specs=[SMEM_SPEC] * 2 + [VMEM_SPEC] * 7,
        out_specs=[VMEM_SPEC] * 2,
        compiler_params=params(8),
        name="finish",
    )(
        core,
        live_flags,
        mine,
        z_got,
        core_got,
        both_got,
        gate_scale.reshape(1, columns),
        tokens,
        d_tokens,
    )
    return (result, d_result)


def solution(mesh):
    placed = (
        P("tm", "mp"),
        P("tm", "mp"),
        P("tm", "mp"),
        P("tm", "mp"),
        P("tm", "mp"),
        P("tm", "mp"),
        P("tm"),
        P("mp", None),
        P("mp"),
        P("tm", "mp"),
        P("tm", "mp"),
    )
    return jax.shard_map(
        per_device,
        mesh=mesh,
        in_specs=placed,
        out_specs=(P("tm", "mp"), P("tm", "mp")),
        check_vma=False,
    )
```

time: 248 us -> 194 us (0.78)
  the two profiles are of different devices: /device:TPU:1 before, /device:TPU:47 now
where the time goes in v2:
time: 194 us; the launch traced here: 193 us
  waiting for transfers between devices  78.3 us (40%)
  starting transfers between devices  77.6 us (40%)
  Pallas kernels  24.8 us (13%)
  local copies, waits for them, and re-layouts  10.6 us (5%)
    all_to_all x2, waiting for transfers between devices, exchange(): return lax.all_to_all(a, 'tm', 0, 0, axis_index_groups=same_y(), tiled=True)  26.9 us
    ppermute x1, waiting for transfers between devices, per_device(): both_got = lax.ppermute(both_send, 'mp', flip(3))  21.4 us
    all_to_all x2, starting transfers between devices, exchange(): return lax.all_to_all(a, 'tm', 0, 0, axis_index_groups=same_y(), tiled=True)  20.6 us
    ppermute x3, waiting for transfers between devices, y(): return lax.ppermute(a, 'tm', over_y(k))  12.6 us
    pallas_call x1, Pallas kernels, per_device(): pl.pallas_call(attend_kernel, out_shape=shape(NZ * (rows + STAT_ROWS), 2...  9.63 us
    ppermute x3, waiting for transfers between devices, per_device(): acts = [act] + [lax.ppermute(act, 'mp', over_x(k)) for k in (1, 2, 3)]  9.45 us
    ppermute x3, starting transfers between devices, y(): return lax.ppermute(a, 'tm', over_y(k))  9.2 us
    ppermute x3, starting transfers between devices, per_device(): acts = [act] + [lax.ppermute(act, 'mp', over_x(k)) for k in (1, 2, 3)]  8.43 us
  transfers between devices with their start and end apart: 17, of which 10 were waited for; matrix products, arithmetic and copies ran while one was open for 2% of the time, Pallas kernels for 9%

profile of v2, /device:TPU:47, one launch (start us, length us, event | category | flops | bytes accessed | tf_op | source)
XLA Modules:
  0.0 192.5 jit_solution(2310069899613510078)
XLA Ops:
  0.7 3.0 %pack.1 = (bf16[1536,256]{1,0:T(8,128)(2,1)}, bf16[384,512]{1,0:T(8,128)(2,1)}, bf16[192,512]{1,0:T(8,128)(2,1)}) custom-call(s32[1]{0:T(128)} %bitcast.2.odd, s32[192]{0:T(256)} %flags.3, bf16[192,256]{1,0:T(8,128)(2,1)} %refs_0_.1, bf16[192,256]{1,0:T(8,128)(2,1)} %refs_1_.1, bf16[192,256]{1,0:T(8,128)(2,1)} %refs_2_.1, bf16[192,256]{1,0:T(8,128)(2,1)} %refs_3_.1, ...), custom_call_target="tpu_custom_call" | custom-call | tf_op jit(solution)/shard_map/pack/pallas_call | solution.py:271
  3.7 1.9 collective-permute-start.1
  5.6 5.9 %collective-permute-done.1.got = bf16[192,512]{1,0:T(8,128)(2,1)S(1)} collective-permute-done((bf16[192,512]{1,0:T(8,128)(2,1)}, bf16[192,512]{1,0:T(8,128)(2,1)S(1)}, u32[]{:S(2)}, u32[]{:S(2)}) %collective-permute-start.1) | collective-permute-done | bytes 196640 | tf_op jit(solution)/shard_map/ppermute | solution.py:307
  11.5 12.1 %all-to-all-start = ((bf16[8,192,256]{2,1,0:T(8,128)(2,1)}), bf16[8,192,256]{2,1,0:T(8,128)(2,1)S(1)}, u32[]{:S(2)}, u32[]{:S(2)}) async-start(bf16[8,192,256]{2,1,0:T(8,128)(2,1)} %bitcast.9), calls=%async_computation | async-start | bytes 1572864 | tf_op jit(solution)/shard_map/all_to_all | solution.py:300
  24.3 3.2 %collective-permute-start.2 = (bf16[384,512]{1,0:T(8,128)(2,1)}, bf16[384,512]{1,0:T(8,128)(2,1)S(1)}, u32[]{:S(2)}, u32[]{:S(2)}) collective-permute-start(bf16[384,512]{1,0:T(8,128)(2,1)} %join.2.refs_0_), channel_id=1, source_target_pairs={{0,16},{16,32},{32,48},{48,0},{64,80},{80,96},{96,112},{112,64},{1... | collective-permute-start | bytes 1179656 | tf_op jit(solution)/shard_map/ppermute | solution.py:297
  27.6 3.2 %constant_dynamic-slice_fusion = (bf16[256,1280]{1,0:T(8,128)(2,1)}, bf16[256,1280]{1,0:T(8,128)(2,1)}, bf16[256,1280]{1,0:T(8,128)(2,1)}, bf16[256,1280]{1,0:T(8,128)(2,1)}) fusion(bf16[256,5120]{1,0:T(8,128)(2,1)} %param.18, s32[]{:T(128)S(6)} %select_n.66, s32[]{:T(128)S(6)} %select_n.64, s32[]{:T(128)S(6)} %select_n.62, s32[]{:T(128)S(6)} %select_n.60), kind=kLoop, calls=%fused_computation | loop fusion | bytes 5242896 | tf_op jit(solution)/shard_map/dynamic_slice | solution.py:305
  30.9 2.1 %collective-permute-start = (bf16[256,1280]{1,0:T(8,128)(2,1)}, bf16[256,1280]{1,0:T(8,128)(2,1)S(1)}, u32[]{:S(2)}, u32[]{:S(2)}) collective-permute-start(bf16[256,1280]{1,0:T(8,128)(2,1)} %get-tuple-element.44), channel_id=1, source_target_pairs={{0,4},{1,5},{2,6},{3,7},{4,8},{5,9},{6,10},{7,11},{8,12},{9,13},{1... | collective-permute-start | bytes 1966088 | tf_op jit(solution)/shard_map/ppermute | solution.py:308
  33.0 3.2 %collective-permute-start.4 = (bf16[256,1280]{1,0:T(8,128)(2,1)}, bf16[256,1280]{1,0:T(8,128)(2,1)S(1)}, u32[]{:S(2)}, u32[]{:S(2)}) collective-permute-start(bf16[256,1280]{1,0:T(8,128)(2,1)} %get-tuple-element.42), channel_id=1, source_target_pairs={{0,12},{1,13},{2,14},{3,15},{4,0},{5,1},{6,2},{7,3},{8,4},{9,5},{1... | collective-permute-start | bytes 1966088 | tf_op jit(solution)/shard_map/ppermute | solution.py:308
  36.1 3.0 %collective-permute-start.3 = (bf16[256,1280]{1,0:T(8,128)(2,1)}, bf16[256,1280]{1,0:T(8,128)(2,1)S(1)}, u32[]{:S(2)}, u32[]{:S(2)}) collective-permute-start(bf16[256,1280]{1,0:T(8,128)(2,1)} %get-tuple-element.28), channel_id=1, source_target_pairs={{0,8},{1,9},{2,10},{3,11},{4,12},{5,13},{6,14},{7,15},{8,0},{9,1},... | collective-permute-start | bytes 1966088 | tf_op jit(solution)/shard_map/ppermute | solution.py:313
  39.2 2.2 %collective-permute-start.5 = (bf16[384,512]{1,0:T(8,128)(2,1)}, bf16[384,512]{1,0:T(8,128)(2,1)S(1)}, u32[]{:S(2)}, u32[]{:S(2)}) collective-permute-start(bf16[384,512]{1,0:T(8,128)(2,1)} %join.2.refs_0_), channel_id=1, source_target_pairs={{0,48},{16,0},{32,16},{48,32},{64,112},{80,64},{96,80},{112,96},{1... | collective-permute-start | bytes 1179656 | tf_op jit(solution)/shard_map/ppermute | solution.py:297
  41.4 3.8 %collective-permute-start.6 = (bf16[384,512]{1,0:T(8,128)(2,1)}, bf16[384,512]{1,0:T(8,128)(2,1)S(1)}, u32[]{:S(2)}, u32[]{:S(2)}) collective-permute-start(bf16[384,512]{1,0:T(8,128)(2,1)} %join.2.refs_0_), channel_id=1, source_target_pairs={{0,32},{16,48},{32,0},{48,16},{64,96},{80,112},{96,64},{112,80},{1... | collective-permute-start | bytes 1179656 | tf_op jit(solution)/shard_map/ppermute | solution.py:297
  45.2 3.5 %collective-permute-done.5.refs_2_ = bf16[384,512]{1,0:T(8,128)(2,1)S(1)} collective-permute-done((bf16[384,512]{1,0:T(8,128)(2,1)}, bf16[384,512]{1,0:T(8,128)(2,1)S(1)}, u32[]{:S(2)}, u32[]{:S(2)}) %collective-permute-start.5) | collective-permute-done | bytes 393248 | tf_op jit(solution)/shard_map/ppermute | solution.py:297
  48.7 9.1 %collective-permute-done.6.refs_3_ = bf16[384,512]{1,0:T(8,128)(2,1)S(1)} collective-permute-done((bf16[384,512]{1,0:T(8,128)(2,1)}, bf16[384,512]{1,0:T(8,128)(2,1)S(1)}, u32[]{:S(2)}, u32[]{:S(2)}) %collective-permute-start.6) | collective-permute-done | bytes 393248 | tf_op jit(solution)/shard_map/ppermute | solution.py:297
  60.4 9.6 %attend.1 = bf16[1664,256]{1,0:T(8,128)(2,1)} custom-call(bf16[384,512]{1,0:T(8,128)(2,1)} %join.2.refs_0_, bf16[384,512]{1,0:T(8,128)(2,1)S(1)} %collective-permute-done.2.refs_1_, bf16[384,512]{1,0:T(8,128)(2,1)S(1)} %collective-permute-done.5.refs_2_, bf16[384,512]{1,0:T(8,128)(2,1)S(1)} %copy-done.8, bf16[1536,256]{1,0:T(8,128)(2,1)S(1)} %bitcast.8), custom_call_target="tpu_custom_call" | custom-call | tf_op jit(solution)/shard_map/attend/pallas_call | solution.py:316
  71.4 8.5 %all-to-all-start.1 = ((bf16[8,208,256]{2,1,0:T(8,128)(2,1)}), bf16[8,208,256]{2,1,0:T(8,128)(2,1)S(1)}, u32[]{:S(2)}, u32[]{:S(2)}) async-start(bf16[8,208,256]{2,1,0:T(8,128)(2,1)} %bitcast.5), calls=%async_computation.1 | async-start | bytes 1703936 | tf_op jit(solution)/shard_map/all_to_all | solution.py:300
  85.1 6.6 %collective-permute-start.11 = (bf16[1024,1280]{1,0:T(8,128)(2,1)S(1)}, bf16[1024,1280]{1,0:T(8,128)(2,1)}, u32[]{:S(2)}, u32[]{:S(2)}) collective-permute-start(bf16[1024,1280]{1,0:T(8,128)(2,1)S(1)} %stack.1.refs_4_), channel_id=1, source_target_pairs={{0,1},{1,0},{2,3},{3,2},{4,5},{5,4},{6,7},{7,6},{8,9},{9,8},{10,11... | collective-permute-start | bytes 7864328 | tf_op jit(solution)/shard_map/ppermute | solution.py:352
  91.7 26.0 %all-to-all-done.1 = bf16[8,208,256]{2,1,0:T(8,128)(2,1)S(1)} async-done(((bf16[8,208,256]{2,1,0:T(8,128)(2,1)}), bf16[8,208,256]{2,1,0:T(8,128)(2,1)S(1)}, u32[]{:S(2)}, u32[]{:S(2)}) %all-to-all-start.1) | async-done | bytes 852000 | tf_op jit(solution)/shard_map/all_to_all | solution.py:300
  117.7 2.9 %merge.1 = (bf16[192,512]{1,0:T(8,128)(2,1)}, bf16[192,256]{1,0:T(8,128)(2,1)}) custom-call(s32[1]{0:T(128)} %bitcast.core, bf16[1664,256]{1,0:T(8,128)(2,1)S(1)} %bitcast.7), custom_call_target="tpu_custom_call" | custom-call | tf_op jit(solution)/shard_map/merge/pallas_call | solution.py:334
  120.7 5.5 %collective-permute-start.7 = (bf16[192,256]{1,0:T(8,128)(2,1)}, bf16[192,256]{1,0:T(8,128)(2,1)S(1)}, u32[]{:S(2)}, u32[]{:S(2)}) collective-permute-start(bf16[192,256]{1,0:T(8,128)(2,1)} %get-tuple-element.32), channel_id=1, source_target_pairs={{0,1},{1,0},{2,3},{3,2},{4,5},{5,4},{6,7},{7,6},{8,9},{9,8},{10,11... | collective-permute-start | bytes 294920 | tf_op jit(solution)/shard_map/ppermute | solution.py:353
  126.2 1.1 collective-permute-done.7.got
  128.0 3.7 %collective-permute-start.8 = (bf16[192,512]{1,0:T(8,128)(2,1)}, bf16[192,512]{1,0:T(8,128)(2,1)S(1)}, u32[]{:S(2)}, u32[]{:S(2)}) collective-permute-start(bf16[192,512]{1,0:T(8,128)(2,1)} %join.3.refs_0_), channel_id=1, source_target_pairs={{0,4},{1,5},{2,6},{3,7},{4,8},{5,9},{6,10},{7,11},{8,12},{9,13},{1... | collective-permute-start | bytes 589832 | tf_op jit(solution)/shard_map/ppermute | solution.py:354
  131.7 2.7 %collective-permute-start.9 = (bf16[192,512]{1,0:T(8,128)(2,1)}, bf16[192,512]{1,0:T(8,128)(2,1)S(1)}, u32[]{:S(2)}, u32[]{:S(2)}) collective-permute-start(bf16[192,512]{1,0:T(8,128)(2,1)} %join.3.refs_0_), channel_id=1, source_target_pairs={{0,8},{1,9},{2,10},{3,11},{4,12},{5,13},{6,14},{7,15},{8,0},{9,1},... | collective-permute-start | bytes 589832 | tf_op jit(solution)/shard_map/ppermute | solution.py:354
  134.4 2.0 %collective-permute-start.10 = (bf16[192,512]{1,0:T(8,128)(2,1)}, bf16[192,512]{1,0:T(8,128)(2,1)S(1)}, u32[]{:S(2)}, u32[]{:S(2)}) collective-permute-start(bf16[192,512]{1,0:T(8,128)(2,1)} %join.3.refs_0_), channel_id=1, source_target_pairs={{0,12},{1,13},{2,14},{3,15},{4,0},{5,1},{6,2},{7,3},{8,4},{9,5},{1... | collective-permute-start | bytes 589832 | tf_op jit(solution)/shard_map/ppermute | solution.py:354
  136.6 4.5 %collective-permute-done.9.refs_2_ = bf16[192,512]{1,0:T(8,128)(2,1)S(1)} collective-permute-done((bf16[192,512]{1,0:T(8,128)(2,1)}, bf16[192,512]{1,0:T(8,128)(2,1)S(1)}, u32[]{:S(2)}, u32[]{:S(2)}) %collective-permute-start.9) | collective-permute-done | bytes 196640 | tf_op jit(solution)/shard_map/ppermute | solution.py:354
  141.1 4.9 %collective-permute-done.10.refs_3_ = bf16[192,512]{1,0:T(8,128)(2,1)S(1)} collective-permute-done((bf16[192,512]{1,0:T(8,128)(2,1)}, bf16[192,512]{1,0:T(8,128)(2,1)S(1)}, u32[]{:S(2)}, u32[]{:S(2)}) %collective-permute-start.10) | collective-permute-done | bytes 196640 | tf_op jit(solution)/shard_map/ppermute | solution.py:354
  146.0 2.8 %project.3 = (bf16[192,320]{1,0:T(8,128)(2,1)S(1)}, bf16[192,320]{1,0:T(8,128)(2,1)S(1)}) custom-call(s32[2]{0:T(128)S(1)} %pad_add_fusion.1.place, bf16[192,512]{1,0:T(8,128)(2,1)} %join.3.refs_0_, bf16[192,512]{1,0:T(8,128)(2,1)S(1)} %collective-permute-done.8.refs_1_, bf16[192,512]{1,0:T(8,128)(2,1)S(1)} %collective-permute-done.9.refs_2_, ...), custom_call_target="tpu_custom_call" | custom-call | tf_op jit(solution)/shard_map/project/pallas_call | solution.py:357
  148.9 8.1 %collective-permute-start.12 = (bf16[192,320]{1,0:T(8,128)(2,1)S(1)}, bf16[192,320]{1,0:T(8,128)(2,1)S(1)}, u32[]{:S(2)}, u32[]{:S(2)}) collective-permute-start(bf16[192,320]{1,0:T(8,128)(2,1)S(1)} %get-tuple-element.39), channel_id=1, source_target_pairs={{0,2},{1,3},{2,0},{3,1},{4,6},{5,7},{6,4},{7,5},{8,10},{9,11},{10,... | collective-permute-start | bytes 368648 | tf_op jit(solution)/shard_map/ppermute | solution.py:368
  157.0 2.8 %project.2 = (f32[192,320]{1,0:T(8,128)S(1)}, bf16[192,320]{1,0:T(8,128)(2,1)S(1)}) custom-call(s32[2]{0:T(128)S(1)} %pad_add_fusion.place, bf16[192,512]{1,0:T(8,128)(2,1)} %join.3.refs_0_, bf16[192,512]{1,0:T(8,128)(2,1)S(1)} %collective-permute-done.8.refs_1_, bf16[192,512]{1,0:T(8,128)(2,1)S(1)} %collective-permute-done.9.refs_2_, ...), custom_call_target="tpu_custom_call" | custom-call | tf_op jit(solution)/shard_map/project/pallas_call | solution.py:357
  159.8 3.0 %collective-permute-start.13 = (bf16[192,320]{1,0:T(8,128)(2,1)S(1)}, bf16[192,320]{1,0:T(8,128)(2,1)S(1)}, u32[]{:S(2)}, u32[]{:S(2)}) collective-permute-start(bf16[192,320]{1,0:T(8,128)(2,1)S(1)} %get-tuple-element.40), channel_id=1, source_target_pairs={{0,1},{1,0},{2,3},{3,2},{4,5},{5,4},{6,7},{7,6},{8,9},{9,8},{10,11... | collective-permute-start | bytes 368648 | tf_op jit(solution)/shard_map/ppermute | solution.py:370
  162.8 6.0 %collective-permute-start.14 = (bf16[192,320]{1,0:T(8,128)(2,1)S(1)}, bf16[192,320]{1,0:T(8,128)(2,1)S(1)}, u32[]{:S(2)}, u32[]{:S(2)}) collective-permute-start(bf16[192,320]{1,0:T(8,128)(2,1)S(1)} %get-tuple-element.41), channel_id=1, source_target_pairs={{0,3},{1,2},{2,1},{3,0},{4,7},{5,6},{6,5},{7,4},{8,11},{9,10},{10,... | collective-permute-start | bytes 368648 | tf_op jit(solution)/shard_map/ppermute | solution.py:369
  169.7 21.4 %collective-permute-done.14.both_got = bf16[192,320]{1,0:T(8,128)(2,1)S(1)} collective-permute-done((bf16[192,320]{1,0:T(8,128)(2,1)S(1)}, bf16[192,320]{1,0:T(8,128)(2,1)S(1)}, u32[]{:S(2)}, u32[]{:S(2)}) %collective-permute-start.14) | collective-permute-done | bytes 122912 | tf_op jit(solution)/shard_map/ppermute | solution.py:369
  191.1 1.4 finish.1
  (41 shorter events, 11.5 us)
Async XLA Ops:
  3.7 7.9 %collective-permute-start.1 = (bf16[192,512]{1,0:T(8,128)(2,1)}, bf16[192,512]{1,0:T(8,128)(2,1)S(1)}, u32[]{:S(2)}, u32[]{:S(2)}) collective-permute-start(bf16[192,512]{1,0:T(8,128)(2,1)} %get-tuple-element.25), channel_id=1, source_target_pairs={{0,64},{16,80},{32,96},{48,112},{64,0},{80,16},{96,32},{112,48},{1... | collective-permute-start | bytes 589832 | tf_op jit(solution)/shard_map/ppermute | solution.py:307
  11.5 47.9 %all-to-all-start = ((bf16[8,192,256]{2,1,0:T(8,128)(2,1)}), bf16[8,192,256]{2,1,0:T(8,128)(2,1)S(1)}, u32[]{:S(2)}, u32[]{:S(2)}) async-start(bf16[8,192,256]{2,1,0:T(8,128)(2,1)} %bitcast.9), calls=%async_computation | async-start | bytes 1572864 | tf_op jit(solution)/shard_map/all_to_all | solution.py:300
  24.3 11.8 %collective-permute-start.2 = (bf16[384,512]{1,0:T(8,128)(2,1)}, bf16[384,512]{1,0:T(8,128)(2,1)S(1)}, u32[]{:S(2)}, u32[]{:S(2)}) collective-permute-start(bf16[384,512]{1,0:T(8,128)(2,1)} %join.2.refs_0_), channel_id=1, source_target_pairs={{0,16},{16,32},{32,48},{48,0},{64,80},{80,96},{96,112},{112,64},{1... | collective-permute-start | bytes 1179656 | tf_op jit(solution)/shard_map/ppermute | solution.py:297
  30.9 39.2 %collective-permute-start = (bf16[256,1280]{1,0:T(8,128)(2,1)}, bf16[256,1280]{1,0:T(8,128)(2,1)S(1)}, u32[]{:S(2)}, u32[]{:S(2)}) collective-permute-start(bf16[256,1280]{1,0:T(8,128)(2,1)} %get-tuple-element.44), channel_id=1, source_target_pairs={{0,4},{1,5},{2,6},{3,7},{4,8},{5,9},{6,10},{7,11},{8,12},{9,13},{1... | collective-permute-start | bytes 1966088 | tf_op jit(solution)/shard_map/ppermute | solution.py:308
  33.0 37.1 %collective-permute-start.4 = (bf16[256,1280]{1,0:T(8,128)(2,1)}, bf16[256,1280]{1,0:T(8,128)(2,1)S(1)}, u32[]{:S(2)}, u32[]{:S(2)}) collective-permute-start(bf16[256,1280]{1,0:T(8,128)(2,1)} %get-tuple-element.42), channel_id=1, source_target_pairs={{0,12},{1,13},{2,14},{3,15},{4,0},{5,1},{6,2},{7,3},{8,4},{9,5},{1... | collective-permute-start | bytes 1966088 | tf_op jit(solution)/shard_map/ppermute | solution.py:308
  36.1 34.0 %collective-permute-start.3 = (bf16[256,1280]{1,0:T(8,128)(2,1)}, bf16[256,1280]{1,0:T(8,128)(2,1)S(1)}, u32[]{:S(2)}, u32[]{:S(2)}) collective-permute-start(bf16[256,1280]{1,0:T(8,128)(2,1)} %get-tuple-element.28), channel_id=1, source_target_pairs={{0,8},{1,9},{2,10},{3,11},{4,12},{5,13},{6,14},{7,15},{8,0},{9,1},... | collective-permute-start | bytes 1966088 | tf_op jit(solution)/shard_map/ppermute | solution.py:313
  39.2 9.5 %collective-permute-start.5 = (bf16[384,512]{1,0:T(8,128)(2,1)}, bf16[384,512]{1,0:T(8,128)(2,1)S(1)}, u32[]{:S(2)}, u32[]{:S(2)}) collective-permute-start(bf16[384,512]{1,0:T(8,128)(2,1)} %join.2.refs_0_), channel_id=1, source_target_pairs={{0,48},{16,0},{32,16},{48,32},{64,112},{80,64},{96,80},{112,96},{1... | collective-permute-start | bytes 1179656 | tf_op jit(solution)/shard_map/ppermute | solution.py:297
  41.4 16.4 %collective-permute-start.6 = (bf16[384,512]{1,0:T(8,128)(2,1)}, bf16[384,512]{1,0:T(8,128)(2,1)S(1)}, u32[]{:S(2)}, u32[]{:S(2)}) collective-permute-start(bf16[384,512]{1,0:T(8,128)(2,1)} %join.2.refs_0_), channel_id=1, source_target_pairs={{0,32},{16,48},{32,0},{48,16},{64,96},{80,112},{96,64},{112,80},{1... | collective-permute-start | bytes 1179656 | tf_op jit(solution)/shard_map/ppermute | solution.py:297
  57.8 0.8 copy-start.7
  59.4 1.0 copy-start.8
  70.1 1.1 copy-start.1
  70.1 1.3 copy-start.3
  70.1 0.9 copy-start.5
  71.4 46.4 %all-to-all-start.1 = ((bf16[8,208,256]{2,1,0:T(8,128)(2,1)}), bf16[8,208,256]{2,1,0:T(8,128)(2,1)S(1)}, u32[]{:S(2)}, u32[]{:S(2)}) async-start(bf16[8,208,256]{2,1,0:T(8,128)(2,1)} %bitcast.5), calls=%async_computation.1 | async-start | bytes 1703936 | tf_op jit(solution)/shard_map/all_to_all | solution.py:300
  79.9 1.1 copy-start
  80.9 1.1 copy-start.2
  82.0 1.1 copy-start.4
  83.1 1.1 copy-start.6
  85.1 51.5 %collective-permute-start.11 = (bf16[1024,1280]{1,0:T(8,128)(2,1)S(1)}, bf16[1024,1280]{1,0:T(8,128)(2,1)}, u32[]{:S(2)}, u32[]{:S(2)}) collective-permute-start(bf16[1024,1280]{1,0:T(8,128)(2,1)S(1)} %stack.1.refs_4_), channel_id=1, source_target_pairs={{0,1},{1,0},{2,3},{3,2},{4,5},{5,4},{6,7},{7,6},{8,9},{9,8},{10,11... | collective-permute-start | bytes 7864328 | tf_op jit(solution)/shard_map/ppermute | solution.py:352
  120.7 6.6 %collective-permute-start.7 = (bf16[192,256]{1,0:T(8,128)(2,1)}, bf16[192,256]{1,0:T(8,128)(2,1)S(1)}, u32[]{:S(2)}, u32[]{:S(2)}) collective-permute-start(bf16[192,256]{1,0:T(8,128)(2,1)} %get-tuple-element.32), channel_id=1, source_target_pairs={{0,1},{1,0},{2,3},{3,2},{4,5},{5,4},{6,7},{7,6},{8,9},{9,8},{10,11... | collective-permute-start | bytes 294920 | tf_op jit(solution)/shard_map/ppermute | solution.py:353
  128.0 8.6 %collective-permute-start.8 = (bf16[192,512]{1,0:T(8,128)(2,1)}, bf16[192,512]{1,0:T(8,128)(2,1)S(1)}, u32[]{:S(2)}, u32[]{:S(2)}) collective-permute-start(bf16[192,512]{1,0:T(8,128)(2,1)} %join.3.refs_0_), channel_id=1, source_target_pairs={{0,4},{1,5},{2,6},{3,7},{4,8},{5,9},{6,10},{7,11},{8,12},{9,13},{1... | collective-permute-start | bytes 589832 | tf_op jit(solution)/shard_map/ppermute | solution.py:354
  131.7 9.4 %collective-permute-start.9 = (bf16[192,512]{1,0:T(8,128)(2,1)}, bf16[192,512]{1,0:T(8,128)(2,1)S(1)}, u32[]{:S(2)}, u32[]{:S(2)}) collective-permute-start(bf16[192,512]{1,0:T(8,128)(2,1)} %join.3.refs_0_), channel_id=1, source_target_pairs={{0,8},{1,9},{2,10},{3,11},{4,12},{5,13},{6,14},{7,15},{8,0},{9,1},... | collective-permute-start | bytes 589832 | tf_op jit(solution)/shard_map/ppermute | solution.py:354
  134.4 11.6 %collective-permute-start.10 = (bf16[192,512]{1,0:T(8,128)(2,1)}, bf16[192,512]{1,0:T(8,128)(2,1)S(1)}, u32[]{:S(2)}, u32[]{:S(2)}) collective-permute-start(bf16[192,512]{1,0:T(8,128)(2,1)} %join.3.refs_0_), channel_id=1, source_target_pairs={{0,12},{1,13},{2,14},{3,15},{4,0},{5,1},{6,2},{7,3},{8,4},{9,5},{1... | collective-permute-start | bytes 589832 | tf_op jit(solution)/shard_map/ppermute | solution.py:354
  148.8 19.9 %copy-start.12 = (f32[320]{0:T(512)S(1)}, f32[320]{0:T(512)}, u32[]{:S(2)}) copy-start(f32[320]{0:T(512)} %param.19) | copy-start | bytes 3844
  148.9 42.3 %copy-start.9 = (bf16[192,320]{1,0:T(8,128)(2,1)S(1)}, bf16[192,320]{1,0:T(8,128)(2,1)}, u32[]{:S(2)}) copy-start(bf16[192,320]{1,0:T(8,128)(2,1)} %tokens.1) | copy-start | bytes 368644
  148.9 42.2 %copy-start.10 = (bf16[192,320]{1,0:T(8,128)(2,1)S(1)}, bf16[192,320]{1,0:T(8,128)(2,1)}, u32[]{:S(2)}) copy-start(bf16[192,320]{1,0:T(8,128)(2,1)} %d_tokens.1) | copy-start | bytes 368644
  148.9 42.2 %copy-start.11 = (s32[192]{0:T(256)S(1)}, s32[192]{0:T(256)}, u32[]{:S(2)}) copy-start(s32[192]{0:T(256)} %flags.3) | copy-start | bytes 2308
  148.9 20.8 %collective-permute-start.12 = (bf16[192,320]{1,0:T(8,128)(2,1)S(1)}, bf16[192,320]{1,0:T(8,128)(2,1)S(1)}, u32[]{:S(2)}, u32[]{:S(2)}) collective-permute-start(bf16[192,320]{1,0:T(8,128)(2,1)S(1)} %get-tuple-element.39), channel_id=1, source_target_pairs={{0,2},{1,3},{2,0},{3,1},{4,6},{5,7},{6,4},{7,5},{8,10},{9,11},{10,... | collective-permute-start | bytes 368648 | tf_op jit(solution)/shard_map/ppermute | solution.py:368
  159.8 9.9 %collective-permute-start.13 = (bf16[192,320]{1,0:T(8,128)(2,1)S(1)}, bf16[192,320]{1,0:T(8,128)(2,1)S(1)}, u32[]{:S(2)}, u32[]{:S(2)}) collective-permute-start(bf16[192,320]{1,0:T(8,128)(2,1)S(1)} %get-tuple-element.40), channel_id=1, source_target_pairs={{0,1},{1,0},{2,3},{3,2},{4,5},{5,4},{6,7},{7,6},{8,9},{9,8},{10,11... | collective-permute-start | bytes 368648 | tf_op jit(solution)/shard_map/ppermute | solution.py:370
  162.8 28.3 %collective-permute-start.14 = (bf16[192,320]{1,0:T(8,128)(2,1)S(1)}, bf16[192,320]{1,0:T(8,128)(2,1)S(1)}, u32[]{:S(2)}, u32[]{:S(2)}) collective-permute-start(bf16[192,320]{1,0:T(8,128)(2,1)S(1)} %get-tuple-element.41), channel_id=1, source_target_pairs={{0,3},{1,2},{2,1},{3,0},{4,7},{5,6},{6,5},{7,4},{8,11},{9,10},{10,... | collective-permute-start | bytes 368648 | tf_op jit(solution)/shard_map/ppermute | solution.py:369

commit v3 on v2

v3 whole, which is shorter than its diff:
```python
import functools
import math

import jax
import jax.numpy as jnp
from jax import lax
from jax.experimental import pallas as pl
from jax.experimental.pallas import tpu as pltpu
from jax.sharding import PartitionSpec as P

HD = 128
FRAME = 32
NZ, NY, NX = 8, 4, 4
FACTOR = 1.0 / math.sqrt(HD)
LOG2E = math.log2(math.e)
STAT_ROWS = 16
BF = jnp.bfloat16
F32 = jnp.float32
def params(mib):
    return pltpu.CompilerParams(vmem_limit_bytes=mib * 1024 * 1024)


SMEM_SPEC = pl.BlockSpec(memory_space=pltpu.SMEM)
VMEM_SPEC = pl.BlockSpec(memory_space=pltpu.VMEM)
HBM_SPEC = pl.BlockSpec(memory_space=pltpu.HBM)


def over_z(k):
    return [(z * NY + y, (z ^ k) * NY + y) for z in range(NZ) for y in range(NY)]


def over_y(k):
    return [(z * NY + y, z * NY + (y + k) % NY) for z in range(NZ) for y in range(NY)]


def flip(bits):
    return [(i, i ^ bits) for i in range(4 * NX)]


def same_y():
    return [[z * NY + y for z in range(NZ)] for y in range(NY)]


def over_x(k):
    return [(x * 4 + r, (x + k) % NX * 4 + r) for x in range(NX) for r in range(4)]


def over_x_and_core():
    return [[x * 4 + h * 2 + c for x in range(NX) for c in range(2)] for h in range(2)]


def over_half_and_core():
    return [[x * 4 + r for r in range(4)] for x in range(NX)]


def load(sources, held, sems):
    copies = [pltpu.make_async_copy(a, b, sems.at[i]) for i, (a, b) in enumerate(zip(sources, held))]
    for copy in copies:
        copy.start()
    for copy in copies:
        copy.wait()


def run_all(copies):
    for copy in copies:
        copy.start()
    for copy in copies:
        copy.wait()


def masked_rows(flags, f, ref):
    block = ref[pl.ds(f * FRAME, FRAME), :]
    return jnp.where(flags[f * FRAME] > 0, block, jnp.zeros_like(block))


def pack_keys_kernel(odd, flags, *refs):
    sources, (kv_own, kv_other), held, (kv, other, sems) = refs[:4], refs[4:6], refs[6:10], refs[10:]
    load(sources, held, sems)
    k, v, dk, dv = held
    is_odd = odd[0] > 0
    rows_all = other.shape[0]
    for f in range(rows_all // FRAME):
        rows = pl.ds(f * FRAME, FRAME)
        blocks = (k[rows, :], masked_rows(flags, f, dk), v[rows, :], masked_rows(flags, f, dv))
        for i, block in enumerate(blocks):
            first, second = block[:, :HD], block[:, HD:]
            kv[rows, i * HD : (i + 1) * HD] = jnp.where(is_odd, second, first)
            other[rows, i * HD : (i + 1) * HD] = jnp.where(is_odd, first, second)
    run_all(
        [
            pltpu.make_async_copy(other, kv_other, sems.at[0]),
            pltpu.make_async_copy(kv, kv_own.at[pl.ds(0, rows_all)], sems.at[1]),
        ]
    )


def pack_queries_kernel(flags, q_in, dq_in, qd_out, q, dq, first, second, sems):
    load((q_in, dq_in), (q, dq), sems)
    rows_all = q.shape[0]
    for f in range(rows_all // FRAME):
        rows = pl.ds(f * FRAME, FRAME)
        for i, block in enumerate((masked_rows(flags, f, dq), q[rows, :])):
            first[rows, i * HD : (i + 1) * HD] = block[:, :HD]
            second[rows, i * HD : (i + 1) * HD] = block[:, HD:]
    run_all(
        [
            pltpu.make_async_copy(
                second if i % 2 else first, qd_out.at[pl.ds(i * rows_all, rows_all)], sems.at[i]
            )
            for i in range(NZ)
        ]
    )


def join_kernel(got, own_in, own, sem):
    del own_in
    rows = got.shape[0]
    copy = pltpu.make_async_copy(got, own.at[pl.ds(rows, rows)], sem)
    copy.start()
    copy.wait()


def in_three(value):
    high = value.astype(BF).astype(F32)
    middle = (value - high).astype(BF).astype(F32)
    low = (value - high - middle).astype(BF).astype(F32)
    return high, middle, low


def attend_kernel(*refs):
    kv_in, qd_in, out = refs[:4], refs[4], refs[5]
    kv, qd, held, sems = refs[6:]
    rows = kv_in[0].shape[0]
    run_all(
        [
            pltpu.make_async_copy(kv_in[i], kv.at[pl.ds(i * rows, rows)], sems.at[i])
            for i in range(4)
        ]
        + [pltpu.make_async_copy(qd_in, qd, sems.at[4])]
    )
    contract = (((1,), (1,)), ((), ()))
    steps = qd.shape[0] // rows
    blocks = NZ // steps
    block = rows // blocks

    for j in range(steps):
        both = qd[j * rows : (j + 1) * rows, :]
        scores = lax.dot_general(both[:, HD:], kv[:, :HD], contract, preferred_element_type=F32)
        slopes = lax.dot_general(both, kv[:, : 2 * HD], contract, preferred_element_type=F32)
        peak = jnp.max(scores, axis=1, keepdims=True) * (FACTOR * LOG2E)
        weights = jnp.exp2(scores * (FACTOR * LOG2E) - peak)
        total = jnp.sum(weights, axis=1, keepdims=True)
        product = weights * slopes
        slope = jnp.sum(product, axis=1, keepdims=True)
        weighted = jnp.dot(weights.astype(BF), kv[:, 2 * HD :], preferred_element_type=F32)
        tangent = jnp.dot(product.astype(BF), kv[:, 2 * HD : 3 * HD], preferred_element_type=F32)
        inverse = 1.0 / total
        mean = slope * (inverse * FACTOR)
        primal = weighted[:, :HD] * inverse
        tangent = (tangent * FACTOR + weighted[:, HD:]) * inverse - mean * primal
        lanes = lax.broadcasted_iota(jnp.int32, (rows, HD), 1)
        stats = jnp.zeros((rows, HD), F32)
        for i, part in enumerate(in_three(peak + jnp.log2(total)) + in_three(mean)):
            stats = jnp.where(lanes == i, part, stats)
        for p in range(blocks):
            mine = slice(p * block, (p + 1) * block)
            at = p * (block + STAT_ROWS)
            held[j, at : at + block, :HD] = primal[mine].astype(BF)
            held[j, at : at + block, HD:] = tangent[mine].astype(BF)
            tile = jnp.concatenate([stats[mine], jnp.zeros((2 * HD - block, HD), F32)], axis=0)
            held[j, at + block : at + block + STAT_ROWS, :] = tile.T[:STAT_ROWS].astype(BF)
    count = held.shape[1]
    run_all(
        [
            pltpu.make_async_copy(held.at[i], out.at[pl.ds(i * count, count)], sems.at[i])
            for i in range(steps)
        ]
    )


def merge_kernel(parts, out, merged, sems):
    rows = merged.shape[1]
    step = rows + STAT_ROWS
    tiles = [parts[i * step + rows : (i + 1) * step, :].astype(F32) for i in range(NZ)]
    stats = jnp.concatenate(tiles, axis=0).T[:rows]

    def value(i, first):
        lane = i * STAT_ROWS + first
        return sum(stats[:, lane + j : lane + j + 1] for j in range(3))

    for h in range(2):
        group = range(h, NZ, 2)
        sizes = [value(i, 0) for i in group]
        means = [value(i, 3) for i in group]
        peak = functools.reduce(jnp.maximum, sizes)
        sizes = [jnp.exp2(size - peak) for size in sizes]
        inverse = 1.0 / sum(sizes)
        sizes = [size * inverse for size in sizes]
        mean = sum(size * m for size, m in zip(sizes, means))
        primal = jnp.zeros((rows, HD), F32)
        tangent = jnp.zeros((rows, HD), F32)
        for i, size, m in zip(group, sizes, means):
            at = i * step
            a = parts[at : at + rows, :HD].astype(F32)
            primal += size * a
            tangent += size * parts[at : at + rows, HD:].astype(F32) + (size * (m - mean)) * a
        at = slice(h * HD, (h + 1) * HD)
        merged[0, :, at] = primal.astype(BF)
        merged[1, :, at] = tangent.astype(BF)
    run_all(
        [pltpu.make_async_copy(merged, out.at[pl.ds(2 * i, 2)], sems.at[i]) for i in range(NX)]
    )


def stack_kernel(*refs):
    pieces, out, sems = refs[:NX], refs[NX], refs[NX + 1]
    run_all([pltpu.make_async_copy(pieces[i], out.at[i], sems.at[i]) for i in range(NX)])


def project_kernel(place, acts, w_own, w_other, out):
    width = out.shape[2]
    core, x = place[0], place[1]
    for half in range(2):
        columns = slice(2 * half * width, 2 * (half + 1) * width)
        total = jnp.zeros((out.shape[1], 2 * width), F32)
        for k in range(NX):
            i = 2 * lax.rem(x + NX - k, NX)
            total += jnp.dot(acts[i + core], w_own[k, :, columns], preferred_element_type=F32)
            total += jnp.dot(acts[i + 1 - core], w_other[k, :, columns], preferred_element_type=F32)
        out[2 * half] = total[:, :width].astype(BF)
        out[2 * half + 1] = total[:, width:].astype(BF)


def finish_kernel(flags, got, gate, tokens, d_tokens, result, d_result):
    scale = gate[...]
    for f in range(tokens.shape[0] // FRAME):
        rows = pl.ds(f * FRAME, FRAME)
        live = flags[f * FRAME] > 0
        primal = got[0, rows, :].astype(F32) + got[2, rows, :].astype(F32)
        tangent = got[1, rows, :].astype(F32) + got[3, rows, :].astype(F32)
        base = tokens[rows, :].astype(F32)
        d_base = d_tokens[rows, :].astype(F32)
        d_base = jnp.where(live, d_base, jnp.zeros_like(d_base))
        result[rows, :] = (base + scale * primal).astype(BF)
        d_result[rows, :] = (d_base + scale * tangent).astype(BF)


def per_device(
    queries,
    d_queries,
    key_rows,
    value_rows,
    d_key_rows,
    d_value_rows,
    live_flags,
    out_weight,
    gate_scale,
    tokens,
    d_tokens,
):
    rows, width = queries.shape
    columns = tokens.shape[1]
    t, m = lax.axis_index("tm"), lax.axis_index("mp")
    odd = (t // NY % 2).astype(jnp.int32).reshape(1)
    core = (m % 2).astype(jnp.int32).reshape(1)
    x = (m // 4).astype(jnp.int32).reshape(1)
    group = 4 * columns

    def shape(*dims):
        return jax.ShapeDtypeStruct(dims, BF)

    def after(a, b):
        return lax.optimization_barrier((a, b))[0]

    def exchange(a, axis, groups):
        return lax.all_to_all(a, axis, 0, 0, axis_index_groups=groups, tiled=True)

    def y(a, k):
        return lax.ppermute(a, "tm", over_y(k))

    kv, kv_other = pl.pallas_call(
        pack_keys_kernel,
        out_shape=[shape(2 * rows, 4 * HD), shape(rows, 4 * HD)],
        in_specs=[SMEM_SPEC] * 2 + [HBM_SPEC] * 4,
        out_specs=[HBM_SPEC] * 2,
        scratch_shapes=[pltpu.VMEM((rows, width), BF)] * 4
        + [pltpu.VMEM((rows, 4 * HD), BF)] * 2
        + [pltpu.SemaphoreType.DMA((4,))],
        compiler_params=params(60),
        name="pack_keys",
    )(odd, live_flags, key_rows, value_rows, d_key_rows, d_value_rows)
    kv_got = lax.ppermute(kv_other, "tm", over_z(1))

    queries, out_weight = after((queries, out_weight), kv)
    weights = [
        lax.dynamic_slice(out_weight, (0, (x[0] + k) % NX * group), (width, group))
        for k in range(NX)
    ]
    qd = pl.pallas_call(
        pack_queries_kernel,
        out_shape=shape(NZ * rows, 2 * HD),
        in_specs=[SMEM_SPEC] + [HBM_SPEC] * 2,
        out_specs=HBM_SPEC,
        scratch_shapes=[pltpu.VMEM((rows, width), BF)] * 2
        + [pltpu.VMEM((rows, 2 * HD), BF)] * 2
        + [pltpu.SemaphoreType.DMA((NZ,))],
        compiler_params=params(60),
        name="pack_queries",
    )(live_flags, queries, d_queries)
    qd, kv_got = lax.optimization_barrier((qd, kv_got))
    qd = exchange(qd, "tm", same_y())

    kv = pl.pallas_call(
        join_kernel,
        out_shape=shape(2 * rows, 4 * HD),
        in_specs=[HBM_SPEC] * 2,
        out_specs=HBM_SPEC,
        scratch_shapes=[pltpu.SemaphoreType.DMA],
        input_output_aliases={1: 0},
        compiler_params=params(8),
        name="join",
    )(kv_got, kv)
    weights = after(weights, kv)
    kv = [kv] + [y(kv, k) for k in (1, 3, 2)]

    for k in (1, 3):
        weights[k] = lax.ppermute(weights[k], "mp", over_x(k))
    qd = after(qd, weights)

    parts = pl.pallas_call(
        attend_kernel,
        out_shape=shape(NZ * (rows + STAT_ROWS), 2 * HD),
        in_specs=[HBM_SPEC] * 5,
        out_specs=HBM_SPEC,
        scratch_shapes=[
            pltpu.VMEM((NZ * rows, 4 * HD), BF),
            pltpu.VMEM((NZ * rows, 2 * HD), BF),
            pltpu.VMEM((4, 2 * (rows + STAT_ROWS), 2 * HD), BF),
            pltpu.SemaphoreType.DMA((5,)),
        ],
        compiler_params=params(60),
        name="attend",
    )(*kv, qd)
    weights[2] = lax.ppermute(after(weights[2], parts), "mp", over_x(2))
    parts = exchange(parts, "tm", same_y())

    w_own = pl.pallas_call(
        stack_kernel,
        out_shape=shape(NX, width, group),
        in_specs=[HBM_SPEC] * NX,
        out_specs=HBM_SPEC,
        scratch_shapes=[pltpu.SemaphoreType.DMA((NX,))],
        compiler_params=params(8),
        name="stack",
    )(*weights)
    w_other = lax.ppermute(w_own, "mp", flip(1))

    acts = pl.pallas_call(
        merge_kernel,
        out_shape=shape(2 * NX, rows, 2 * HD),
        in_specs=[VMEM_SPEC],
        out_specs=HBM_SPEC,
        scratch_shapes=[pltpu.VMEM((2, rows, 2 * HD), BF), pltpu.SemaphoreType.DMA((NX,))],
        compiler_params=params(60),
        name="merge",
    )(parts)
    acts = exchange(acts, "mp", over_x_and_core())

    sums = pl.pallas_call(
        project_kernel,
        out_shape=shape(4, rows, columns),
        in_specs=[SMEM_SPEC] + [VMEM_SPEC] * 3,
        out_specs=VMEM_SPEC,
        compiler_params=params(24),
        name="project",
    )(jnp.concatenate([core, x]), acts, w_own, w_other)
    got = exchange(sums, "mp", over_half_and_core())

    result, d_result = pl.pallas_call(
        finish_kernel,
        out_shape=[shape(rows, columns)] * 2,
        in_specs=[SMEM_SPEC] + [VMEM_SPEC] * 4,
        out_specs=[VMEM_SPEC] * 2,
        compiler_params=params(8),
        name="finish",
    )(live_flags, got, gate_scale.reshape(1, columns), tokens, d_tokens)
    return (result, d_result)


def solution(mesh):
    placed = (
        P("tm", "mp"),
        P("tm", "mp"),
        P("tm", "mp"),
        P("tm", "mp"),
        P("tm", "mp"),
        P("tm", "mp"),
        P("tm"),
        P("mp", None),
        P("mp"),
        P("tm", "mp"),
        P("tm", "mp"),
    )
    return jax.shard_map(
        per_device,
        mesh=mesh,
        in_specs=placed,
        out_specs=(P("tm", "mp"), P("tm", "mp")),
        check_vma=False,
    )
```

time: 194 us -> 190 us (0.979)
  the two profiles are of different devices: /device:TPU:47 before, /device:TPU:1 now
where the time goes in v3:
time: 190 us; the launch traced here: 187 us
  starting transfers between devices  83.8 us (44%)
  waiting for transfers between devices  68.9 us (36%)
  Pallas kernels  23.8 us (13%)
  local copies, waits for them, and re-layouts  8.73 us (5%)
    all_to_all x4, starting transfers between devices, exchange(): return lax.all_to_all(a, axis, 0, 0, axis_index_groups=groups, tiled=True)  53.3 us
    all_to_all x4, waiting for transfers between devices, exchange(): return lax.all_to_all(a, axis, 0, 0, axis_index_groups=groups, tiled=True)  49.7 us
    ppermute x1, waiting for transfers between devices, per_device(): weights[2] = lax.ppermute(after(weights[2], parts), 'mp', over_x(2))  13.1 us
    ppermute x3, starting transfers between devices, y(): return lax.ppermute(a, 'tm', over_y(k))  10.1 us
    pallas_call x1, Pallas kernels, per_device(): pl.pallas_call(attend_kernel, out_shape=shape(NZ * (rows + STAT_ROWS), 2...  9.16 us
    ppermute x2, starting transfers between devices, per_device(): weights[k] = lax.ppermute(weights[k], 'mp', over_x(k))  6.49 us
    unnamed x24, local copies, waits for them, and re-layouts  5.27 us
    ppermute x1, starting transfers between devices, per_device(): w_other = lax.ppermute(w_own, 'mp', flip(1))  4.92 us
  transfers between devices with their start and end apart: 12, of which 9 were waited for; matrix products, arithmetic and copies ran while one was open for 2% of the time, Pallas kernels for 4%

profile of v3, /device:TPU:1, one launch (start us, length us, event | category | flops | bytes accessed | tf_op | source)
XLA Modules:
  0.0 186.7 jit_solution(16526367461851752808)
XLA Ops:
  0.7 2.6 %pack_keys.1 = (bf16[384,512]{1,0:T(8,128)(2,1)}, bf16[192,512]{1,0:T(8,128)(2,1)}) custom-call(s32[1]{0:T(128)} %bitcast.2.odd, s32[192]{0:T(256)} %flags.5, bf16[192,256]{1,0:T(8,128)(2,1)} %refs_0_.1, bf16[192,256]{1,0:T(8,128)(2,1)} %refs_1_.1, bf16[192,256]{1,0:T(8,128)(2,1)} %refs_2_.1, bf16[192,256]{1,0:T(8,128)(2,1)} %refs_3_.1), custom_call_target="tpu_custom_call" | custom-call | tf_op jit(solution)/shard_map/pack_keys/pallas_call | solution.py:281
  3.3 4.4 %collective-permute-start = (bf16[192,512]{1,0:T(8,128)(2,1)}, bf16[192,512]{1,0:T(8,128)(2,1)S(1)}, u32[]{:S(2)}, u32[]{:S(2)}) collective-permute-start(bf16[192,512]{1,0:T(8,128)(2,1)} %get-tuple-element.16), channel_id=1, source_target_pairs={{0,64},{16,80},{32,96},{48,112},{64,0},{80,16},{96,32},{112,48},{1... | collective-permute-start | bytes 589832 | tf_op jit(solution)/shard_map/ppermute | solution.py:292
  7.6 2.6 %pack_queries.1 = bf16[1536,256]{1,0:T(8,128)(2,1)} custom-call(s32[192]{0:T(256)} %flags.5, bf16[192,256]{1,0:T(8,128)(2,1)} %q_in, bf16[192,256]{1,0:T(8,128)(2,1)} %dq_in.1), custom_call_target="tpu_custom_call" | custom-call | tf_op jit(solution)/shard_map/pack_queries/pallas_call | solution.py:299
  10.9 13.3 %all-to-all-start = ((bf16[8,192,256]{2,1,0:T(8,128)(2,1)}), bf16[8,192,256]{2,1,0:T(8,128)(2,1)S(1)}, u32[]{:S(2)}, u32[]{:S(2)}) async-start(bf16[8,192,256]{2,1,0:T(8,128)(2,1)} %bitcast.8), calls=%async_computation | async-start | bytes 1572864 | tf_op jit(solution)/shard_map/all_to_all | solution.py:276
  24.2 2.8 %constant_dynamic-slice_fusion = (bf16[256,1280]{1,0:T(8,128)(2,1)S(1)}, bf16[256,1280]{1,0:T(8,128)(2,1)}, bf16[256,1280]{1,0:T(8,128)(2,1)S(1)}, bf16[256,1280]{1,0:T(8,128)(2,1)S(1)}) fusion(bf16[256,5120]{1,0:T(8,128)(2,1)} %param.18, s32[]{:T(128)S(6)} %select_n.57, s32[]{:T(128)S(6)} %select_n.55, s32[]{:T(128)S(6)} %select_n.53, s32[]{:T(128)S(6)} %select_n.51), kind=kLoop, calls=%fused_computation | loop fusion | bytes 5242896 | tf_op jit(solution)/shard_map/dynamic_slice | solution.py:296
  27.3 3.1 %collective-permute-start.4 = (bf16[256,1280]{1,0:T(8,128)(2,1)S(1)}, bf16[256,1280]{1,0:T(8,128)(2,1)S(1)}, u32[]{:S(2)}, u32[]{:S(2)}) collective-permute-start(bf16[256,1280]{1,0:T(8,128)(2,1)S(1)} %get-tuple-element.21), channel_id=1, source_target_pairs={{0,4},{1,5},{2,6},{3,7},{4,8},{5,9},{6,10},{7,11},{8,12},{9,13},{1... | collective-permute-start | bytes 1966088 | tf_op jit(solution)/shard_map/ppermute | solution.py:327
  30.4 3.4 %collective-permute-start.5 = (bf16[256,1280]{1,0:T(8,128)(2,1)S(1)}, bf16[256,1280]{1,0:T(8,128)(2,1)S(1)}, u32[]{:S(2)}, u32[]{:S(2)}) collective-permute-start(bf16[256,1280]{1,0:T(8,128)(2,1)S(1)} %get-tuple-element.23), channel_id=1, source_target_pairs={{0,12},{1,13},{2,14},{3,15},{4,0},{5,1},{6,2},{7,3},{8,4},{9,5},{1... | collective-permute-start | bytes 1966088 | tf_op jit(solution)/shard_map/ppermute | solution.py:327
  33.8 3.2 %collective-permute-start.1 = (bf16[384,512]{1,0:T(8,128)(2,1)S(1)}, bf16[384,512]{1,0:T(8,128)(2,1)}, u32[]{:S(2)}, u32[]{:S(2)}) collective-permute-start(bf16[384,512]{1,0:T(8,128)(2,1)S(1)} %join.1.refs_0_), channel_id=1, source_target_pairs={{0,16},{16,32},{32,48},{48,0},{64,80},{80,96},{96,112},{112,64},{1... | collective-permute-start | bytes 1179656 | tf_op jit(solution)/shard_map/ppermute | solution.py:279
  37.0 3.4 %collective-permute-start.2 = (bf16[384,512]{1,0:T(8,128)(2,1)S(1)}, bf16[384,512]{1,0:T(8,128)(2,1)}, u32[]{:S(2)}, u32[]{:S(2)}) collective-permute-start(bf16[384,512]{1,0:T(8,128)(2,1)S(1)} %join.1.refs_0_), channel_id=1, source_target_pairs={{0,48},{16,0},{32,16},{48,32},{64,112},{80,64},{96,80},{112,96},{1... | collective-permute-start | bytes 1179656 | tf_op jit(solution)/shard_map/ppermute | solution.py:279
  40.4 3.5 %collective-permute-start.3 = (bf16[384,512]{1,0:T(8,128)(2,1)S(1)}, bf16[384,512]{1,0:T(8,128)(2,1)}, u32[]{:S(2)}, u32[]{:S(2)}) collective-permute-start(bf16[384,512]{1,0:T(8,128)(2,1)S(1)} %join.1.refs_0_), channel_id=1, source_target_pairs={{0,32},{16,48},{32,0},{48,16},{64,96},{80,112},{96,64},{112,80},{1... | collective-permute-start | bytes 1179656 | tf_op jit(solution)/shard_map/ppermute | solution.py:279
  43.9 1.0 collective-permute-done.4.refs_1_
  44.9 1.6 collective-permute-done.5.refs_3_
  46.5 5.6 %all-to-all-done = bf16[8,192,256]{2,1,0:T(8,128)(2,1)S(1)} async-done(((bf16[8,192,256]{2,1,0:T(8,128)(2,1)}), bf16[8,192,256]{2,1,0:T(8,128)(2,1)S(1)}, u32[]{:S(2)}, u32[]{:S(2)}) %all-to-all-start) | async-done | bytes 786464 | tf_op jit(solution)/shard_map/all_to_all | solution.py:276
  52.1 3.0 %collective-permute-done.3.refs_3_ = bf16[384,512]{1,0:T(8,128)(2,1)} collective-permute-done((bf16[384,512]{1,0:T(8,128)(2,1)S(1)}, bf16[384,512]{1,0:T(8,128)(2,1)}, u32[]{:S(2)}, u32[]{:S(2)}) %collective-permute-start.3) | collective-permute-done | bytes 393248 | tf_op jit(solution)/shard_map/ppermute | solution.py:279
  55.1 9.2 %attend.1 = bf16[1664,256]{1,0:T(8,128)(2,1)} custom-call(bf16[384,512]{1,0:T(8,128)(2,1)} %copy-done.2, bf16[384,512]{1,0:T(8,128)(2,1)} %collective-permute-done.1.refs_1_, bf16[384,512]{1,0:T(8,128)(2,1)} %collective-permute-done.2.refs_2_, bf16[384,512]{1,0:T(8,128)(2,1)} %collective-permute-done.3.refs_3_, bf16[1536,256]{1,0:T(8,128)(2,1)} %bitcast.9), custom_call_target="tpu_custom_call" | custom-call | tf_op jit(solution)/shard_map/attend/pallas_call | solution.py:330
  64.2 13.2 %all-to-all-start.1 = ((bf16[8,208,256]{2,1,0:T(8,128)(2,1)}), bf16[8,208,256]{2,1,0:T(8,128)(2,1)}, u32[]{:S(2)}, u32[]{:S(2)}) async-start(bf16[8,208,256]{2,1,0:T(8,128)(2,1)} %bitcast.7), calls=%async_computation.1 | async-start | bytes 1703936 | tf_op jit(solution)/shard_map/all_to_all | solution.py:276
  77.4 4.6 %collective-permute-start.6 = (bf16[256,1280]{1,0:T(8,128)(2,1)}, bf16[256,1280]{1,0:T(8,128)(2,1)S(1)}, u32[]{:S(2)}, u32[]{:S(2)}) collective-permute-start(bf16[256,1280]{1,0:T(8,128)(2,1)} %get-tuple-element.25), channel_id=1, source_target_pairs={{0,8},{1,9},{2,10},{3,11},{4,12},{5,13},{6,14},{7,15},{8,0},{9,1},... | collective-permute-start | bytes 1966088 | tf_op jit(solution)/shard_map/ppermute | solution.py:344
  82.1 13.1 %collective-permute-done.6.refs_2_ = bf16[256,1280]{1,0:T(8,128)(2,1)S(1)} collective-permute-done((bf16[256,1280]{1,0:T(8,128)(2,1)}, bf16[256,1280]{1,0:T(8,128)(2,1)S(1)}, u32[]{:S(2)}, u32[]{:S(2)}) %collective-permute-start.6) | collective-permute-done | bytes 655392 | tf_op jit(solution)/shard_map/ppermute | solution.py:344
  95.1 1.1 copy-done.4
  96.2 1.1 copy-done.6
  97.3 0.9 stack.1.w_own
  98.2 4.9 %collective-permute-start.7 = (bf16[4,256,1280]{2,1,0:T(8,128)(2,1)S(1)}, bf16[4,256,1280]{2,1,0:T(8,128)(2,1)}, u32[]{:S(2)}, u32[]{:S(2)}) collective-permute-start(bf16[4,256,1280]{2,1,0:T(8,128)(2,1)S(1)} %stack.1.w_own), channel_id=1, source_target_pairs={{0,1},{1,0},{2,3},{3,2},{4,5},{5,4},{6,7},{7,6},{8,9},{9,8},{10,11... | collective-permute-start | bytes 7864328 | tf_op jit(solution)/shard_map/ppermute | solution.py:356
  103.1 4.2 %all-to-all-done.1 = bf16[8,208,256]{2,1,0:T(8,128)(2,1)} async-done(((bf16[8,208,256]{2,1,0:T(8,128)(2,1)}), bf16[8,208,256]{2,1,0:T(8,128)(2,1)}, u32[]{:S(2)}, u32[]{:S(2)}) %all-to-all-start.1) | async-done | bytes 852000 | tf_op jit(solution)/shard_map/all_to_all | solution.py:276
  107.3 3.7 %merge.1 = bf16[8,192,256]{2,1,0:T(8,128)(2,1)} custom-call(bf16[1664,256]{1,0:T(8,128)(2,1)} %bitcast.6.parts), custom_call_target="tpu_custom_call" | custom-call | tf_op jit(solution)/shard_map/merge/pallas_call | solution.py:358
  111.0 18.3 %all-to-all-start.2 = ((bf16[8,192,256]{2,1,0:T(8,128)(2,1)}), bf16[8,192,256]{2,1,0:T(8,128)(2,1)S(1)}, u32[]{:S(2)}, u32[]{:S(2)}) async-start(bf16[8,192,256]{2,1,0:T(8,128)(2,1)} %merge.1), calls=%async_computation.2 | async-start | bytes 1572864 | tf_op jit(solution)/shard_map/all_to_all | solution.py:276
  129.9 11.6 %all-to-all-done.2.acts = bf16[8,192,256]{2,1,0:T(8,128)(2,1)S(1)} async-done(((bf16[8,192,256]{2,1,0:T(8,128)(2,1)}), bf16[8,192,256]{2,1,0:T(8,128)(2,1)S(1)}, u32[]{:S(2)}, u32[]{:S(2)}) %all-to-all-start.2) | async-done | bytes 786464 | tf_op jit(solution)/shard_map/all_to_all | solution.py:276
  142.2 3.2 %project.1 = bf16[4,192,320]{2,1,0:T(8,128)(2,1)S(1)} custom-call(s32[2]{0:T(128)S(1)} %copy-done.10, bf16[8,192,256]{2,1,0:T(8,128)(2,1)S(1)} %all-to-all-done.2.acts, bf16[4,256,1280]{2,1,0:T(8,128)(2,1)S(1)} %stack.1.w_own, bf16[4,256,1280]{2,1,0:T(8,128)(2,1)} %collective-permute-done.7.w_other), custom_call_target="tpu_custom_call" | custom-call | tf_op jit(solution)/shard_map/project/pallas_call | solution.py:369
  145.5 0.8 copy-done
  146.3 8.4 %all-to-all-start.3 = ((bf16[4,192,320]{2,1,0:T(8,128)(2,1)}), bf16[4,192,320]{2,1,0:T(8,128)(2,1)S(1)}, u32[]{:S(2)}, u32[]{:S(2)}) async-start(bf16[4,192,320]{2,1,0:T(8,128)(2,1)} %copy-done), calls=%async_computation.3 | async-start | bytes 1179648 | tf_op jit(solution)/shard_map/all_to_all | solution.py:276
  155.4 28.3 %all-to-all-done.3.got = bf16[4,192,320]{2,1,0:T(8,128)(2,1)S(1)} async-done(((bf16[4,192,320]{2,1,0:T(8,128)(2,1)}), bf16[4,192,320]{2,1,0:T(8,128)(2,1)S(1)}, u32[]{:S(2)}, u32[]{:S(2)}) %all-to-all-start.3) | async-done | bytes 491552 | tf_op jit(solution)/shard_map/all_to_all | solution.py:276
  183.7 0.9 copy-done.8
  185.3 1.4 finish.1
  (27 shorter events, 3.6 us)
Async XLA Ops:
  3.3 7.6 %collective-permute-start = (bf16[192,512]{1,0:T(8,128)(2,1)}, bf16[192,512]{1,0:T(8,128)(2,1)S(1)}, u32[]{:S(2)}, u32[]{:S(2)}) collective-permute-start(bf16[192,512]{1,0:T(8,128)(2,1)} %get-tuple-element.16), channel_id=1, source_target_pairs={{0,64},{16,80},{32,96},{48,112},{64,0},{80,16},{96,32},{112,48},{1... | collective-permute-start | bytes 589832 | tf_op jit(solution)/shard_map/ppermute | solution.py:292
  10.9 41.2 %all-to-all-start = ((bf16[8,192,256]{2,1,0:T(8,128)(2,1)}), bf16[8,192,256]{2,1,0:T(8,128)(2,1)S(1)}, u32[]{:S(2)}, u32[]{:S(2)}) async-start(bf16[8,192,256]{2,1,0:T(8,128)(2,1)} %bitcast.8), calls=%async_computation | async-start | bytes 1572864 | tf_op jit(solution)/shard_map/all_to_all | solution.py:276
  24.2 2.8 %copy-start.1 = (bf16[384,512]{1,0:T(8,128)(2,1)S(1)}, bf16[384,512]{1,0:T(8,128)(2,1)}, u32[]{:S(2)}) copy-start(bf16[384,512]{1,0:T(8,128)(2,1)} %get-tuple-element.14.own_in) | copy-start | bytes 1179652
  27.3 27.8 %copy-start.2 = (bf16[384,512]{1,0:T(8,128)(2,1)}, bf16[384,512]{1,0:T(8,128)(2,1)S(1)}, u32[]{:S(2)}) copy-start(bf16[384,512]{1,0:T(8,128)(2,1)S(1)} %join.1.refs_0_) | copy-start | bytes 1179652
  27.3 17.6 %collective-permute-start.4 = (bf16[256,1280]{1,0:T(8,128)(2,1)S(1)}, bf16[256,1280]{1,0:T(8,128)(2,1)S(1)}, u32[]{:S(2)}, u32[]{:S(2)}) collective-permute-start(bf16[256,1280]{1,0:T(8,128)(2,1)S(1)} %get-tuple-element.21), channel_id=1, source_target_pairs={{0,4},{1,5},{2,6},{3,7},{4,8},{5,9},{6,10},{7,11},{8,12},{9,13},{1... | collective-permute-start | bytes 1966088 | tf_op jit(solution)/shard_map/ppermute | solution.py:327
  30.4 16.1 %collective-permute-start.5 = (bf16[256,1280]{1,0:T(8,128)(2,1)S(1)}, bf16[256,1280]{1,0:T(8,128)(2,1)S(1)}, u32[]{:S(2)}, u32[]{:S(2)}) collective-permute-start(bf16[256,1280]{1,0:T(8,128)(2,1)S(1)} %get-tuple-element.23), channel_id=1, source_target_pairs={{0,12},{1,13},{2,14},{3,15},{4,0},{5,1},{6,2},{7,3},{8,4},{9,5},{1... | collective-permute-start | bytes 1966088 | tf_op jit(solution)/shard_map/ppermute | solution.py:327
  33.8 18.3 %collective-permute-start.1 = (bf16[384,512]{1,0:T(8,128)(2,1)S(1)}, bf16[384,512]{1,0:T(8,128)(2,1)}, u32[]{:S(2)}, u32[]{:S(2)}) collective-permute-start(bf16[384,512]{1,0:T(8,128)(2,1)S(1)} %join.1.refs_0_), channel_id=1, source_target_pairs={{0,16},{16,32},{32,48},{48,0},{64,80},{80,96},{96,112},{112,64},{1... | collective-permute-start | bytes 1179656 | tf_op jit(solution)/shard_map/ppermute | solution.py:279
  37.0 15.1 %collective-permute-start.2 = (bf16[384,512]{1,0:T(8,128)(2,1)S(1)}, bf16[384,512]{1,0:T(8,128)(2,1)}, u32[]{:S(2)}, u32[]{:S(2)}) collective-permute-start(bf16[384,512]{1,0:T(8,128)(2,1)S(1)} %join.1.refs_0_), channel_id=1, source_target_pairs={{0,48},{16,0},{32,16},{48,32},{64,112},{80,64},{96,80},{112,96},{1... | collective-permute-start | bytes 1179656 | tf_op jit(solution)/shard_map/ppermute | solution.py:279
  40.4 14.7 %collective-permute-start.3 = (bf16[384,512]{1,0:T(8,128)(2,1)S(1)}, bf16[384,512]{1,0:T(8,128)(2,1)}, u32[]{:S(2)}, u32[]{:S(2)}) collective-permute-start(bf16[384,512]{1,0:T(8,128)(2,1)S(1)} %join.1.refs_0_), channel_id=1, source_target_pairs={{0,32},{16,48},{32,0},{48,16},{64,96},{80,112},{96,64},{112,80},{1... | collective-permute-start | bytes 1179656 | tf_op jit(solution)/shard_map/ppermute | solution.py:279
  44.9 37.2 %copy-start.3 = (bf16[256,1280]{1,0:T(8,128)(2,1)}, bf16[256,1280]{1,0:T(8,128)(2,1)S(1)}, u32[]{:S(2)}) copy-start(bf16[256,1280]{1,0:T(8,128)(2,1)S(1)} %collective-permute-done.4.refs_1_) | copy-start | bytes 1966084
  46.5 35.6 %copy-start.5 = (bf16[256,1280]{1,0:T(8,128)(2,1)}, bf16[256,1280]{1,0:T(8,128)(2,1)S(1)}, u32[]{:S(2)}) copy-start(bf16[256,1280]{1,0:T(8,128)(2,1)S(1)} %collective-permute-done.5.refs_3_) | copy-start | bytes 1966084
  52.1 3.0 %copy-start.11 = (bf16[8,192,256]{2,1,0:T(8,128)(2,1)}, bf16[8,192,256]{2,1,0:T(8,128)(2,1)S(1)}, u32[]{:S(2)}) copy-start(bf16[8,192,256]{2,1,0:T(8,128)(2,1)S(1)} %all-to-all-done) | copy-start | bytes 2359300
  64.2 43.0 %all-to-all-start.1 = ((bf16[8,208,256]{2,1,0:T(8,128)(2,1)}), bf16[8,208,256]{2,1,0:T(8,128)(2,1)}, u32[]{:S(2)}, u32[]{:S(2)}) async-start(bf16[8,208,256]{2,1,0:T(8,128)(2,1)} %bitcast.7), calls=%async_computation.1 | async-start | bytes 1703936 | tf_op jit(solution)/shard_map/all_to_all | solution.py:276
  77.4 17.7 %collective-permute-start.6 = (bf16[256,1280]{1,0:T(8,128)(2,1)}, bf16[256,1280]{1,0:T(8,128)(2,1)S(1)}, u32[]{:S(2)}, u32[]{:S(2)}) collective-permute-start(bf16[256,1280]{1,0:T(8,128)(2,1)} %get-tuple-element.25), channel_id=1, source_target_pairs={{0,8},{1,9},{2,10},{3,11},{4,12},{5,13},{6,14},{7,15},{8,0},{9,1},... | collective-permute-start | bytes 1966088 | tf_op jit(solution)/shard_map/ppermute | solution.py:344
  95.1 1.1 copy-start.4
  96.2 1.1 copy-start.6
  98.2 31.8 %collective-permute-start.7 = (bf16[4,256,1280]{2,1,0:T(8,128)(2,1)S(1)}, bf16[4,256,1280]{2,1,0:T(8,128)(2,1)}, u32[]{:S(2)}, u32[]{:S(2)}) collective-permute-start(bf16[4,256,1280]{2,1,0:T(8,128)(2,1)S(1)} %stack.1.w_own), channel_id=1, source_target_pairs={{0,1},{1,0},{2,3},{3,2},{4,5},{5,4},{6,7},{7,6},{8,9},{9,8},{10,11... | collective-permute-start | bytes 7864328 | tf_op jit(solution)/shard_map/ppermute | solution.py:356
  111.0 30.6 %all-to-all-start.2 = ((bf16[8,192,256]{2,1,0:T(8,128)(2,1)}), bf16[8,192,256]{2,1,0:T(8,128)(2,1)S(1)}, u32[]{:S(2)}, u32[]{:S(2)}) async-start(bf16[8,192,256]{2,1,0:T(8,128)(2,1)} %merge.1), calls=%async_computation.2 | async-start | bytes 1572864 | tf_op jit(solution)/shard_map/all_to_all | solution.py:276
  129.9 53.8 %copy-start.7 = (bf16[192,320]{1,0:T(8,128)(2,1)S(1)}, bf16[192,320]{1,0:T(8,128)(2,1)}, u32[]{:S(2)}) copy-start(bf16[192,320]{1,0:T(8,128)(2,1)} %tokens.1) | copy-start | bytes 368644
  141.6 0.7 copy-start.10
  145.5 0.8 copy-start
  146.3 37.4 %all-to-all-start.3 = ((bf16[4,192,320]{2,1,0:T(8,128)(2,1)}), bf16[4,192,320]{2,1,0:T(8,128)(2,1)S(1)}, u32[]{:S(2)}, u32[]{:S(2)}) async-start(bf16[4,192,320]{2,1,0:T(8,128)(2,1)} %copy-done), calls=%async_computation.3 | async-start | bytes 1179648 | tf_op jit(solution)/shard_map/all_to_all | solution.py:276
  183.7 0.9 copy-start.8
  184.6 0.7 copy-start.9

commit v4 on v0

v4 whole, which is shorter than its diff:
```python
import functools
import math

import jax
import jax.numpy as jnp
from jax import lax
from jax.experimental import pallas as pl
from jax.experimental.pallas import tpu as pltpu
from jax.sharding import Mesh
from jax.sharding import PartitionSpec as P

HD = 128
FRAME = 32
NZ, NY, NX = 8, 4, 4
TM, MP = ("z", "z0", "y"), ("x", "half", "core")
FACTOR = 1.0 / math.sqrt(HD)
LOG2E = math.log2(math.e)
STAT_ROWS = 16
BF = jnp.bfloat16
F32 = jnp.float32
def params(mib):
    return pltpu.CompilerParams(vmem_limit_bytes=mib * 1024 * 1024)


SMEM_SPEC = pl.BlockSpec(memory_space=pltpu.SMEM)
VMEM_SPEC = pl.BlockSpec(memory_space=pltpu.VMEM)
HBM_SPEC = pl.BlockSpec(memory_space=pltpu.HBM)


def over_z(k):
    return [(z * NY + y, (z ^ k) * NY + y) for z in range(NZ) for y in range(NY)]


def over_y(k):
    return [(z * NY + y, z * NY + (y + k) % NY) for z in range(NZ) for y in range(NY)]


def flip(bits):
    return [(i, i ^ bits) for i in range(4 * NX)]


def load(sources, held, sems):
    copies = [pltpu.make_async_copy(a, b, sems.at[i]) for i, (a, b) in enumerate(zip(sources, held))]
    for copy in copies:
        copy.start()
    for copy in copies:
        copy.wait()


def run_all(copies):
    for copy in copies:
        copy.start()
    for copy in copies:
        copy.wait()


def masked_rows(flags, f, ref):
    block = ref[pl.ds(f * FRAME, FRAME), :]
    return jnp.where(flags[f * FRAME] > 0, block, jnp.zeros_like(block))


def pack_kernel(odd, flags, *refs):
    sources, (qd_own, kv_own, other_head), held = refs[:6], refs[6:9], refs[9:15]
    qd, kv, other, sems = refs[15:]
    load(sources, held, sems)
    q, dq, k, v, dk, dv = held
    is_odd = odd[0] > 0
    rows_all = other.shape[0]
    for f in range(rows_all // FRAME):
        rows = pl.ds(f * FRAME, FRAME)
        blocks = (
            masked_rows(flags, f, dq),
            q[rows, :],
            k[rows, :],
            masked_rows(flags, f, dk),
            v[rows, :],
            masked_rows(flags, f, dv),
        )
        for i, block in enumerate(blocks):
            first, second = block[:, :HD], block[:, HD:]
            own = jnp.where(is_odd, second, first)
            other[rows, i * HD : (i + 1) * HD] = jnp.where(is_odd, first, second)
            if i < 2:
                qd[rows, i * HD : (i + 1) * HD] = own
            else:
                kv[rows, (i - 2) * HD : (i - 1) * HD] = own
    top = pl.ds(0, rows_all)
    run_all(
        [
            pltpu.make_async_copy(other, other_head, sems.at[0]),
            pltpu.make_async_copy(qd, qd_own.at[top], sems.at[1]),
            pltpu.make_async_copy(kv, kv_own.at[top], sems.at[2]),
        ]
    )


def join_kernel(got, qd_in, kv_in, qd, kv, held, sems):
    del qd_in, kv_in
    rows = got.shape[0]
    below = pl.ds(rows, rows)
    run_all([pltpu.make_async_copy(got, held, sems.at[0])])
    run_all(
        [
            pltpu.make_async_copy(held.at[:, pl.ds(0, 2 * HD)], qd.at[below], sems.at[0]),
            pltpu.make_async_copy(held.at[:, pl.ds(2 * HD, 4 * HD)], kv.at[below], sems.at[1]),
        ]
    )


def cut_kernel(w_in, w_out, held, sems):
    group = w_out.shape[2]
    run_all([pltpu.make_async_copy(w_in, held, sems.at[0])])
    run_all(
        [
            pltpu.make_async_copy(held.at[:, pl.ds(i * group, group)], w_out.at[i], sems.at[i])
            for i in range(NX)
        ]
    )


def in_three(value):
    high = value.astype(BF).astype(F32)
    middle = (value - high).astype(BF).astype(F32)
    low = (value - high - middle).astype(BF).astype(F32)
    return high, middle, low


def attend_kernel(*refs):
    kv_in, qd_in, out = refs[:8], refs[8], refs[9]
    kv, qd, held, sems = refs[10:]
    rows = kv_in[0].shape[0]
    half = rows // 2
    run_all(
        [
            pltpu.make_async_copy(kv_in[i], kv.at[pl.ds(i * rows, rows)], sems.at[i])
            for i in range(8)
        ]
        + [pltpu.make_async_copy(qd_in, qd, sems.at[8])]
    )
    contract = (((1,), (1,)), ((), ()))
    both = qd[...]
    scores = lax.dot_general(both[:, HD:], kv[:, :HD], contract, preferred_element_type=F32)
    slopes = lax.dot_general(both, kv[:, : 2 * HD], contract, preferred_element_type=F32)
    peak = jnp.max(scores, axis=1, keepdims=True) * (FACTOR * LOG2E)
    weights = jnp.exp2(scores * (FACTOR * LOG2E) - peak)
    total = jnp.sum(weights, axis=1, keepdims=True)
    product = weights * slopes
    slope = jnp.sum(product, axis=1, keepdims=True)
    weighted = jnp.dot(weights.astype(BF), kv[:, 2 * HD :], preferred_element_type=F32)
    tangent = jnp.dot(product.astype(BF), kv[:, 2 * HD : 3 * HD], preferred_element_type=F32)
    inverse = 1.0 / total
    mean = slope * (inverse * FACTOR)
    primal = weighted[:, :HD] * inverse
    tangent = (tangent * FACTOR + weighted[:, HD:]) * inverse - mean * primal
    lanes = lax.broadcasted_iota(jnp.int32, (rows, HD), 1)
    stats = jnp.zeros((rows, HD), F32)
    for i, part in enumerate(in_three(peak + jnp.log2(total)) + in_three(mean)):
        stats = jnp.where(lanes == i, part, stats)
    for p in range(2):
        mine = slice(p * half, (p + 1) * half)
        at = p * (half + STAT_ROWS)
        held[at : at + half, :HD] = primal[mine].astype(BF)
        held[at : at + half, HD:] = tangent[mine].astype(BF)
        tile = jnp.concatenate([stats[mine], jnp.zeros((2 * HD - half, HD), F32)], axis=0)
        held[at + half : at + half + STAT_ROWS, :] = tile.T[:STAT_ROWS].astype(BF)
    run_all([pltpu.make_async_copy(held, out, sems.at[0])])


def merge_kernel(odd, one, two, out, merged, sems):
    rows = merged.shape[2]
    parts = (one, two)
    is_odd = odd[0] > 0
    found = []
    for p in range(2):
        at = p * (rows + STAT_ROWS)
        tiles = [part[at + rows : at + rows + STAT_ROWS, :].astype(F32) for part in parts]
        stats = jnp.concatenate(tiles * 4, axis=0).T[:rows]

        def value(i, first):
            lane = i * STAT_ROWS + first
            return sum(stats[:, lane + j : lane + j + 1] for j in range(3))

        sizes = [value(i, 0) for i in range(2)]
        means = [value(i, 3) for i in range(2)]
        peak = jnp.maximum(*sizes)
        sizes = [jnp.exp2(size - peak) for size in sizes]
        inverse = 1.0 / sum(sizes)
        sizes = [size * inverse for size in sizes]
        mean = sum(size * m for size, m in zip(sizes, means))
        primal = jnp.zeros((rows, HD), F32)
        tangent = jnp.zeros((rows, HD), F32)
        for part, size, m in zip(parts, sizes, means):
            a = part[at : at + rows, :HD].astype(F32)
            primal += size * a
            tangent += size * part[at : at + rows, HD:].astype(F32) + (size * (m - mean)) * a
        found.append((primal.astype(BF), tangent.astype(BF)))
    for kind in range(2):
        own, other = found[0][kind], found[1][kind]
        merged[0, kind] = jnp.where(is_odd, other, own)
        merged[1, kind] = jnp.where(is_odd, own, other)
    copies = []
    for parity in range(2):
        for i in range(NX):
            j = parity * NX + i
            copies.append(
                pltpu.make_async_copy(merged.at[parity], out.at[pl.ds(2 * j, 2)], sems.at[j])
            )
    run_all(copies)


def project_kernel(place, acts, w_own, w_other, mine, others):
    width = mine.shape[1]
    c = place[1]
    for half in range(2):

        @pl.when(place[0] == half)
        def _():
            columns = slice(2 * half * width, 2 * (half + 1) * width)
            total = jnp.zeros((mine.shape[0], 2 * width), F32)
            for k in range(NX):
                for w, i in ((w_own, 2 * k + c), (w_other, 2 * k + 1 - c)):
                    heads = jnp.concatenate([acts[i], acts[2 * NX + i]], axis=1)
                    total += jnp.dot(heads, w[k, :, columns], preferred_element_type=F32)
            first, second = total[:, :width], total[:, width:]
            mine[...] = jnp.where(c > 0, second, first).astype(mine.dtype)
            others[...] = jnp.where(c > 0, first, second).astype(others.dtype)


def finish_kernel(
    core, flags, mine, z_got, core_got, both_got, gate, tokens, d_tokens, result, d_result
):
    is_second = core[0] > 0
    scale = gate[...]
    for f in range(tokens.shape[0] // FRAME):
        rows = pl.ds(f * FRAME, FRAME)
        live = flags[f * FRAME] > 0
        kept = mine[rows, :] + z_got[rows, :].astype(F32)
        other = core_got[rows, :].astype(F32) + both_got[rows, :].astype(F32)
        primal = jnp.where(is_second, other, kept)
        tangent = jnp.where(is_second, kept, other)
        base = tokens[rows, :].astype(F32)
        d_base = d_tokens[rows, :].astype(F32)
        d_base = jnp.where(live, d_base, jnp.zeros_like(d_base))
        result[rows, :] = (base + scale * primal).astype(BF)
        d_result[rows, :] = (d_base + scale * tangent).astype(BF)


def per_device(
    queries,
    d_queries,
    key_rows,
    value_rows,
    d_key_rows,
    d_value_rows,
    live_flags,
    out_weight,
    gate_scale,
    tokens,
    d_tokens,
):
    rows, width = queries.shape
    columns = tokens.shape[1]
    t, m = lax.axis_index(TM), lax.axis_index(MP)
    odd = (t // NY % 2).astype(jnp.int32).reshape(1)
    core = (m % 2).astype(jnp.int32).reshape(1)
    group = 4 * columns

    def shape(*dims):
        return jax.ShapeDtypeStruct(dims, BF)

    def after(a, b):
        return lax.optimization_barrier((a, b))[0]

    def exchange(a, axes):
        return lax.all_to_all(a, axes, 0, 0, tiled=True)

    def y(a, k):
        return lax.ppermute(a, TM, over_y(k))

    def z(a, k):
        return lax.ppermute(a, TM, over_z(k))

    qd, kv, other_head = pl.pallas_call(
        pack_kernel,
        out_shape=[shape(2 * rows, 2 * HD), shape(2 * rows, 4 * HD), shape(rows, 6 * HD)],
        in_specs=[SMEM_SPEC] * 2 + [HBM_SPEC] * 6,
        out_specs=[HBM_SPEC] * 3,
        scratch_shapes=[pltpu.VMEM((rows, width), BF)] * 6
        + [
            pltpu.VMEM((rows, 2 * HD), BF),
            pltpu.VMEM((rows, 4 * HD), BF),
            pltpu.VMEM((rows, 6 * HD), BF),
            pltpu.SemaphoreType.DMA((6,)),
        ],
        compiler_params=params(60),
        name="pack",
    )(odd, live_flags, queries, d_queries, key_rows, value_rows, d_key_rows, d_value_rows)
    weights = pl.pallas_call(
        cut_kernel,
        out_shape=shape(NX, width, group),
        in_specs=[HBM_SPEC],
        out_specs=HBM_SPEC,
        scratch_shapes=[pltpu.VMEM(out_weight.shape, BF), pltpu.SemaphoreType.DMA((NX,))],
        compiler_params=params(60),
        name="cut",
    )(after(out_weight, kv))
    got = z(other_head, 1)
    got = after(got, weights)
    qd, kv = pl.pallas_call(
        join_kernel,
        out_shape=[shape(2 * rows, 2 * HD), shape(2 * rows, 4 * HD)],
        in_specs=[HBM_SPEC] * 3,
        out_specs=[HBM_SPEC] * 2,
        scratch_shapes=[pltpu.VMEM((rows, 6 * HD), BF), pltpu.SemaphoreType.DMA((2,))],
        input_output_aliases={1: 0, 2: 1},
        compiler_params=params(60),
        name="join",
    )(got, qd, kv)
    kv_far = z(kv, 2)
    qd_far = z(qd, 4)
    kv = [kv] + [y(kv, k) for k in (1, 3, 2)] + [kv_far] + [y(kv_far, k) for k in (1, 3, 2)]

    w_own = exchange(after(weights, got), "x")
    qd_far = after(qd_far, w_own)

    def attend(piece):
        part = shape(2 * (rows + STAT_ROWS), 2 * HD)
        return pl.pallas_call(
            attend_kernel,
            out_shape=part,
            in_specs=[HBM_SPEC] * 9,
            out_specs=HBM_SPEC,
            scratch_shapes=[
                pltpu.VMEM((16 * rows, 4 * HD), BF),
                pltpu.VMEM((2 * rows, 2 * HD), BF),
                pltpu.VMEM(part.shape, BF),
                pltpu.SemaphoreType.DMA((9,)),
            ],
            compiler_params=params(60),
            name="attend",
        )(*kv, piece)

    far = attend(qd_far)
    near = attend(after(qd, far))
    returned = z(far, 4)

    w_other = lax.ppermute(after(w_own, far), MP, flip(1))

    acts = pl.pallas_call(
        merge_kernel,
        out_shape=shape(4 * NX, rows, HD),
        in_specs=[SMEM_SPEC] + [VMEM_SPEC] * 2,
        out_specs=HBM_SPEC,
        scratch_shapes=[pltpu.VMEM((2, 2, rows, HD), BF), pltpu.SemaphoreType.DMA((2 * NX,))],
        compiler_params=params(60),
        name="merge",
    )(odd, near, returned)
    acts = exchange(acts, ("z0", "x", "core"))

    half = (m // 2 % 2).astype(jnp.int32).reshape(1)

    def project(which, dtype):
        return pl.pallas_call(
            project_kernel,
            out_shape=[jax.ShapeDtypeStruct((rows, columns), dtype), shape(rows, columns)],
            in_specs=[SMEM_SPEC] + [VMEM_SPEC] * 3,
            out_specs=[VMEM_SPEC] * 2,
            compiler_params=params(24),
            name="project",
        )(jnp.concatenate([which, core]), acts, w_own, w_other)

    z_send, both_send = project(1 - half, BF)
    mine, core_send = project(half, F32)
    z_got = lax.ppermute(z_send, MP, flip(2))
    both_got = lax.ppermute(both_send, MP, flip(3))
    core_got = lax.ppermute(core_send, MP, flip(1))

    result, d_result = pl.pallas_call(
        finish_kernel,
        out_shape=[shape(rows, columns)] * 2,
        in_specs=[SMEM_SPEC] * 2 + [VMEM_SPEC] * 7,
        out_specs=[VMEM_SPEC] * 2,
        compiler_params=params(8),
        name="finish",
    )(
        core,
        live_flags,
        mine,
        z_got,
        core_got,
        both_got,
        gate_scale.reshape(1, columns),
        tokens,
        d_tokens,
    )
    return (result, d_result)


def solution(mesh):
    parts = mesh.devices.reshape(NZ // 2, 2, NY, NX, 2, 2)
    placed = (
        P(TM, MP),
        P(TM, MP),
        P(TM, MP),
        P(TM, MP),
        P(TM, MP),
        P(TM, MP),
        P(TM),
        P(MP, None),
        P(MP),
        P(TM, MP),
        P(TM, MP),
    )
    return jax.shard_map(
        per_device,
        mesh=Mesh(parts, TM + MP),
        in_specs=placed,
        out_specs=(P(TM, MP), P(TM, MP)),
        check_vma=False,
    )
```

time: 489 us -> 175 us (0.36)
  waiting for transfers between devices: 396 us -> 61.5 us
  starting transfers between devices: 0.08 us -> 80.3 us
  local copies, waits for them, and re-layouts: 38.8 us -> 1.46 us
  matrix products: 30.7 us -> 0 us
  Pallas kernels: 0 us -> 30 us
  between operations: 14.2 us -> 1.02 us
  other arithmetic: 8.09 us -> 0.15 us
    all_gather x1 -> x0, waiting for transfers between devices: 233 us -> none  [side_by_side(): lax.all_gather(both, axis, axis=dim, tiled=True)]
    unnamed x3 -> x0, waiting for transfers between devices: 163 us -> none
    ppermute x0 -> x14, starting transfers between devices: none -> 68.4 us  [the longest x6 26 us: y(): return lax.ppermute(a, TM, over_y(k))]
    ppermute x0 -> x14, waiting for transfers between devices: none -> 55.5 us  [the longest x1 22 us: per_device(): both_got = lax.ppermute(both_send, MP, flip(3))]
    dot_general x8 -> x0, matrix products: 30.7 us -> none  [the longest x1 10.6 us: attend(): jnp.einsum('qhd,khd->qhk', queries_h, dkeys_h, preferred_element_type=jnp...]
    pallas_call x0 -> x9, Pallas kernels: none -> 30 us  [the longest x2 12.2 us: attend(): pl.pallas_call(attend_kernel, out_shape=part, in_specs=[HBM_SPEC] * 9, ou...]
    unnamed x23 -> x18, local copies, waits for them, and re-layouts: 28.2 us -> 1.46 us
    all_to_all x0 -> x2, starting transfers between devices: none -> 12 us  [exchange(): return lax.all_to_all(a, axes, 0, 0, tiled=True)]
  transfers between devices with their start and end apart: 2 -> 16, of which waited for: 2 -> 9; matrix products, arithmetic and copies ran while one was open for 0% -> 0% of each run, Pallas kernels for 0% -> 8%
where the time goes in v4:
time: 175 us
  starting transfers between devices  80.3 us (46%)
  waiting for transfers between devices  61.5 us (35%)
  Pallas kernels  30 us (17%)
    ppermute x6, starting transfers between devices, y(): return lax.ppermute(a, TM, over_y(k))  26 us
    ppermute x4, starting transfers between devices, z(): return lax.ppermute(a, TM, over_z(k))  23.1 us
    ppermute x1, waiting for transfers between devices, per_device(): both_got = lax.ppermute(both_send, MP, flip(3))  22 us
    ppermute x4, waiting for transfers between devices, z(): return lax.ppermute(a, TM, over_z(k))  17.1 us
    pallas_call x2, Pallas kernels, attend(): pl.pallas_call(attend_kernel, out_shape=part, in_specs=[HBM_SPEC] * 9, ou...  12.2 us
    ppermute x1, starting transfers between devices, per_device(): z_got = lax.ppermute(z_send, MP, flip(2))  12.2 us
    all_to_all x2, starting transfers between devices, exchange(): return lax.all_to_all(a, axes, 0, 0, tiled=True)  12 us
    ppermute x6, waiting for transfers between devices, y(): return lax.ppermute(a, TM, over_y(k))  11.7 us
  transfers between devices with their start and end apart: 16, of which 9 were waited for; matrix products, arithmetic and copies ran while one was open for 0% of the time, Pallas kernels for 8%

profile of v4, /device:TPU:1, one launch (start us, length us, event | category | flops | bytes accessed | tf_op | source)
XLA Modules:
  0.0 174.5 jit_solution(13653035698224347698)
XLA Ops:
  0.7 2.8 %pack.1 = (bf16[384,256]{1,0:T(8,128)(2,1)}, bf16[384,512]{1,0:T(8,128)(2,1)}, bf16[192,768]{1,0:T(8,128)(2,1)}) custom-call(s32[1]{0:T(128)} %bitcast.2.odd, s32[192]{0:T(256)} %flags.3, bf16[192,256]{1,0:T(8,128)(2,1)} %refs_0_.1, bf16[192,256]{1,0:T(8,128)(2,1)} %refs_1_.1, bf16[192,256]{1,0:T(8,128)(2,1)} %refs_2_.1, bf16[192,256]{1,0:T(8,128)(2,1)} %refs_3_.1, ...), custom_call_target="tpu_custom_call" | custom-call | tf_op jit(solution)/shard_map/pack/pallas_call | solution.py:283
  3.5 4.4 %collective-permute-start = (bf16[192,768]{1,0:T(8,128)(2,1)}, bf16[192,768]{1,0:T(8,128)(2,1)S(1)}, u32[]{:S(2)}, u32[]{:S(2)}) collective-permute-start(bf16[192,768]{1,0:T(8,128)(2,1)} %get-tuple-element.17), channel_id=1, source_target_pairs={{0,64},{16,80},{32,96},{48,112},{64,0},{80,16},{96,32},{112,48},{1... | collective-permute-start | bytes 884744 | tf_op jit(solution)/shard_map/ppermute | solution.py:281
  7.9 3.3 %cut.1 = bf16[4,256,1280]{2,1,0:T(8,128)(2,1)} custom-call(bf16[256,5120]{1,0:T(8,128)(2,1)} %w_in), custom_call_target="tpu_custom_call" | custom-call | tf_op jit(solution)/shard_map/cut/pallas_call | solution.py:298
  12.9 6.5 %all-to-all-start = ((bf16[4,256,1280]{2,1,0:T(8,128)(2,1)}), bf16[4,256,1280]{2,1,0:T(8,128)(2,1)S(1)}, u32[]{:S(2)}, u32[]{:S(2)}) async-start(bf16[4,256,1280]{2,1,0:T(8,128)(2,1)} %cut.1), calls=%async_computation | async-start | bytes 5242880 | tf_op jit(solution)/shard_map/all_to_all | solution.py:275
  19.5 1.7 join.1
  21.2 4.9 %collective-permute-start.4 = (bf16[384,512]{1,0:T(8,128)(2,1)}, bf16[384,512]{1,0:T(8,128)(2,1)S(1)}, u32[]{:S(2)}, u32[]{:S(2)}) collective-permute-start(bf16[384,512]{1,0:T(8,128)(2,1)} %get-tuple-element.22.refs_0_), channel_id=1, source_target_pairs={{0,128},{16,144},{32,160},{48,176},{64,192},{80,208},{96,224},{112... | collective-permute-start | bytes 1179656 | tf_op jit(solution)/shard_map/ppermute | solution.py:281
  26.1 4.8 %collective-permute-start.3 = (bf16[384,512]{1,0:T(8,128)(2,1)}, bf16[384,512]{1,0:T(8,128)(2,1)S(1)}, u32[]{:S(2)}, u32[]{:S(2)}) collective-permute-start(bf16[384,512]{1,0:T(8,128)(2,1)} %get-tuple-element.22.refs_0_), channel_id=1, source_target_pairs={{0,32},{16,48},{32,0},{48,16},{64,96},{80,112},{96,64},{112,80},{1... | collective-permute-start | bytes 1179656 | tf_op jit(solution)/shard_map/ppermute | solution.py:278
  30.9 8.8 %collective-permute-start.8 = (bf16[384,256]{1,0:T(8,128)(2,1)}, bf16[384,256]{1,0:T(8,128)(2,1)S(1)}, u32[]{:S(2)}, u32[]{:S(2)}) collective-permute-start(bf16[384,256]{1,0:T(8,128)(2,1)} %get-tuple-element.26.refs_8_), channel_id=1, source_target_pairs={{0,256},{16,272},{32,288},{48,304},{64,320},{80,336},{96,352},{112... | collective-permute-start | bytes 589832 | tf_op jit(solution)/shard_map/ppermute | solution.py:281
  39.7 2.7 %collective-permute-start.2 = (bf16[384,512]{1,0:T(8,128)(2,1)}, bf16[384,512]{1,0:T(8,128)(2,1)}, u32[]{:S(2)}, u32[]{:S(2)}) collective-permute-start(bf16[384,512]{1,0:T(8,128)(2,1)} %get-tuple-element.22.refs_0_), channel_id=1, source_target_pairs={{0,48},{16,0},{32,16},{48,32},{64,112},{80,64},{96,80},{112,96},{1... | collective-permute-start | bytes 1179656 | tf_op jit(solution)/shard_map/ppermute | solution.py:278
  42.4 2.6 %collective-permute-start.1 = (bf16[384,512]{1,0:T(8,128)(2,1)}, bf16[384,512]{1,0:T(8,128)(2,1)}, u32[]{:S(2)}, u32[]{:S(2)}) collective-permute-start(bf16[384,512]{1,0:T(8,128)(2,1)} %get-tuple-element.22.refs_0_), channel_id=1, source_target_pairs={{0,16},{16,32},{32,48},{48,0},{64,80},{80,96},{96,112},{112,64},{1... | collective-permute-start | bytes 1179656 | tf_op jit(solution)/shard_map/ppermute | solution.py:278
  45.8 10.6 %collective-permute-start.7 = (bf16[384,512]{1,0:T(8,128)(2,1)S(1)}, bf16[384,512]{1,0:T(8,128)(2,1)}, u32[]{:S(2)}, u32[]{:S(2)}) collective-permute-start(bf16[384,512]{1,0:T(8,128)(2,1)S(1)} %collective-permute-done.4.refs_4_), channel_id=1, source_target_pairs={{0,32},{16,48},{32,0},{48,16},{64,96},{80,112},{96,64},{112,80},{1... | collective-permute-start | bytes 1179656 | tf_op jit(solution)/shard_map/ppermute | solution.py:278
  56.4 1.9 %collective-permute-start.6 = (bf16[384,512]{1,0:T(8,128)(2,1)S(1)}, bf16[384,512]{1,0:T(8,128)(2,1)}, u32[]{:S(2)}, u32[]{:S(2)}) collective-permute-start(bf16[384,512]{1,0:T(8,128)(2,1)S(1)} %collective-permute-done.4.refs_4_), channel_id=1, source_target_pairs={{0,48},{16,0},{32,16},{48,32},{64,112},{80,64},{96,80},{112,96},{1... | collective-permute-start | bytes 1179656 | tf_op jit(solution)/shard_map/ppermute | solution.py:278
  58.4 3.4 %collective-permute-start.5 = (bf16[384,512]{1,0:T(8,128)(2,1)S(1)}, bf16[384,512]{1,0:T(8,128)(2,1)}, u32[]{:S(2)}, u32[]{:S(2)}) collective-permute-start(bf16[384,512]{1,0:T(8,128)(2,1)S(1)} %collective-permute-done.4.refs_4_), channel_id=1, source_target_pairs={{0,16},{16,32},{32,48},{48,0},{64,80},{80,96},{96,112},{112,64},{1... | collective-permute-start | bytes 1179656 | tf_op jit(solution)/shard_map/ppermute | solution.py:278
  61.8 2.6 %collective-permute-done.7.refs_7_ = bf16[384,512]{1,0:T(8,128)(2,1)} collective-permute-done((bf16[384,512]{1,0:T(8,128)(2,1)S(1)}, bf16[384,512]{1,0:T(8,128)(2,1)}, u32[]{:S(2)}, u32[]{:S(2)}) %collective-permute-start.7) | collective-permute-done | bytes 393248 | tf_op jit(solution)/shard_map/ppermute | solution.py:278
  64.4 6.2 %collective-permute-done.6.refs_6_ = bf16[384,512]{1,0:T(8,128)(2,1)} collective-permute-done((bf16[384,512]{1,0:T(8,128)(2,1)S(1)}, bf16[384,512]{1,0:T(8,128)(2,1)}, u32[]{:S(2)}, u32[]{:S(2)}) %collective-permute-start.6) | collective-permute-done | bytes 393248 | tf_op jit(solution)/shard_map/ppermute | solution.py:278
  70.6 2.9 %collective-permute-done.5.refs_5_ = bf16[384,512]{1,0:T(8,128)(2,1)} collective-permute-done((bf16[384,512]{1,0:T(8,128)(2,1)S(1)}, bf16[384,512]{1,0:T(8,128)(2,1)}, u32[]{:S(2)}, u32[]{:S(2)}) %collective-permute-start.5) | collective-permute-done | bytes 393248 | tf_op jit(solution)/shard_map/ppermute | solution.py:278
  73.4 6.1 %attend.2 = bf16[416,256]{1,0:T(8,128)(2,1)} custom-call(bf16[384,512]{1,0:T(8,128)(2,1)} %get-tuple-element.22.refs_0_, bf16[384,512]{1,0:T(8,128)(2,1)} %collective-permute-done.1.refs_1_, bf16[384,512]{1,0:T(8,128)(2,1)} %collective-permute-done.2.refs_2_, bf16[384,512]{1,0:T(8,128)(2,1)} %copy-done.4, bf16[384,512]{1,0:T(8,128)(2,1)} %copy-done.3, ...), custom_call_target="tpu_custom_call" | custom-call | tf_op jit(solution)/shard_map/attend/pallas_call | solution.py:328
  79.6 5.0 %collective-permute-start.9 = (bf16[416,256]{1,0:T(8,128)(2,1)}, bf16[416,256]{1,0:T(8,128)(2,1)S(1)}, u32[]{:S(2)}, u32[]{:S(2)}) collective-permute-start(bf16[416,256]{1,0:T(8,128)(2,1)} %attend.2), channel_id=1, source_target_pairs={{0,256},{16,272},{32,288},{48,304},{64,320},{80,336},{96,352},{112... | collective-permute-start | bytes 638984 | tf_op jit(solution)/shard_map/ppermute | solution.py:281
  84.5 6.1 %attend.3.one = bf16[416,256]{1,0:T(8,128)(2,1)} custom-call(bf16[384,512]{1,0:T(8,128)(2,1)} %get-tuple-element.22.refs_0_, bf16[384,512]{1,0:T(8,128)(2,1)} %collective-permute-done.1.refs_1_, bf16[384,512]{1,0:T(8,128)(2,1)} %collective-permute-done.2.refs_2_, bf16[384,512]{1,0:T(8,128)(2,1)} %copy-done.4, bf16[384,512]{1,0:T(8,128)(2,1)} %copy-done.3, ...), custom_call_target="tpu_custom_call" | custom-call | tf_op jit(solution)/shard_map/attend/pallas_call | solution.py:328
  90.7 15.4 %collective-permute-done.9.two = bf16[416,256]{1,0:T(8,128)(2,1)S(1)} collective-permute-done((bf16[416,256]{1,0:T(8,128)(2,1)}, bf16[416,256]{1,0:T(8,128)(2,1)S(1)}, u32[]{:S(2)}, u32[]{:S(2)}) %collective-permute-start.9) | collective-permute-done | bytes 213024 | tf_op jit(solution)/shard_map/ppermute | solution.py:281
  106.7 3.1 %merge.1 = bf16[16,192,128]{2,1,0:T(8,128)(2,1)} custom-call(s32[1]{0:T(128)} %bitcast.2.odd, bf16[416,256]{1,0:T(8,128)(2,1)} %attend.3.one, bf16[416,256]{1,0:T(8,128)(2,1)} %copy-done.6), custom_call_target="tpu_custom_call" | custom-call | tf_op jit(solution)/shard_map/merge/pallas_call | solution.py:349
  109.9 5.4 %all-to-all-start.1 = ((bf16[16,192,128]{2,1,0:T(8,128)(2,1)}), bf16[16,192,128]{2,1,0:T(8,128)(2,1)S(1)}, u32[]{:S(2)}, u32[]{:S(2)}) async-start(bf16[16,192,128]{2,1,0:T(8,128)(2,1)} %merge.1), calls=%async_computation.1 | async-start | bytes 1572864 | tf_op jit(solution)/shard_map/all_to_all | solution.py:275
  115.3 2.0 %collective-permute-start.10 = (bf16[4,256,1280]{2,1,0:T(8,128)(2,1)S(1)}, bf16[4,256,1280]{2,1,0:T(8,128)(2,1)}, u32[]{:S(2)}, u32[]{:S(2)}) collective-permute-start(bf16[4,256,1280]{2,1,0:T(8,128)(2,1)S(1)} %all-to-all-done.w_own), channel_id=1, source_target_pairs={{0,1},{1,0},{2,3},{3,2},{4,5},{5,4},{6,7},{7,6},{8,9},{9,8},{10,11... | collective-permute-start | bytes 7864328 | tf_op jit(solution)/shard_map/ppermute | solution.py:347
  117.5 4.7 %collective-permute-done.10.w_other = bf16[4,256,1280]{2,1,0:T(8,128)(2,1)} collective-permute-done((bf16[4,256,1280]{2,1,0:T(8,128)(2,1)S(1)}, bf16[4,256,1280]{2,1,0:T(8,128)(2,1)}, u32[]{:S(2)}, u32[]{:S(2)}) %collective-permute-start.10) | collective-permute-done | bytes 2621472 | tf_op jit(solution)/shard_map/ppermute | solution.py:347
  122.2 6.1 %all-to-all-done.1.acts = bf16[16,192,128]{2,1,0:T(8,128)(2,1)S(1)} async-done(((bf16[16,192,128]{2,1,0:T(8,128)(2,1)}), bf16[16,192,128]{2,1,0:T(8,128)(2,1)S(1)}, u32[]{:S(2)}, u32[]{:S(2)}) %all-to-all-start.1) | async-done | bytes 786464 | tf_op jit(solution)/shard_map/all_to_all | solution.py:275
  128.3 2.7 %project.3 = (bf16[192,320]{1,0:T(8,128)(2,1)S(1)}, bf16[192,320]{1,0:T(8,128)(2,1)S(1)}) custom-call(s32[2]{0:T(128)S(1)} %pad_add_fusion.1.place, bf16[16,192,128]{2,1,0:T(8,128)(2,1)S(1)} %all-to-all-done.1.acts, bf16[4,256,1280]{2,1,0:T(8,128)(2,1)S(1)} %all-to-all-done.w_own, bf16[4,256,1280]{2,1,0:T(8,128)(2,1)} %collective-permute-done.10.w_other), custom_call_target="tpu_custom_call" | custom-call | tf_op jit(solution)/shard_map/project/pallas_call | solution.py:363
  131.0 12.2 %collective-permute-start.11 = (bf16[192,320]{1,0:T(8,128)(2,1)S(1)}, bf16[192,320]{1,0:T(8,128)(2,1)S(1)}, u32[]{:S(2)}, u32[]{:S(2)}) collective-permute-start(bf16[192,320]{1,0:T(8,128)(2,1)S(1)} %get-tuple-element.29), channel_id=1, source_target_pairs={{0,2},{1,3},{2,0},{3,1},{4,6},{5,7},{6,4},{7,5},{8,10},{9,11},{10,... | collective-permute-start | bytes 368648 | tf_op jit(solution)/shard_map/ppermute | solution.py:374
  143.2 3.0 %collective-permute-start.13 = (bf16[192,320]{1,0:T(8,128)(2,1)S(1)}, bf16[192,320]{1,0:T(8,128)(2,1)S(1)}, u32[]{:S(2)}, u32[]{:S(2)}) collective-permute-start(bf16[192,320]{1,0:T(8,128)(2,1)S(1)} %get-tuple-element.31), channel_id=1, source_target_pairs={{0,3},{1,2},{2,1},{3,0},{4,7},{5,6},{6,5},{7,4},{8,11},{9,10},{10,... | collective-permute-start | bytes 368648 | tf_op jit(solution)/shard_map/ppermute | solution.py:375
  146.2 2.7 %project.2 = (f32[192,320]{1,0:T(8,128)S(1)}, bf16[192,320]{1,0:T(8,128)(2,1)S(1)}) custom-call(s32[2]{0:T(128)S(1)} %pad_add_fusion.place, bf16[16,192,128]{2,1,0:T(8,128)(2,1)S(1)} %all-to-all-done.1.acts, bf16[4,256,1280]{2,1,0:T(8,128)(2,1)S(1)} %all-to-all-done.w_own, bf16[4,256,1280]{2,1,0:T(8,128)(2,1)} %collective-permute-done.10.w_other), custom_call_target="tpu_custom_call" | custom-call | tf_op jit(solution)/shard_map/project/pallas_call | solution.py:363
  149.0 2.1 %collective-permute-start.12 = (bf16[192,320]{1,0:T(8,128)(2,1)S(1)}, bf16[192,320]{1,0:T(8,128)(2,1)S(1)}, u32[]{:S(2)}, u32[]{:S(2)}) collective-permute-start(bf16[192,320]{1,0:T(8,128)(2,1)S(1)} %get-tuple-element.30), channel_id=1, source_target_pairs={{0,1},{1,0},{2,3},{3,2},{4,5},{5,4},{6,7},{7,6},{8,9},{9,8},{10,11... | collective-permute-start | bytes 368648 | tf_op jit(solution)/shard_map/ppermute | solution.py:376
  151.1 22.0 %collective-permute-done.13.both_got = bf16[192,320]{1,0:T(8,128)(2,1)S(1)} collective-permute-done((bf16[192,320]{1,0:T(8,128)(2,1)S(1)}, bf16[192,320]{1,0:T(8,128)(2,1)S(1)}, u32[]{:S(2)}, u32[]{:S(2)}) %collective-permute-start.13) | collective-permute-done | bytes 122912 | tf_op jit(solution)/shard_map/ppermute | solution.py:375
  173.1 1.4 finish.1
  (30 shorter events, 3.4 us)
Async XLA Ops:
  3.5 8.7 %collective-permute-start = (bf16[192,768]{1,0:T(8,128)(2,1)}, bf16[192,768]{1,0:T(8,128)(2,1)S(1)}, u32[]{:S(2)}, u32[]{:S(2)}) collective-permute-start(bf16[192,768]{1,0:T(8,128)(2,1)} %get-tuple-element.17), channel_id=1, source_target_pairs={{0,64},{16,80},{32,96},{48,112},{64,0},{80,16},{96,32},{112,48},{1... | collective-permute-start | bytes 884744 | tf_op jit(solution)/shard_map/ppermute | solution.py:281
  12.2 0.7 copy-start.5
  12.9 48.8 %all-to-all-start = ((bf16[4,256,1280]{2,1,0:T(8,128)(2,1)}), bf16[4,256,1280]{2,1,0:T(8,128)(2,1)S(1)}, u32[]{:S(2)}, u32[]{:S(2)}) async-start(bf16[4,256,1280]{2,1,0:T(8,128)(2,1)} %cut.1), calls=%async_computation | async-start | bytes 5242880 | tf_op jit(solution)/shard_map/all_to_all | solution.py:275
  21.2 24.6 %collective-permute-start.4 = (bf16[384,512]{1,0:T(8,128)(2,1)}, bf16[384,512]{1,0:T(8,128)(2,1)S(1)}, u32[]{:S(2)}, u32[]{:S(2)}) collective-permute-start(bf16[384,512]{1,0:T(8,128)(2,1)} %get-tuple-element.22.refs_0_), channel_id=1, source_target_pairs={{0,128},{16,144},{32,160},{48,176},{64,192},{80,208},{96,224},{112... | collective-permute-start | bytes 1179656 | tf_op jit(solution)/shard_map/ppermute | solution.py:281
  26.1 32.3 %collective-permute-start.3 = (bf16[384,512]{1,0:T(8,128)(2,1)}, bf16[384,512]{1,0:T(8,128)(2,1)S(1)}, u32[]{:S(2)}, u32[]{:S(2)}) collective-permute-start(bf16[384,512]{1,0:T(8,128)(2,1)} %get-tuple-element.22.refs_0_), channel_id=1, source_target_pairs={{0,32},{16,48},{32,0},{48,16},{64,96},{80,112},{96,64},{112,80},{1... | collective-permute-start | bytes 1179656 | tf_op jit(solution)/shard_map/ppermute | solution.py:278
  30.9 25.5 %collective-permute-start.8 = (bf16[384,256]{1,0:T(8,128)(2,1)}, bf16[384,256]{1,0:T(8,128)(2,1)S(1)}, u32[]{:S(2)}, u32[]{:S(2)}) collective-permute-start(bf16[384,256]{1,0:T(8,128)(2,1)} %get-tuple-element.26.refs_8_), channel_id=1, source_target_pairs={{0,256},{16,272},{32,288},{48,304},{64,320},{80,336},{96,352},{112... | collective-permute-start | bytes 589832 | tf_op jit(solution)/shard_map/ppermute | solution.py:281
  39.7 22.0 %collective-permute-start.2 = (bf16[384,512]{1,0:T(8,128)(2,1)}, bf16[384,512]{1,0:T(8,128)(2,1)}, u32[]{:S(2)}, u32[]{:S(2)}) collective-permute-start(bf16[384,512]{1,0:T(8,128)(2,1)} %get-tuple-element.22.refs_0_), channel_id=1, source_target_pairs={{0,48},{16,0},{32,16},{48,32},{64,112},{80,64},{96,80},{112,96},{1... | collective-permute-start | bytes 1179656 | tf_op jit(solution)/shard_map/ppermute | solution.py:278
  42.4 19.3 %collective-permute-start.1 = (bf16[384,512]{1,0:T(8,128)(2,1)}, bf16[384,512]{1,0:T(8,128)(2,1)}, u32[]{:S(2)}, u32[]{:S(2)}) collective-permute-start(bf16[384,512]{1,0:T(8,128)(2,1)} %get-tuple-element.22.refs_0_), channel_id=1, source_target_pairs={{0,16},{16,32},{32,48},{48,0},{64,80},{80,96},{96,112},{112,64},{1... | collective-permute-start | bytes 1179656 | tf_op jit(solution)/shard_map/ppermute | solution.py:278
  45.8 27.7 %copy-start.3 = (bf16[384,512]{1,0:T(8,128)(2,1)}, bf16[384,512]{1,0:T(8,128)(2,1)S(1)}, u32[]{:S(2)}) copy-start(bf16[384,512]{1,0:T(8,128)(2,1)S(1)} %collective-permute-done.4.refs_4_) | copy-start | bytes 1179652
  45.8 18.6 %collective-permute-start.7 = (bf16[384,512]{1,0:T(8,128)(2,1)S(1)}, bf16[384,512]{1,0:T(8,128)(2,1)}, u32[]{:S(2)}, u32[]{:S(2)}) collective-permute-start(bf16[384,512]{1,0:T(8,128)(2,1)S(1)} %collective-permute-done.4.refs_4_), channel_id=1, source_target_pairs={{0,32},{16,48},{32,0},{48,16},{64,96},{80,112},{96,64},{112,80},{1... | collective-permute-start | bytes 1179656 | tf_op jit(solution)/shard_map/ppermute | solution.py:278
  56.4 2.0 %copy-start.7 = (bf16[384,256]{1,0:T(8,128)(2,1)}, bf16[384,256]{1,0:T(8,128)(2,1)S(1)}, u32[]{:S(2)}) copy-start(bf16[384,256]{1,0:T(8,128)(2,1)S(1)} %collective-permute-done.8.refs_8_) | copy-start | bytes 589828
  56.4 14.2 %collective-permute-start.6 = (bf16[384,512]{1,0:T(8,128)(2,1)S(1)}, bf16[384,512]{1,0:T(8,128)(2,1)}, u32[]{:S(2)}, u32[]{:S(2)}) collective-permute-start(bf16[384,512]{1,0:T(8,128)(2,1)S(1)} %collective-permute-done.4.refs_4_), channel_id=1, source_target_pairs={{0,48},{16,0},{32,16},{48,32},{64,112},{80,64},{96,80},{112,96},{1... | collective-permute-start | bytes 1179656 | tf_op jit(solution)/shard_map/ppermute | solution.py:278
  58.4 15.1 %copy-start.4 = (bf16[384,512]{1,0:T(8,128)(2,1)}, bf16[384,512]{1,0:T(8,128)(2,1)S(1)}, u32[]{:S(2)}) copy-start(bf16[384,512]{1,0:T(8,128)(2,1)S(1)} %collective-permute-done.3.refs_3_) | copy-start | bytes 1179652
  58.4 15.1 %collective-permute-start.5 = (bf16[384,512]{1,0:T(8,128)(2,1)S(1)}, bf16[384,512]{1,0:T(8,128)(2,1)}, u32[]{:S(2)}, u32[]{:S(2)}) collective-permute-start(bf16[384,512]{1,0:T(8,128)(2,1)S(1)} %collective-permute-done.4.refs_4_), channel_id=1, source_target_pairs={{0,16},{16,32},{32,48},{48,0},{64,80},{80,96},{96,112},{112,64},{1... | collective-permute-start | bytes 1179656 | tf_op jit(solution)/shard_map/ppermute | solution.py:278
  79.6 26.5 %collective-permute-start.9 = (bf16[416,256]{1,0:T(8,128)(2,1)}, bf16[416,256]{1,0:T(8,128)(2,1)S(1)}, u32[]{:S(2)}, u32[]{:S(2)}) collective-permute-start(bf16[416,256]{1,0:T(8,128)(2,1)} %attend.2), channel_id=1, source_target_pairs={{0,256},{16,272},{32,288},{48,304},{64,320},{80,336},{96,352},{112... | collective-permute-start | bytes 638984 | tf_op jit(solution)/shard_map/ppermute | solution.py:281
  106.0 0.7 copy-start.6
  109.9 18.4 %all-to-all-start.1 = ((bf16[16,192,128]{2,1,0:T(8,128)(2,1)}), bf16[16,192,128]{2,1,0:T(8,128)(2,1)S(1)}, u32[]{:S(2)}, u32[]{:S(2)}) async-start(bf16[16,192,128]{2,1,0:T(8,128)(2,1)} %merge.1), calls=%async_computation.1 | async-start | bytes 1572864 | tf_op jit(solution)/shard_map/all_to_all | solution.py:275
  115.3 6.9 %collective-permute-start.10 = (bf16[4,256,1280]{2,1,0:T(8,128)(2,1)S(1)}, bf16[4,256,1280]{2,1,0:T(8,128)(2,1)}, u32[]{:S(2)}, u32[]{:S(2)}) collective-permute-start(bf16[4,256,1280]{2,1,0:T(8,128)(2,1)S(1)} %all-to-all-done.w_own), channel_id=1, source_target_pairs={{0,1},{1,0},{2,3},{3,2},{4,5},{5,4},{6,7},{7,6},{8,9},{9,8},{10,11... | collective-permute-start | bytes 7864328 | tf_op jit(solution)/shard_map/ppermute | solution.py:347
  131.0 20.1 %collective-permute-start.11 = (bf16[192,320]{1,0:T(8,128)(2,1)S(1)}, bf16[192,320]{1,0:T(8,128)(2,1)S(1)}, u32[]{:S(2)}, u32[]{:S(2)}) collective-permute-start(bf16[192,320]{1,0:T(8,128)(2,1)S(1)} %get-tuple-element.29), channel_id=1, source_target_pairs={{0,2},{1,3},{2,0},{3,1},{4,6},{5,7},{6,4},{7,5},{8,10},{9,11},{10,... | collective-permute-start | bytes 368648 | tf_op jit(solution)/shard_map/ppermute | solution.py:374
  143.2 7.9 %copy-start.8 = (f32[320]{0:T(512)S(1)}, f32[320]{0:T(512)}, u32[]{:S(2)}) copy-start(f32[320]{0:T(512)} %param.19) | copy-start | bytes 3844
  143.2 29.9 %copy-start = (bf16[192,320]{1,0:T(8,128)(2,1)S(1)}, bf16[192,320]{1,0:T(8,128)(2,1)}, u32[]{:S(2)}) copy-start(bf16[192,320]{1,0:T(8,128)(2,1)} %tokens.1) | copy-start | bytes 368644
  143.2 29.9 %copy-start.1 = (bf16[192,320]{1,0:T(8,128)(2,1)S(1)}, bf16[192,320]{1,0:T(8,128)(2,1)}, u32[]{:S(2)}) copy-start(bf16[192,320]{1,0:T(8,128)(2,1)} %d_tokens.1) | copy-start | bytes 368644
  143.2 29.9 %copy-start.2 = (s32[192]{0:T(256)S(1)}, s32[192]{0:T(256)}, u32[]{:S(2)}) copy-start(s32[192]{0:T(256)} %flags.3) | copy-start | bytes 2308
  143.2 29.8 %collective-permute-start.13 = (bf16[192,320]{1,0:T(8,128)(2,1)S(1)}, bf16[192,320]{1,0:T(8,128)(2,1)S(1)}, u32[]{:S(2)}, u32[]{:S(2)}) collective-permute-start(bf16[192,320]{1,0:T(8,128)(2,1)S(1)} %get-tuple-element.31), channel_id=1, source_target_pairs={{0,3},{1,2},{2,1},{3,0},{4,7},{5,6},{6,5},{7,4},{8,11},{9,10},{10,... | collective-permute-start | bytes 368648 | tf_op jit(solution)/shard_map/ppermute | solution.py:375
  149.0 24.1 %collective-permute-start.12 = (bf16[192,320]{1,0:T(8,128)(2,1)S(1)}, bf16[192,320]{1,0:T(8,128)(2,1)S(1)}, u32[]{:S(2)}, u32[]{:S(2)}) collective-permute-start(bf16[192,320]{1,0:T(8,128)(2,1)S(1)} %get-tuple-element.30), channel_id=1, source_target_pairs={{0,1},{1,0},{2,3},{3,2},{4,5},{5,4},{6,7},{7,6},{8,9},{9,8},{10,11... | collective-permute-start | bytes 368648 | tf_op jit(solution)/shard_map/ppermute | solution.py:376

commit v5 on v4

--- a/solution.py
+++ b/solution.py
@@ -317,8 +317,9 @@
         name="join",
     )(got, qd, kv)
     kv_far = z(kv, 2)
-    qd_far = z(qd, 4)
-    kv = [kv] + [y(kv, k) for k in (1, 3, 2)] + [kv_far] + [y(kv_far, k) for k in (1, 3, 2)]
+    near_rows = [y(kv, k) for k in (1, 3, 2)]
+    qd_far = z(after(qd, (near_rows[:2], kv_far)), 4)
+    kv = [kv] + near_rows + [kv_far] + [y(kv_far, k) for k in (1, 3, 2)]
 
     w_own = exchange(after(weights, got), "x")
     qd_far = after(qd_far, w_own)

time: 175 us -> 173 us (0.989)
  waiting for transfers between devices: 61.5 us -> 53.4 us
  starting transfers between devices: 80.3 us -> 86.2 us
    ppermute x6, waiting for transfers between devices: 11.7 us -> 0.02 us  [y(): return lax.ppermute(a, TM, over_y(k))]
    all_to_all x2, starting transfers between devices: 12 us -> 20.8 us  [exchange(): return lax.all_to_all(a, axes, 0, 0, tiled=True)]
    ppermute x6, starting transfers between devices: 26 us -> 20.2 us  [y(): return lax.ppermute(a, TM, over_y(k))]
    ppermute x4, waiting for transfers between devices: 17.1 us -> 20.7 us  [z(): return lax.ppermute(a, TM, over_z(k))]
    ppermute x4, starting transfers between devices: 23.1 us -> 25.6 us  [z(): return lax.ppermute(a, TM, over_z(k))]
  transfers between devices with their start and end apart: 16 -> 16, of which waited for: 9 -> 7; matrix products, arithmetic and copies ran while one was open for 0% -> 0% of each run, Pallas kernels for 8% -> 8%
where the time goes in v5:
time: 173 us; the launch traced here: 172 us
  starting transfers between devices  86.2 us (50%)
  waiting for transfers between devices  53.4 us (31%)
  Pallas kernels  30 us (17%)
    ppermute x4, starting transfers between devices, z(): return lax.ppermute(a, TM, over_z(k))  25.6 us
    ppermute x1, waiting for transfers between devices, per_device(): both_got = lax.ppermute(both_send, MP, flip(3))  21.9 us
    all_to_all x2, starting transfers between devices, exchange(): return lax.all_to_all(a, axes, 0, 0, tiled=True)  20.8 us
    ppermute x4, waiting for transfers between devices, z(): return lax.ppermute(a, TM, over_z(k))  20.7 us
    ppermute x6, starting transfers between devices, y(): return lax.ppermute(a, TM, over_y(k))  20.2 us
    ppermute x1, starting transfers between devices, per_device(): z_got = lax.ppermute(z_send, MP, flip(2))  12.5 us
    pallas_call x2, Pallas kernels, attend(): pl.pallas_call(attend_kernel, out_shape=part, in_specs=[HBM_SPEC] * 9, ou...  12.2 us
    all_to_all x2, waiting for transfers between devices, exchange(): return lax.all_to_all(a, axes, 0, 0, tiled=True)  6.06 us
  transfers between devices with their start and end apart: 16, of which 7 were waited for; matrix products, arithmetic and copies ran while one was open for 0% of the time, Pallas kernels for 8%

profile of v5, /device:TPU:1, one launch (start us, length us, event | category | flops | bytes accessed | tf_op | source)
XLA Modules:
  0.0 172.2 jit_solution(6962500522577050586)
XLA Ops:
  0.7 2.8 %pack.1 = (bf16[384,256]{1,0:T(8,128)(2,1)}, bf16[384,512]{1,0:T(8,128)(2,1)}, bf16[192,768]{1,0:T(8,128)(2,1)}) custom-call(s32[1]{0:T(128)} %bitcast.2.odd, s32[192]{0:T(256)} %flags.3, bf16[192,256]{1,0:T(8,128)(2,1)} %refs_0_.1, bf16[192,256]{1,0:T(8,128)(2,1)} %refs_1_.1, bf16[192,256]{1,0:T(8,128)(2,1)} %refs_2_.1, bf16[192,256]{1,0:T(8,128)(2,1)} %refs_3_.1, ...), custom_call_target="tpu_custom_call" | custom-call | tf_op jit(solution)/shard_map/pack/pallas_call | solution.py:283
  3.5 4.4 %collective-permute-start = (bf16[192,768]{1,0:T(8,128)(2,1)}, bf16[192,768]{1,0:T(8,128)(2,1)S(1)}, u32[]{:S(2)}, u32[]{:S(2)}) collective-permute-start(bf16[192,768]{1,0:T(8,128)(2,1)} %get-tuple-element.18), channel_id=1, source_target_pairs={{0,64},{16,80},{32,96},{48,112},{64,0},{80,16},{96,32},{112,48},{1... | collective-permute-start | bytes 884744 | tf_op jit(solution)/shard_map/ppermute | solution.py:281
  7.9 3.3 %cut.1 = bf16[4,256,1280]{2,1,0:T(8,128)(2,1)} custom-call(bf16[256,5120]{1,0:T(8,128)(2,1)} %w_in), custom_call_target="tpu_custom_call" | custom-call | tf_op jit(solution)/shard_map/cut/pallas_call | solution.py:298
  11.2 1.0 collective-permute-done.got
  12.9 6.5 %all-to-all-start = ((bf16[4,256,1280]{2,1,0:T(8,128)(2,1)}), bf16[4,256,1280]{2,1,0:T(8,128)(2,1)S(1)}, u32[]{:S(2)}, u32[]{:S(2)}) async-start(bf16[4,256,1280]{2,1,0:T(8,128)(2,1)} %cut.1), calls=%async_computation | async-start | bytes 5242880 | tf_op jit(solution)/shard_map/all_to_all | solution.py:275
  19.5 1.7 join.1
  21.2 4.9 %collective-permute-start.4 = (bf16[384,512]{1,0:T(8,128)(2,1)}, bf16[384,512]{1,0:T(8,128)(2,1)S(1)}, u32[]{:S(2)}, u32[]{:S(2)}) collective-permute-start(bf16[384,512]{1,0:T(8,128)(2,1)} %get-tuple-element.23.refs_0_), channel_id=1, source_target_pairs={{0,128},{16,144},{32,160},{48,176},{64,192},{80,208},{96,224},{112... | collective-permute-start | bytes 1179656 | tf_op jit(solution)/shard_map/ppermute | solution.py:281
  26.1 4.6 %collective-permute-start.2 = (bf16[384,512]{1,0:T(8,128)(2,1)}, bf16[384,512]{1,0:T(8,128)(2,1)S(1)}, u32[]{:S(2)}, u32[]{:S(2)}) collective-permute-start(bf16[384,512]{1,0:T(8,128)(2,1)} %get-tuple-element.23.refs_0_), channel_id=1, source_target_pairs={{0,48},{16,0},{32,16},{48,32},{64,112},{80,64},{96,80},{112,96},{1... | collective-permute-start | bytes 1179656 | tf_op jit(solution)/shard_map/ppermute | solution.py:278
  30.7 1.9 %collective-permute-start.1 = (bf16[384,512]{1,0:T(8,128)(2,1)}, bf16[384,512]{1,0:T(8,128)(2,1)S(1)}, u32[]{:S(2)}, u32[]{:S(2)}) collective-permute-start(bf16[384,512]{1,0:T(8,128)(2,1)} %get-tuple-element.23.refs_0_), channel_id=1, source_target_pairs={{0,16},{16,32},{32,48},{48,0},{64,80},{80,96},{96,112},{112,64},{1... | collective-permute-start | bytes 1179656 | tf_op jit(solution)/shard_map/ppermute | solution.py:278
  32.7 3.5 %collective-permute-start.3 = (bf16[384,512]{1,0:T(8,128)(2,1)}, bf16[384,512]{1,0:T(8,128)(2,1)}, u32[]{:S(2)}, u32[]{:S(2)}) collective-permute-start(bf16[384,512]{1,0:T(8,128)(2,1)} %get-tuple-element.23.refs_0_), channel_id=1, source_target_pairs={{0,32},{16,48},{32,0},{48,16},{64,96},{80,112},{96,64},{112,80},{1... | collective-permute-start | bytes 1179656 | tf_op jit(solution)/shard_map/ppermute | solution.py:278
  36.2 7.0 %collective-permute-done.4.refs_4_ = bf16[384,512]{1,0:T(8,128)(2,1)S(1)} collective-permute-done((bf16[384,512]{1,0:T(8,128)(2,1)}, bf16[384,512]{1,0:T(8,128)(2,1)S(1)}, u32[]{:S(2)}, u32[]{:S(2)}) %collective-permute-start.4) | collective-permute-done | bytes 393248 | tf_op jit(solution)/shard_map/ppermute | solution.py:281
  43.2 4.8 %collective-permute-start.7 = (bf16[384,512]{1,0:T(8,128)(2,1)S(1)}, bf16[384,512]{1,0:T(8,128)(2,1)}, u32[]{:S(2)}, u32[]{:S(2)}) collective-permute-start(bf16[384,512]{1,0:T(8,128)(2,1)S(1)} %collective-permute-done.4.refs_4_), channel_id=1, source_target_pairs={{0,32},{16,48},{32,0},{48,16},{64,96},{80,112},{96,64},{112,80},{1... | collective-permute-start | bytes 1179656 | tf_op jit(solution)/shard_map/ppermute | solution.py:278
  48.1 2.8 %collective-permute-start.6 = (bf16[384,512]{1,0:T(8,128)(2,1)S(1)}, bf16[384,512]{1,0:T(8,128)(2,1)}, u32[]{:S(2)}, u32[]{:S(2)}) collective-permute-start(bf16[384,512]{1,0:T(8,128)(2,1)S(1)} %collective-permute-done.4.refs_4_), channel_id=1, source_target_pairs={{0,48},{16,0},{32,16},{48,32},{64,112},{80,64},{96,80},{112,96},{1... | collective-permute-start | bytes 1179656 | tf_op jit(solution)/shard_map/ppermute | solution.py:278
  50.9 2.5 %collective-permute-start.5 = (bf16[384,512]{1,0:T(8,128)(2,1)S(1)}, bf16[384,512]{1,0:T(8,128)(2,1)}, u32[]{:S(2)}, u32[]{:S(2)}) collective-permute-start(bf16[384,512]{1,0:T(8,128)(2,1)S(1)} %collective-permute-done.4.refs_4_), channel_id=1, source_target_pairs={{0,16},{16,32},{32,48},{48,0},{64,80},{80,96},{96,112},{112,64},{1... | collective-permute-start | bytes 1179656 | tf_op jit(solution)/shard_map/ppermute | solution.py:278
  53.4 8.8 %collective-permute-start.8 = (bf16[384,256]{1,0:T(8,128)(2,1)}, bf16[384,256]{1,0:T(8,128)(2,1)}, u32[]{:S(2)}, u32[]{:S(2)}) collective-permute-start(bf16[384,256]{1,0:T(8,128)(2,1)} %get-tuple-element.28.refs_8_), channel_id=1, source_target_pairs={{0,256},{16,272},{32,288},{48,304},{64,320},{80,336},{96,352},{112... | collective-permute-start | bytes 589832 | tf_op jit(solution)/shard_map/ppermute | solution.py:281
  62.2 8.8 %collective-permute-done.8.refs_8_ = bf16[384,256]{1,0:T(8,128)(2,1)} collective-permute-done((bf16[384,256]{1,0:T(8,128)(2,1)}, bf16[384,256]{1,0:T(8,128)(2,1)}, u32[]{:S(2)}, u32[]{:S(2)}) %collective-permute-start.8) | collective-permute-done | bytes 196640 | tf_op jit(solution)/shard_map/ppermute | solution.py:281
  71.1 6.1 %attend.2 = bf16[416,256]{1,0:T(8,128)(2,1)} custom-call(bf16[384,512]{1,0:T(8,128)(2,1)} %get-tuple-element.23.refs_0_, bf16[384,512]{1,0:T(8,128)(2,1)} %copy-done.5, bf16[384,512]{1,0:T(8,128)(2,1)} %copy-done.4, bf16[384,512]{1,0:T(8,128)(2,1)} %collective-permute-done.3.refs_3_, bf16[384,512]{1,0:T(8,128)(2,1)} %copy-done.3, ...), custom_call_target="tpu_custom_call" | custom-call | tf_op jit(solution)/shard_map/attend/pallas_call | solution.py:329
  77.2 7.5 %collective-permute-start.9 = (bf16[416,256]{1,0:T(8,128)(2,1)}, bf16[416,256]{1,0:T(8,128)(2,1)S(1)}, u32[]{:S(2)}, u32[]{:S(2)}) collective-permute-start(bf16[416,256]{1,0:T(8,128)(2,1)} %attend.2), channel_id=1, source_target_pairs={{0,256},{16,272},{32,288},{48,304},{64,320},{80,336},{96,352},{112... | collective-permute-start | bytes 638984 | tf_op jit(solution)/shard_map/ppermute | solution.py:281
  84.6 6.1 %attend.3.one = bf16[416,256]{1,0:T(8,128)(2,1)} custom-call(bf16[384,512]{1,0:T(8,128)(2,1)} %get-tuple-element.23.refs_0_, bf16[384,512]{1,0:T(8,128)(2,1)} %copy-done.5, bf16[384,512]{1,0:T(8,128)(2,1)} %copy-done.4, bf16[384,512]{1,0:T(8,128)(2,1)} %collective-permute-done.3.refs_3_, bf16[384,512]{1,0:T(8,128)(2,1)} %copy-done.3, ...), custom_call_target="tpu_custom_call" | custom-call | tf_op jit(solution)/shard_map/attend/pallas_call | solution.py:329
  90.8 3.9 %collective-permute-done.9.two = bf16[416,256]{1,0:T(8,128)(2,1)S(1)} collective-permute-done((bf16[416,256]{1,0:T(8,128)(2,1)}, bf16[416,256]{1,0:T(8,128)(2,1)S(1)}, u32[]{:S(2)}, u32[]{:S(2)}) %collective-permute-start.9) | collective-permute-done | bytes 213024 | tf_op jit(solution)/shard_map/ppermute | solution.py:281
  95.3 3.1 %merge.1 = bf16[16,192,128]{2,1,0:T(8,128)(2,1)} custom-call(s32[1]{0:T(128)} %bitcast.2.odd, bf16[416,256]{1,0:T(8,128)(2,1)} %attend.3.one, bf16[416,256]{1,0:T(8,128)(2,1)} %copy-done.7), custom_call_target="tpu_custom_call" | custom-call | tf_op jit(solution)/shard_map/merge/pallas_call | solution.py:350
  98.5 14.3 %all-to-all-start.1 = ((bf16[16,192,128]{2,1,0:T(8,128)(2,1)}), bf16[16,192,128]{2,1,0:T(8,128)(2,1)S(1)}, u32[]{:S(2)}, u32[]{:S(2)}) async-start(bf16[16,192,128]{2,1,0:T(8,128)(2,1)} %merge.1), calls=%async_computation.1 | async-start | bytes 1572864 | tf_op jit(solution)/shard_map/all_to_all | solution.py:275
  112.8 2.0 %collective-permute-start.10 = (bf16[4,256,1280]{2,1,0:T(8,128)(2,1)S(1)}, bf16[4,256,1280]{2,1,0:T(8,128)(2,1)}, u32[]{:S(2)}, u32[]{:S(2)}) collective-permute-start(bf16[4,256,1280]{2,1,0:T(8,128)(2,1)S(1)} %all-to-all-done.w_own), channel_id=1, source_target_pairs={{0,1},{1,0},{2,3},{3,2},{4,5},{5,4},{6,7},{7,6},{8,9},{9,8},{10,11... | collective-permute-start | bytes 7864328 | tf_op jit(solution)/shard_map/ppermute | solution.py:348
  115.0 4.7 %collective-permute-done.10.w_other = bf16[4,256,1280]{2,1,0:T(8,128)(2,1)} collective-permute-done((bf16[4,256,1280]{2,1,0:T(8,128)(2,1)S(1)}, bf16[4,256,1280]{2,1,0:T(8,128)(2,1)}, u32[]{:S(2)}, u32[]{:S(2)}) %collective-permute-start.10) | collective-permute-done | bytes 2621472 | tf_op jit(solution)/shard_map/ppermute | solution.py:348
  119.7 6.1 %all-to-all-done.1.acts = bf16[16,192,128]{2,1,0:T(8,128)(2,1)S(1)} async-done(((bf16[16,192,128]{2,1,0:T(8,128)(2,1)}), bf16[16,192,128]{2,1,0:T(8,128)(2,1)S(1)}, u32[]{:S(2)}, u32[]{:S(2)}) %all-to-all-start.1) | async-done | bytes 786464 | tf_op jit(solution)/shard_map/all_to_all | solution.py:275
  125.8 2.7 %project.3 = (bf16[192,320]{1,0:T(8,128)(2,1)S(1)}, bf16[192,320]{1,0:T(8,128)(2,1)S(1)}) custom-call(s32[2]{0:T(128)S(1)} %pad_add_fusion.1.place, bf16[16,192,128]{2,1,0:T(8,128)(2,1)S(1)} %all-to-all-done.1.acts, bf16[4,256,1280]{2,1,0:T(8,128)(2,1)S(1)} %all-to-all-done.w_own, bf16[4,256,1280]{2,1,0:T(8,128)(2,1)} %collective-permute-done.10.w_other), custom_call_target="tpu_custom_call" | custom-call | tf_op jit(solution)/shard_map/project/pallas_call | solution.py:364
  128.5 12.5 %collective-permute-start.11 = (bf16[192,320]{1,0:T(8,128)(2,1)S(1)}, bf16[192,320]{1,0:T(8,128)(2,1)S(1)}, u32[]{:S(2)}, u32[]{:S(2)}) collective-permute-start(bf16[192,320]{1,0:T(8,128)(2,1)S(1)} %get-tuple-element.31), channel_id=1, source_target_pairs={{0,2},{1,3},{2,0},{3,1},{4,6},{5,7},{6,4},{7,5},{8,10},{9,11},{10,... | collective-permute-start | bytes 368648 | tf_op jit(solution)/shard_map/ppermute | solution.py:375
  141.0 2.8 %collective-permute-start.13 = (bf16[192,320]{1,0:T(8,128)(2,1)S(1)}, bf16[192,320]{1,0:T(8,128)(2,1)S(1)}, u32[]{:S(2)}, u32[]{:S(2)}) collective-permute-start(bf16[192,320]{1,0:T(8,128)(2,1)S(1)} %get-tuple-element.33), channel_id=1, source_target_pairs={{0,3},{1,2},{2,1},{3,0},{4,7},{5,6},{6,5},{7,4},{8,11},{9,10},{10,... | collective-permute-start | bytes 368648 | tf_op jit(solution)/shard_map/ppermute | solution.py:376
  143.9 2.7 %project.2 = (f32[192,320]{1,0:T(8,128)S(1)}, bf16[192,320]{1,0:T(8,128)(2,1)S(1)}) custom-call(s32[2]{0:T(128)S(1)} %pad_add_fusion.place, bf16[16,192,128]{2,1,0:T(8,128)(2,1)S(1)} %all-to-all-done.1.acts, bf16[4,256,1280]{2,1,0:T(8,128)(2,1)S(1)} %all-to-all-done.w_own, bf16[4,256,1280]{2,1,0:T(8,128)(2,1)} %collective-permute-done.10.w_other), custom_call_target="tpu_custom_call" | custom-call | tf_op jit(solution)/shard_map/project/pallas_call | solution.py:364
  146.6 2.3 %collective-permute-start.12 = (bf16[192,320]{1,0:T(8,128)(2,1)S(1)}, bf16[192,320]{1,0:T(8,128)(2,1)S(1)}, u32[]{:S(2)}, u32[]{:S(2)}) collective-permute-start(bf16[192,320]{1,0:T(8,128)(2,1)S(1)} %get-tuple-element.32), channel_id=1, source_target_pairs={{0,1},{1,0},{2,3},{3,2},{4,5},{5,4},{6,7},{7,6},{8,9},{9,8},{10,11... | collective-permute-start | bytes 368648 | tf_op jit(solution)/shard_map/ppermute | solution.py:377
  148.9 21.9 %collective-permute-done.13.both_got = bf16[192,320]{1,0:T(8,128)(2,1)S(1)} collective-permute-done((bf16[192,320]{1,0:T(8,128)(2,1)S(1)}, bf16[192,320]{1,0:T(8,128)(2,1)S(1)}, u32[]{:S(2)}, u32[]{:S(2)}) %collective-permute-start.13) | collective-permute-done | bytes 122912 | tf_op jit(solution)/shard_map/ppermute | solution.py:376
  170.8 1.4 finish.1
  (30 shorter events, 1.6 us)
Async XLA Ops:
  3.5 8.7 %collective-permute-start = (bf16[192,768]{1,0:T(8,128)(2,1)}, bf16[192,768]{1,0:T(8,128)(2,1)S(1)}, u32[]{:S(2)}, u32[]{:S(2)}) collective-permute-start(bf16[192,768]{1,0:T(8,128)(2,1)} %get-tuple-element.18), channel_id=1, source_target_pairs={{0,64},{16,80},{32,96},{48,112},{64,0},{80,16},{96,32},{112,48},{1... | collective-permute-start | bytes 884744 | tf_op jit(solution)/shard_map/ppermute | solution.py:281
  12.2 0.7 copy-start.6
  12.9 58.1 %all-to-all-start = ((bf16[4,256,1280]{2,1,0:T(8,128)(2,1)}), bf16[4,256,1280]{2,1,0:T(8,128)(2,1)S(1)}, u32[]{:S(2)}, u32[]{:S(2)}) async-start(bf16[4,256,1280]{2,1,0:T(8,128)(2,1)} %cut.1), calls=%async_computation | async-start | bytes 5242880 | tf_op jit(solution)/shard_map/all_to_all | solution.py:275
  21.2 22.1 %collective-permute-start.4 = (bf16[384,512]{1,0:T(8,128)(2,1)}, bf16[384,512]{1,0:T(8,128)(2,1)S(1)}, u32[]{:S(2)}, u32[]{:S(2)}) collective-permute-start(bf16[384,512]{1,0:T(8,128)(2,1)} %get-tuple-element.23.refs_0_), channel_id=1, source_target_pairs={{0,128},{16,144},{32,160},{48,176},{64,192},{80,208},{96,224},{112... | collective-permute-start | bytes 1179656 | tf_op jit(solution)/shard_map/ppermute | solution.py:281
  26.1 24.8 %collective-permute-start.2 = (bf16[384,512]{1,0:T(8,128)(2,1)}, bf16[384,512]{1,0:T(8,128)(2,1)S(1)}, u32[]{:S(2)}, u32[]{:S(2)}) collective-permute-start(bf16[384,512]{1,0:T(8,128)(2,1)} %get-tuple-element.23.refs_0_), channel_id=1, source_target_pairs={{0,48},{16,0},{32,16},{48,32},{64,112},{80,64},{96,80},{112,96},{1... | collective-permute-start | bytes 1179656 | tf_op jit(solution)/shard_map/ppermute | solution.py:278
  30.7 22.7 %collective-permute-start.1 = (bf16[384,512]{1,0:T(8,128)(2,1)}, bf16[384,512]{1,0:T(8,128)(2,1)S(1)}, u32[]{:S(2)}, u32[]{:S(2)}) collective-permute-start(bf16[384,512]{1,0:T(8,128)(2,1)} %get-tuple-element.23.refs_0_), channel_id=1, source_target_pairs={{0,16},{16,32},{32,48},{48,0},{64,80},{80,96},{96,112},{112,64},{1... | collective-permute-start | bytes 1179656 | tf_op jit(solution)/shard_map/ppermute | solution.py:278
  32.7 38.4 %collective-permute-start.3 = (bf16[384,512]{1,0:T(8,128)(2,1)}, bf16[384,512]{1,0:T(8,128)(2,1)}, u32[]{:S(2)}, u32[]{:S(2)}) collective-permute-start(bf16[384,512]{1,0:T(8,128)(2,1)} %get-tuple-element.23.refs_0_), channel_id=1, source_target_pairs={{0,32},{16,48},{32,0},{48,16},{64,96},{80,112},{96,64},{112,80},{1... | collective-permute-start | bytes 1179656 | tf_op jit(solution)/shard_map/ppermute | solution.py:278
  43.2 27.8 %copy-start.3 = (bf16[384,512]{1,0:T(8,128)(2,1)}, bf16[384,512]{1,0:T(8,128)(2,1)S(1)}, u32[]{:S(2)}) copy-start(bf16[384,512]{1,0:T(8,128)(2,1)S(1)} %collective-permute-done.4.refs_4_) | copy-start | bytes 1179652
  43.2 27.8 %collective-permute-start.7 = (bf16[384,512]{1,0:T(8,128)(2,1)S(1)}, bf16[384,512]{1,0:T(8,128)(2,1)}, u32[]{:S(2)}, u32[]{:S(2)}) collective-permute-start(bf16[384,512]{1,0:T(8,128)(2,1)S(1)} %collective-permute-done.4.refs_4_), channel_id=1, source_target_pairs={{0,32},{16,48},{32,0},{48,16},{64,96},{80,112},{96,64},{112,80},{1... | collective-permute-start | bytes 1179656 | tf_op jit(solution)/shard_map/ppermute | solution.py:278
  48.1 23.0 %collective-permute-start.6 = (bf16[384,512]{1,0:T(8,128)(2,1)S(1)}, bf16[384,512]{1,0:T(8,128)(2,1)}, u32[]{:S(2)}, u32[]{:S(2)}) collective-permute-start(bf16[384,512]{1,0:T(8,128)(2,1)S(1)} %collective-permute-done.4.refs_4_), channel_id=1, source_target_pairs={{0,48},{16,0},{32,16},{48,32},{64,112},{80,64},{96,80},{112,96},{1... | collective-permute-start | bytes 1179656 | tf_op jit(solution)/shard_map/ppermute | solution.py:278
  50.9 20.2 %copy-start.4 = (bf16[384,512]{1,0:T(8,128)(2,1)}, bf16[384,512]{1,0:T(8,128)(2,1)S(1)}, u32[]{:S(2)}) copy-start(bf16[384,512]{1,0:T(8,128)(2,1)S(1)} %collective-permute-done.2.refs_2_) | copy-start | bytes 1179652
  50.9 20.1 %collective-permute-start.5 = (bf16[384,512]{1,0:T(8,128)(2,1)S(1)}, bf16[384,512]{1,0:T(8,128)(2,1)}, u32[]{:S(2)}, u32[]{:S(2)}) collective-permute-start(bf16[384,512]{1,0:T(8,128)(2,1)S(1)} %collective-permute-done.4.refs_4_), channel_id=1, source_target_pairs={{0,16},{16,32},{32,48},{48,0},{64,80},{80,96},{96,112},{112,64},{1... | collective-permute-start | bytes 1179656 | tf_op jit(solution)/shard_map/ppermute | solution.py:278
  53.4 8.8 %copy-start.5 = (bf16[384,512]{1,0:T(8,128)(2,1)}, bf16[384,512]{1,0:T(8,128)(2,1)S(1)}, u32[]{:S(2)}) copy-start(bf16[384,512]{1,0:T(8,128)(2,1)S(1)} %collective-permute-done.1.refs_1_) | copy-start | bytes 1179652
  53.4 17.6 %collective-permute-start.8 = (bf16[384,256]{1,0:T(8,128)(2,1)}, bf16[384,256]{1,0:T(8,128)(2,1)}, u32[]{:S(2)}, u32[]{:S(2)}) collective-permute-start(bf16[384,256]{1,0:T(8,128)(2,1)} %get-tuple-element.28.refs_8_), channel_id=1, source_target_pairs={{0,256},{16,272},{32,288},{48,304},{64,320},{80,336},{96,352},{112... | collective-permute-start | bytes 589832 | tf_op jit(solution)/shard_map/ppermute | solution.py:281
  77.2 17.5 %collective-permute-start.9 = (bf16[416,256]{1,0:T(8,128)(2,1)}, bf16[416,256]{1,0:T(8,128)(2,1)S(1)}, u32[]{:S(2)}, u32[]{:S(2)}) collective-permute-start(bf16[416,256]{1,0:T(8,128)(2,1)} %attend.2), channel_id=1, source_target_pairs={{0,256},{16,272},{32,288},{48,304},{64,320},{80,336},{96,352},{112... | collective-permute-start | bytes 638984 | tf_op jit(solution)/shard_map/ppermute | solution.py:281
  94.7 0.7 copy-start.7
  98.5 27.3 %all-to-all-start.1 = ((bf16[16,192,128]{2,1,0:T(8,128)(2,1)}), bf16[16,192,128]{2,1,0:T(8,128)(2,1)S(1)}, u32[]{:S(2)}, u32[]{:S(2)}) async-start(bf16[16,192,128]{2,1,0:T(8,128)(2,1)} %merge.1), calls=%async_computation.1 | async-start | bytes 1572864 | tf_op jit(solution)/shard_map/all_to_all | solution.py:275
  112.8 6.9 %collective-permute-start.10 = (bf16[4,256,1280]{2,1,0:T(8,128)(2,1)S(1)}, bf16[4,256,1280]{2,1,0:T(8,128)(2,1)}, u32[]{:S(2)}, u32[]{:S(2)}) collective-permute-start(bf16[4,256,1280]{2,1,0:T(8,128)(2,1)S(1)} %all-to-all-done.w_own), channel_id=1, source_target_pairs={{0,1},{1,0},{2,3},{3,2},{4,5},{5,4},{6,7},{7,6},{8,9},{9,8},{10,11... | collective-permute-start | bytes 7864328 | tf_op jit(solution)/shard_map/ppermute | solution.py:348
  128.5 20.4 %collective-permute-start.11 = (bf16[192,320]{1,0:T(8,128)(2,1)S(1)}, bf16[192,320]{1,0:T(8,128)(2,1)S(1)}, u32[]{:S(2)}, u32[]{:S(2)}) collective-permute-start(bf16[192,320]{1,0:T(8,128)(2,1)S(1)} %get-tuple-element.31), channel_id=1, source_target_pairs={{0,2},{1,3},{2,0},{3,1},{4,6},{5,7},{6,4},{7,5},{8,10},{9,11},{10,... | collective-permute-start | bytes 368648 | tf_op jit(solution)/shard_map/ppermute | solution.py:375
  141.0 7.9 %copy-start.8 = (f32[320]{0:T(512)S(1)}, f32[320]{0:T(512)}, u32[]{:S(2)}) copy-start(f32[320]{0:T(512)} %param.19) | copy-start | bytes 3844
  141.0 29.8 %copy-start = (bf16[192,320]{1,0:T(8,128)(2,1)S(1)}, bf16[192,320]{1,0:T(8,128)(2,1)}, u32[]{:S(2)}) copy-start(bf16[192,320]{1,0:T(8,128)(2,1)} %tokens.1) | copy-start | bytes 368644
  141.0 29.8 %copy-start.1 = (bf16[192,320]{1,0:T(8,128)(2,1)S(1)}, bf16[192,320]{1,0:T(8,128)(2,1)}, u32[]{:S(2)}) copy-start(bf16[192,320]{1,0:T(8,128)(2,1)} %d_tokens.1) | copy-start | bytes 368644
  141.0 29.8 %copy-start.2 = (s32[192]{0:T(256)S(1)}, s32[192]{0:T(256)}, u32[]{:S(2)}) copy-start(s32[192]{0:T(256)} %flags.3) | copy-start | bytes 2308
  141.0 29.8 %collective-permute-start.13 = (bf16[192,320]{1,0:T(8,128)(2,1)S(1)}, bf16[192,320]{1,0:T(8,128)(2,1)S(1)}, u32[]{:S(2)}, u32[]{:S(2)}) collective-permute-start(bf16[192,320]{1,0:T(8,128)(2,1)S(1)} %get-tuple-element.33), channel_id=1, source_target_pairs={{0,3},{1,2},{2,1},{3,0},{4,7},{5,6},{6,5},{7,4},{8,11},{9,10},{10,... | collective-permute-start | bytes 368648 | tf_op jit(solution)/shard_map/ppermute | solution.py:376
  146.6 24.2 %collective-permute-start.12 = (bf16[192,320]{1,0:T(8,128)(2,1)S(1)}, bf16[192,320]{1,0:T(8,128)(2,1)S(1)}, u32[]{:S(2)}, u32[]{:S(2)}) collective-permute-start(bf16[192,320]{1,0:T(8,128)(2,1)S(1)} %get-tuple-element.32), channel_id=1, source_target_pairs={{0,1},{1,0},{2,3},{3,2},{4,5},{5,4},{6,7},{7,6},{8,9},{9,8},{10,11... | collective-permute-start | bytes 368648 | tf_op jit(solution)/shard_map/ppermute | solution.py:377

commit v6 on v5

--- a/solution.py
+++ b/solution.py
@@ -130,24 +130,37 @@
     kv, qd, held, sems = refs[10:]
     rows = kv_in[0].shape[0]
     half = rows // 2
-    run_all(
-        [
-            pltpu.make_async_copy(kv_in[i], kv.at[pl.ds(i * rows, rows)], sems.at[i])
-            for i in range(8)
-        ]
-        + [pltpu.make_async_copy(qd_in, qd, sems.at[8])]
-    )
+    copies = [pltpu.make_async_copy(qd_in, qd, sems.at[8])]
+    for i in range(8):
+        copies.append(pltpu.make_async_copy(kv_in[i], kv.at[pl.ds(i * rows, rows)], sems.at[i]))
+    for copy in copies:
+        copy.start()
     contract = (((1,), (1,)), ((), ()))
+    copies[0].wait()
     both = qd[...]
-    scores = lax.dot_general(both[:, HD:], kv[:, :HD], contract, preferred_element_type=F32)
-    slopes = lax.dot_general(both, kv[:, : 2 * HD], contract, preferred_element_type=F32)
-    peak = jnp.max(scores, axis=1, keepdims=True) * (FACTOR * LOG2E)
-    weights = jnp.exp2(scores * (FACTOR * LOG2E) - peak)
-    total = jnp.sum(weights, axis=1, keepdims=True)
-    product = weights * slopes
-    slope = jnp.sum(product, axis=1, keepdims=True)
-    weighted = jnp.dot(weights.astype(BF), kv[:, 2 * HD :], preferred_element_type=F32)
-    tangent = jnp.dot(product.astype(BF), kv[:, 2 * HD : 3 * HD], preferred_element_type=F32)
+    parts = (slice(0, 4 * rows), slice(4 * rows, 8 * rows))
+    scores, slopes = [], []
+    for p, at in enumerate(parts):
+        for copy in copies[1 + 4 * p : 5 + 4 * p]:
+            copy.wait()
+        scores.append(
+            lax.dot_general(both[:, HD:], kv[at, :HD], contract, preferred_element_type=F32)
+        )
+        slopes.append(
+            lax.dot_general(both, kv[at, : 2 * HD], contract, preferred_element_type=F32)
+        )
+    peak = jnp.maximum(*[jnp.max(part, axis=1, keepdims=True) for part in scores])
+    peak = peak * (FACTOR * LOG2E)
+    total, slope, weighted, tangent = 0.0, 0.0, 0.0, 0.0
+    for at, score, d_score in zip(parts, scores, slopes):
+        weights = jnp.exp2(score * (FACTOR * LOG2E) - peak)
+        product = weights * d_score
+        total += jnp.sum(weights, axis=1, keepdims=True)
+        slope += jnp.sum(product, axis=1, keepdims=True)
+        weighted += jnp.dot(weights.astype(BF), kv[at, 2 * HD :], preferred_element_type=F32)
+        tangent += jnp.dot(
+            product.astype(BF), kv[at, 2 * HD : 3 * HD], preferred_element_type=F32
+        )
     inverse = 1.0 / total
     mean = slope * (inverse * FACTOR)
     primal = weighted[:, :HD] * inverse

time: 173 us -> 173 us (level)
  no operation moved by 1% of the time
where the time goes in v6:
time: 173 us; the launch traced here: 172 us
  starting transfers between devices  86.2 us (50%)
  waiting for transfers between devices  53.6 us (31%)
  Pallas kernels  29.6 us (17%)
    ppermute x4, starting transfers between devices, z(): return lax.ppermute(a, TM, over_z(k))  25.6 us
    ppermute x1, waiting for transfers between devices, per_device(): both_got = lax.ppermute(both_send, MP, flip(3))  21.9 us
    ppermute x4, waiting for transfers between devices, z(): return lax.ppermute(a, TM, over_z(k))  20.9 us
    all_to_all x2, starting transfers between devices, exchange(): return lax.all_to_all(a, axes, 0, 0, tiled=True)  20.8 us
    ppermute x6, starting transfers between devices, y(): return lax.ppermute(a, TM, over_y(k))  20.2 us
    ppermute x1, starting transfers between devices, per_device(): z_got = lax.ppermute(z_send, MP, flip(2))  12.5 us
    pallas_call x2, Pallas kernels, attend(): pl.pallas_call(attend_kernel, out_shape=part, in_specs=[HBM_SPEC] * 9, ou...  11.8 us
    all_to_all x2, waiting for transfers between devices, exchange(): return lax.all_to_all(a, axes, 0, 0, tiled=True)  6.06 us
  transfers between devices with their start and end apart: 16, of which 7 were waited for; matrix products, arithmetic and copies ran while one was open for 0% of the time, Pallas kernels for 8%

profile of v6, /device:TPU:1, one launch (start us, length us, event | category | flops | bytes accessed | tf_op | source)
XLA Modules:
  0.0 172.0 jit_solution(351386057485798192)
XLA Ops:
  0.7 2.8 %pack.1 = (bf16[384,256]{1,0:T(8,128)(2,1)}, bf16[384,512]{1,0:T(8,128)(2,1)}, bf16[192,768]{1,0:T(8,128)(2,1)}) custom-call(s32[1]{0:T(128)} %bitcast.2.odd, s32[192]{0:T(256)} %flags.3, bf16[192,256]{1,0:T(8,128)(2,1)} %refs_0_.1, bf16[192,256]{1,0:T(8,128)(2,1)} %refs_1_.1, bf16[192,256]{1,0:T(8,128)(2,1)} %refs_2_.1, bf16[192,256]{1,0:T(8,128)(2,1)} %refs_3_.1, ...), custom_call_target="tpu_custom_call" | custom-call | tf_op jit(solution)/shard_map/pack/pallas_call | solution.py:296
  3.5 4.4 %collective-permute-start = (bf16[192,768]{1,0:T(8,128)(2,1)}, bf16[192,768]{1,0:T(8,128)(2,1)S(1)}, u32[]{:S(2)}, u32[]{:S(2)}) collective-permute-start(bf16[192,768]{1,0:T(8,128)(2,1)} %get-tuple-element.18), channel_id=1, source_target_pairs={{0,64},{16,80},{32,96},{48,112},{64,0},{80,16},{96,32},{112,48},{1... | collective-permute-start | bytes 884744 | tf_op jit(solution)/shard_map/ppermute | solution.py:294
  7.9 3.3 %cut.1 = bf16[4,256,1280]{2,1,0:T(8,128)(2,1)} custom-call(bf16[256,5120]{1,0:T(8,128)(2,1)} %w_in), custom_call_target="tpu_custom_call" | custom-call | tf_op jit(solution)/shard_map/cut/pallas_call | solution.py:311
  11.2 1.0 collective-permute-done.got
  12.9 6.5 %all-to-all-start = ((bf16[4,256,1280]{2,1,0:T(8,128)(2,1)}), bf16[4,256,1280]{2,1,0:T(8,128)(2,1)S(1)}, u32[]{:S(2)}, u32[]{:S(2)}) async-start(bf16[4,256,1280]{2,1,0:T(8,128)(2,1)} %cut.1), calls=%async_computation | async-start | bytes 5242880 | tf_op jit(solution)/shard_map/all_to_all | solution.py:288
  19.5 1.7 join.1
  21.2 4.9 %collective-permute-start.4 = (bf16[384,512]{1,0:T(8,128)(2,1)}, bf16[384,512]{1,0:T(8,128)(2,1)S(1)}, u32[]{:S(2)}, u32[]{:S(2)}) collective-permute-start(bf16[384,512]{1,0:T(8,128)(2,1)} %get-tuple-element.23.refs_0_), channel_id=1, source_target_pairs={{0,128},{16,144},{32,160},{48,176},{64,192},{80,208},{96,224},{112... | collective-permute-start | bytes 1179656 | tf_op jit(solution)/shard_map/ppermute | solution.py:294
  26.1 4.6 %collective-permute-start.2 = (bf16[384,512]{1,0:T(8,128)(2,1)}, bf16[384,512]{1,0:T(8,128)(2,1)S(1)}, u32[]{:S(2)}, u32[]{:S(2)}) collective-permute-start(bf16[384,512]{1,0:T(8,128)(2,1)} %get-tuple-element.23.refs_0_), channel_id=1, source_target_pairs={{0,48},{16,0},{32,16},{48,32},{64,112},{80,64},{96,80},{112,96},{1... | collective-permute-start | bytes 1179656 | tf_op jit(solution)/shard_map/ppermute | solution.py:291
  30.7 1.9 %collective-permute-start.1 = (bf16[384,512]{1,0:T(8,128)(2,1)}, bf16[384,512]{1,0:T(8,128)(2,1)S(1)}, u32[]{:S(2)}, u32[]{:S(2)}) collective-permute-start(bf16[384,512]{1,0:T(8,128)(2,1)} %get-tuple-element.23.refs_0_), channel_id=1, source_target_pairs={{0,16},{16,32},{32,48},{48,0},{64,80},{80,96},{96,112},{112,64},{1... | collective-permute-start | bytes 1179656 | tf_op jit(solution)/shard_map/ppermute | solution.py:291
  32.7 3.5 %collective-permute-start.3 = (bf16[384,512]{1,0:T(8,128)(2,1)}, bf16[384,512]{1,0:T(8,128)(2,1)}, u32[]{:S(2)}, u32[]{:S(2)}) collective-permute-start(bf16[384,512]{1,0:T(8,128)(2,1)} %get-tuple-element.23.refs_0_), channel_id=1, source_target_pairs={{0,32},{16,48},{32,0},{48,16},{64,96},{80,112},{96,64},{112,80},{1... | collective-permute-start | bytes 1179656 | tf_op jit(solution)/shard_map/ppermute | solution.py:291
  36.2 7.0 %collective-permute-done.4.refs_4_ = bf16[384,512]{1,0:T(8,128)(2,1)S(1)} collective-permute-done((bf16[384,512]{1,0:T(8,128)(2,1)}, bf16[384,512]{1,0:T(8,128)(2,1)S(1)}, u32[]{:S(2)}, u32[]{:S(2)}) %collective-permute-start.4) | collective-permute-done | bytes 393248 | tf_op jit(solution)/shard_map/ppermute | solution.py:294
  43.2 4.8 %collective-permute-start.7 = (bf16[384,512]{1,0:T(8,128)(2,1)S(1)}, bf16[384,512]{1,0:T(8,128)(2,1)}, u32[]{:S(2)}, u32[]{:S(2)}) collective-permute-start(bf16[384,512]{1,0:T(8,128)(2,1)S(1)} %collective-permute-done.4.refs_4_), channel_id=1, source_target_pairs={{0,32},{16,48},{32,0},{48,16},{64,96},{80,112},{96,64},{112,80},{1... | collective-permute-start | bytes 1179656 | tf_op jit(solution)/shard_map/ppermute | solution.py:291
  48.1 2.8 %collective-permute-start.6 = (bf16[384,512]{1,0:T(8,128)(2,1)S(1)}, bf16[384,512]{1,0:T(8,128)(2,1)}, u32[]{:S(2)}, u32[]{:S(2)}) collective-permute-start(bf16[384,512]{1,0:T(8,128)(2,1)S(1)} %collective-permute-done.4.refs_4_), channel_id=1, source_target_pairs={{0,48},{16,0},{32,16},{48,32},{64,112},{80,64},{96,80},{112,96},{1... | collective-permute-start | bytes 1179656 | tf_op jit(solution)/shard_map/ppermute | solution.py:291
  50.9 2.5 %collective-permute-start.5 = (bf16[384,512]{1,0:T(8,128)(2,1)S(1)}, bf16[384,512]{1,0:T(8,128)(2,1)}, u32[]{:S(2)}, u32[]{:S(2)}) collective-permute-start(bf16[384,512]{1,0:T(8,128)(2,1)S(1)} %collective-permute-done.4.refs_4_), channel_id=1, source_target_pairs={{0,16},{16,32},{32,48},{48,0},{64,80},{80,96},{96,112},{112,64},{1... | collective-permute-start | bytes 1179656 | tf_op jit(solution)/shard_map/ppermute | solution.py:291
  53.4 8.8 %collective-permute-start.8 = (bf16[384,256]{1,0:T(8,128)(2,1)}, bf16[384,256]{1,0:T(8,128)(2,1)}, u32[]{:S(2)}, u32[]{:S(2)}) collective-permute-start(bf16[384,256]{1,0:T(8,128)(2,1)} %get-tuple-element.28.refs_8_), channel_id=1, source_target_pairs={{0,256},{16,272},{32,288},{48,304},{64,320},{80,336},{96,352},{112... | collective-permute-start | bytes 589832 | tf_op jit(solution)/shard_map/ppermute | solution.py:294
  62.2 8.8 %collective-permute-done.8.refs_8_ = bf16[384,256]{1,0:T(8,128)(2,1)} collective-permute-done((bf16[384,256]{1,0:T(8,128)(2,1)}, bf16[384,256]{1,0:T(8,128)(2,1)}, u32[]{:S(2)}, u32[]{:S(2)}) %collective-permute-start.8) | collective-permute-done | bytes 196640 | tf_op jit(solution)/shard_map/ppermute | solution.py:294
  71.1 5.9 %attend.2 = bf16[416,256]{1,0:T(8,128)(2,1)} custom-call(bf16[384,512]{1,0:T(8,128)(2,1)} %get-tuple-element.23.refs_0_, bf16[384,512]{1,0:T(8,128)(2,1)} %copy-done.5, bf16[384,512]{1,0:T(8,128)(2,1)} %copy-done.4, bf16[384,512]{1,0:T(8,128)(2,1)} %collective-permute-done.3.refs_3_, bf16[384,512]{1,0:T(8,128)(2,1)} %copy-done.3, ...), custom_call_target="tpu_custom_call" | custom-call | tf_op jit(solution)/shard_map/attend/pallas_call | solution.py:342
  77.0 7.5 %collective-permute-start.9 = (bf16[416,256]{1,0:T(8,128)(2,1)}, bf16[416,256]{1,0:T(8,128)(2,1)S(1)}, u32[]{:S(2)}, u32[]{:S(2)}) collective-permute-start(bf16[416,256]{1,0:T(8,128)(2,1)} %attend.2), channel_id=1, source_target_pairs={{0,256},{16,272},{32,288},{48,304},{64,320},{80,336},{96,352},{112... | collective-permute-start | bytes 638984 | tf_op jit(solution)/shard_map/ppermute | solution.py:294
  84.4 5.9 %attend.3.one = bf16[416,256]{1,0:T(8,128)(2,1)} custom-call(bf16[384,512]{1,0:T(8,128)(2,1)} %get-tuple-element.23.refs_0_, bf16[384,512]{1,0:T(8,128)(2,1)} %copy-done.5, bf16[384,512]{1,0:T(8,128)(2,1)} %copy-done.4, bf16[384,512]{1,0:T(8,128)(2,1)} %collective-permute-done.3.refs_3_, bf16[384,512]{1,0:T(8,128)(2,1)} %copy-done.3, ...), custom_call_target="tpu_custom_call" | custom-call | tf_op jit(solution)/shard_map/attend/pallas_call | solution.py:342
  90.4 4.1 %collective-permute-done.9.two = bf16[416,256]{1,0:T(8,128)(2,1)S(1)} collective-permute-done((bf16[416,256]{1,0:T(8,128)(2,1)}, bf16[416,256]{1,0:T(8,128)(2,1)S(1)}, u32[]{:S(2)}, u32[]{:S(2)}) %collective-permute-start.9) | collective-permute-done | bytes 213024 | tf_op jit(solution)/shard_map/ppermute | solution.py:294
  95.1 3.1 %merge.1 = bf16[16,192,128]{2,1,0:T(8,128)(2,1)} custom-call(s32[1]{0:T(128)} %bitcast.2.odd, bf16[416,256]{1,0:T(8,128)(2,1)} %attend.3.one, bf16[416,256]{1,0:T(8,128)(2,1)} %copy-done.7), custom_call_target="tpu_custom_call" | custom-call | tf_op jit(solution)/shard_map/merge/pallas_call | solution.py:363
  98.3 14.3 %all-to-all-start.1 = ((bf16[16,192,128]{2,1,0:T(8,128)(2,1)}), bf16[16,192,128]{2,1,0:T(8,128)(2,1)S(1)}, u32[]{:S(2)}, u32[]{:S(2)}) async-start(bf16[16,192,128]{2,1,0:T(8,128)(2,1)} %merge.1), calls=%async_computation.1 | async-start | bytes 1572864 | tf_op jit(solution)/shard_map/all_to_all | solution.py:288
  112.6 2.0 %collective-permute-start.10 = (bf16[4,256,1280]{2,1,0:T(8,128)(2,1)S(1)}, bf16[4,256,1280]{2,1,0:T(8,128)(2,1)}, u32[]{:S(2)}, u32[]{:S(2)}) collective-permute-start(bf16[4,256,1280]{2,1,0:T(8,128)(2,1)S(1)} %all-to-all-done.w_own), channel_id=1, source_target_pairs={{0,1},{1,0},{2,3},{3,2},{4,5},{5,4},{6,7},{7,6},{8,9},{9,8},{10,11... | collective-permute-start | bytes 7864328 | tf_op jit(solution)/shard_map/ppermute | solution.py:361
  114.8 4.7 %collective-permute-done.10.w_other = bf16[4,256,1280]{2,1,0:T(8,128)(2,1)} collective-permute-done((bf16[4,256,1280]{2,1,0:T(8,128)(2,1)S(1)}, bf16[4,256,1280]{2,1,0:T(8,128)(2,1)}, u32[]{:S(2)}, u32[]{:S(2)}) %collective-permute-start.10) | collective-permute-done | bytes 2621472 | tf_op jit(solution)/shard_map/ppermute | solution.py:361
  119.5 6.1 %all-to-all-done.1.acts = bf16[16,192,128]{2,1,0:T(8,128)(2,1)S(1)} async-done(((bf16[16,192,128]{2,1,0:T(8,128)(2,1)}), bf16[16,192,128]{2,1,0:T(8,128)(2,1)S(1)}, u32[]{:S(2)}, u32[]{:S(2)}) %all-to-all-start.1) | async-done | bytes 786464 | tf_op jit(solution)/shard_map/all_to_all | solution.py:288
  125.6 2.7 %project.3 = (bf16[192,320]{1,0:T(8,128)(2,1)S(1)}, bf16[192,320]{1,0:T(8,128)(2,1)S(1)}) custom-call(s32[2]{0:T(128)S(1)} %pad_add_fusion.1.place, bf16[16,192,128]{2,1,0:T(8,128)(2,1)S(1)} %all-to-all-done.1.acts, bf16[4,256,1280]{2,1,0:T(8,128)(2,1)S(1)} %all-to-all-done.w_own, bf16[4,256,1280]{2,1,0:T(8,128)(2,1)} %collective-permute-done.10.w_other), custom_call_target="tpu_custom_call" | custom-call | tf_op jit(solution)/shard_map/project/pallas_call | solution.py:377
  128.3 12.5 %collective-permute-start.11 = (bf16[192,320]{1,0:T(8,128)(2,1)S(1)}, bf16[192,320]{1,0:T(8,128)(2,1)S(1)}, u32[]{:S(2)}, u32[]{:S(2)}) collective-permute-start(bf16[192,320]{1,0:T(8,128)(2,1)S(1)} %get-tuple-element.31), channel_id=1, source_target_pairs={{0,2},{1,3},{2,0},{3,1},{4,6},{5,7},{6,4},{7,5},{8,10},{9,11},{10,... | collective-permute-start | bytes 368648 | tf_op jit(solution)/shard_map/ppermute | solution.py:388
  140.8 2.8 %collective-permute-start.13 = (bf16[192,320]{1,0:T(8,128)(2,1)S(1)}, bf16[192,320]{1,0:T(8,128)(2,1)S(1)}, u32[]{:S(2)}, u32[]{:S(2)}) collective-permute-start(bf16[192,320]{1,0:T(8,128)(2,1)S(1)} %get-tuple-element.33), channel_id=1, source_target_pairs={{0,3},{1,2},{2,1},{3,0},{4,7},{5,6},{6,5},{7,4},{8,11},{9,10},{10,... | collective-permute-start | bytes 368648 | tf_op jit(solution)/shard_map/ppermute | solution.py:389
  143.7 2.7 %project.2 = (f32[192,320]{1,0:T(8,128)S(1)}, bf16[192,320]{1,0:T(8,128)(2,1)S(1)}) custom-call(s32[2]{0:T(128)S(1)} %pad_add_fusion.place, bf16[16,192,128]{2,1,0:T(8,128)(2,1)S(1)} %all-to-all-done.1.acts, bf16[4,256,1280]{2,1,0:T(8,128)(2,1)S(1)} %all-to-all-done.w_own, bf16[4,256,1280]{2,1,0:T(8,128)(2,1)} %collective-permute-done.10.w_other), custom_call_target="tpu_custom_call" | custom-call | tf_op jit(solution)/shard_map/project/pallas_call | solution.py:377
  146.4 2.3 %collective-permute-start.12 = (bf16[192,320]{1,0:T(8,128)(2,1)S(1)}, bf16[192,320]{1,0:T(8,128)(2,1)S(1)}, u32[]{:S(2)}, u32[]{:S(2)}) collective-permute-start(bf16[192,320]{1,0:T(8,128)(2,1)S(1)} %get-tuple-element.32), channel_id=1, source_target_pairs={{0,1},{1,0},{2,3},{3,2},{4,5},{5,4},{6,7},{7,6},{8,9},{9,8},{10,11... | collective-permute-start | bytes 368648 | tf_op jit(solution)/shard_map/ppermute | solution.py:390
  148.7 21.9 %collective-permute-done.13.both_got = bf16[192,320]{1,0:T(8,128)(2,1)S(1)} collective-permute-done((bf16[192,320]{1,0:T(8,128)(2,1)S(1)}, bf16[192,320]{1,0:T(8,128)(2,1)S(1)}, u32[]{:S(2)}, u32[]{:S(2)}) %collective-permute-start.13) | collective-permute-done | bytes 122912 | tf_op jit(solution)/shard_map/ppermute | solution.py:389
  170.6 1.4 finish.1
  (30 shorter events, 1.6 us)
Async XLA Ops:
  3.5 8.7 %collective-permute-start = (bf16[192,768]{1,0:T(8,128)(2,1)}, bf16[192,768]{1,0:T(8,128)(2,1)S(1)}, u32[]{:S(2)}, u32[]{:S(2)}) collective-permute-start(bf16[192,768]{1,0:T(8,128)(2,1)} %get-tuple-element.18), channel_id=1, source_target_pairs={{0,64},{16,80},{32,96},{48,112},{64,0},{80,16},{96,32},{112,48},{1... | collective-permute-start | bytes 884744 | tf_op jit(solution)/shard_map/ppermute | solution.py:294
  12.2 0.7 copy-start.6
  12.9 58.1 %all-to-all-start = ((bf16[4,256,1280]{2,1,0:T(8,128)(2,1)}), bf16[4,256,1280]{2,1,0:T(8,128)(2,1)S(1)}, u32[]{:S(2)}, u32[]{:S(2)}) async-start(bf16[4,256,1280]{2,1,0:T(8,128)(2,1)} %cut.1), calls=%async_computation | async-start | bytes 5242880 | tf_op jit(solution)/shard_map/all_to_all | solution.py:288
  21.2 22.1 %collective-permute-start.4 = (bf16[384,512]{1,0:T(8,128)(2,1)}, bf16[384,512]{1,0:T(8,128)(2,1)S(1)}, u32[]{:S(2)}, u32[]{:S(2)}) collective-permute-start(bf16[384,512]{1,0:T(8,128)(2,1)} %get-tuple-element.23.refs_0_), channel_id=1, source_target_pairs={{0,128},{16,144},{32,160},{48,176},{64,192},{80,208},{96,224},{112... | collective-permute-start | bytes 1179656 | tf_op jit(solution)/shard_map/ppermute | solution.py:294
  26.1 24.8 %collective-permute-start.2 = (bf16[384,512]{1,0:T(8,128)(2,1)}, bf16[384,512]{1,0:T(8,128)(2,1)S(1)}, u32[]{:S(2)}, u32[]{:S(2)}) collective-permute-start(bf16[384,512]{1,0:T(8,128)(2,1)} %get-tuple-element.23.refs_0_), channel_id=1, source_target_pairs={{0,48},{16,0},{32,16},{48,32},{64,112},{80,64},{96,80},{112,96},{1... | collective-permute-start | bytes 1179656 | tf_op jit(solution)/shard_map/ppermute | solution.py:291
  30.7 22.7 %collective-permute-start.1 = (bf16[384,512]{1,0:T(8,128)(2,1)}, bf16[384,512]{1,0:T(8,128)(2,1)S(1)}, u32[]{:S(2)}, u32[]{:S(2)}) collective-permute-start(bf16[384,512]{1,0:T(8,128)(2,1)} %get-tuple-element.23.refs_0_), channel_id=1, source_target_pairs={{0,16},{16,32},{32,48},{48,0},{64,80},{80,96},{96,112},{112,64},{1... | collective-permute-start | bytes 1179656 | tf_op jit(solution)/shard_map/ppermute | solution.py:291
  32.7 38.4 %collective-permute-start.3 = (bf16[384,512]{1,0:T(8,128)(2,1)}, bf16[384,512]{1,0:T(8,128)(2,1)}, u32[]{:S(2)}, u32[]{:S(2)}) collective-permute-start(bf16[384,512]{1,0:T(8,128)(2,1)} %get-tuple-element.23.refs_0_), channel_id=1, source_target_pairs={{0,32},{16,48},{32,0},{48,16},{64,96},{80,112},{96,64},{112,80},{1... | collective-permute-start | bytes 1179656 | tf_op jit(solution)/shard_map/ppermute | solution.py:291
  43.2 27.8 %copy-start.3 = (bf16[384,512]{1,0:T(8,128)(2,1)}, bf16[384,512]{1,0:T(8,128)(2,1)S(1)}, u32[]{:S(2)}) copy-start(bf16[384,512]{1,0:T(8,128)(2,1)S(1)} %collective-permute-done.4.refs_4_) | copy-start | bytes 1179652
  43.2 27.8 %collective-permute-start.7 = (bf16[384,512]{1,0:T(8,128)(2,1)S(1)}, bf16[384,512]{1,0:T(8,128)(2,1)}, u32[]{:S(2)}, u32[]{:S(2)}) collective-permute-start(bf16[384,512]{1,0:T(8,128)(2,1)S(1)} %collective-permute-done.4.refs_4_), channel_id=1, source_target_pairs={{0,32},{16,48},{32,0},{48,16},{64,96},{80,112},{96,64},{112,80},{1... | collective-permute-start | bytes 1179656 | tf_op jit(solution)/shard_map/ppermute | solution.py:291
  48.1 23.0 %collective-permute-start.6 = (bf16[384,512]{1,0:T(8,128)(2,1)S(1)}, bf16[384,512]{1,0:T(8,128)(2,1)}, u32[]{:S(2)}, u32[]{:S(2)}) collective-permute-start(bf16[384,512]{1,0:T(8,128)(2,1)S(1)} %collective-permute-done.4.refs_4_), channel_id=1, source_target_pairs={{0,48},{16,0},{32,16},{48,32},{64,112},{80,64},{96,80},{112,96},{1... | collective-permute-start | bytes 1179656 | tf_op jit(solution)/shard_map/ppermute | solution.py:291
  50.9 20.2 %copy-start.4 = (bf16[384,512]{1,0:T(8,128)(2,1)}, bf16[384,512]{1,0:T(8,128)(2,1)S(1)}, u32[]{:S(2)}) copy-start(bf16[384,512]{1,0:T(8,128)(2,1)S(1)} %collective-permute-done.2.refs_2_) | copy-start | bytes 1179652
  50.9 20.1 %collective-permute-start.5 = (bf16[384,512]{1,0:T(8,128)(2,1)S(1)}, bf16[384,512]{1,0:T(8,128)(2,1)}, u32[]{:S(2)}, u32[]{:S(2)}) collective-permute-start(bf16[384,512]{1,0:T(8,128)(2,1)S(1)} %collective-permute-done.4.refs_4_), channel_id=1, source_target_pairs={{0,16},{16,32},{32,48},{48,0},{64,80},{80,96},{96,112},{112,64},{1... | collective-permute-start | bytes 1179656 | tf_op jit(solution)/shard_map/ppermute | solution.py:291
  53.4 8.8 %copy-start.5 = (bf16[384,512]{1,0:T(8,128)(2,1)}, bf16[384,512]{1,0:T(8,128)(2,1)S(1)}, u32[]{:S(2)}) copy-start(bf16[384,512]{1,0:T(8,128)(2,1)S(1)} %collective-permute-done.1.refs_1_) | copy-start | bytes 1179652
  53.4 17.6 %collective-permute-start.8 = (bf16[384,256]{1,0:T(8,128)(2,1)}, bf16[384,256]{1,0:T(8,128)(2,1)}, u32[]{:S(2)}, u32[]{:S(2)}) collective-permute-start(bf16[384,256]{1,0:T(8,128)(2,1)} %get-tuple-element.28.refs_8_), channel_id=1, source_target_pairs={{0,256},{16,272},{32,288},{48,304},{64,320},{80,336},{96,352},{112... | collective-permute-start | bytes 589832 | tf_op jit(solution)/shard_map/ppermute | solution.py:294
  77.0 17.5 %collective-permute-start.9 = (bf16[416,256]{1,0:T(8,128)(2,1)}, bf16[416,256]{1,0:T(8,128)(2,1)S(1)}, u32[]{:S(2)}, u32[]{:S(2)}) collective-permute-start(bf16[416,256]{1,0:T(8,128)(2,1)} %attend.2), channel_id=1, source_target_pairs={{0,256},{16,272},{32,288},{48,304},{64,320},{80,336},{96,352},{112... | collective-permute-start | bytes 638984 | tf_op jit(solution)/shard_map/ppermute | solution.py:294
  94.5 0.7 copy-start.7
  98.3 27.3 %all-to-all-start.1 = ((bf16[16,192,128]{2,1,0:T(8,128)(2,1)}), bf16[16,192,128]{2,1,0:T(8,128)(2,1)S(1)}, u32[]{:S(2)}, u32[]{:S(2)}) async-start(bf16[16,192,128]{2,1,0:T(8,128)(2,1)} %merge.1), calls=%async_computation.1 | async-start | bytes 1572864 | tf_op jit(solution)/shard_map/all_to_all | solution.py:288
  112.6 6.9 %collective-permute-start.10 = (bf16[4,256,1280]{2,1,0:T(8,128)(2,1)S(1)}, bf16[4,256,1280]{2,1,0:T(8,128)(2,1)}, u32[]{:S(2)}, u32[]{:S(2)}) collective-permute-start(bf16[4,256,1280]{2,1,0:T(8,128)(2,1)S(1)} %all-to-all-done.w_own), channel_id=1, source_target_pairs={{0,1},{1,0},{2,3},{3,2},{4,5},{5,4},{6,7},{7,6},{8,9},{9,8},{10,11... | collective-permute-start | bytes 7864328 | tf_op jit(solution)/shard_map/ppermute | solution.py:361
  128.3 20.4 %collective-permute-start.11 = (bf16[192,320]{1,0:T(8,128)(2,1)S(1)}, bf16[192,320]{1,0:T(8,128)(2,1)S(1)}, u32[]{:S(2)}, u32[]{:S(2)}) collective-permute-start(bf16[192,320]{1,0:T(8,128)(2,1)S(1)} %get-tuple-element.31), channel_id=1, source_target_pairs={{0,2},{1,3},{2,0},{3,1},{4,6},{5,7},{6,4},{7,5},{8,10},{9,11},{10,... | collective-permute-start | bytes 368648 | tf_op jit(solution)/shard_map/ppermute | solution.py:388
  140.8 7.9 %copy-start.8 = (f32[320]{0:T(512)S(1)}, f32[320]{0:T(512)}, u32[]{:S(2)}) copy-start(f32[320]{0:T(512)} %param.19) | copy-start | bytes 3844
  140.8 29.8 %copy-start = (bf16[192,320]{1,0:T(8,128)(2,1)S(1)}, bf16[192,320]{1,0:T(8,128)(2,1)}, u32[]{:S(2)}) copy-start(bf16[192,320]{1,0:T(8,128)(2,1)} %tokens.1) | copy-start | bytes 368644
  140.8 29.8 %copy-start.1 = (bf16[192,320]{1,0:T(8,128)(2,1)S(1)}, bf16[192,320]{1,0:T(8,128)(2,1)}, u32[]{:S(2)}) copy-start(bf16[192,320]{1,0:T(8,128)(2,1)} %d_tokens.1) | copy-start | bytes 368644
  140.8 29.8 %copy-start.2 = (s32[192]{0:T(256)S(1)}, s32[192]{0:T(256)}, u32[]{:S(2)}) copy-start(s32[192]{0:T(256)} %flags.3) | copy-start | bytes 2308
  140.8 29.8 %collective-permute-start.13 = (bf16[192,320]{1,0:T(8,128)(2,1)S(1)}, bf16[192,320]{1,0:T(8,128)(2,1)S(1)}, u32[]{:S(2)}, u32[]{:S(2)}) collective-permute-start(bf16[192,320]{1,0:T(8,128)(2,1)S(1)} %get-tuple-element.33), channel_id=1, source_target_pairs={{0,3},{1,2},{2,1},{3,0},{4,7},{5,6},{6,5},{7,4},{8,11},{9,10},{10,... | collective-permute-start | bytes 368648 | tf_op jit(solution)/shard_map/ppermute | solution.py:389
  146.4 24.2 %collective-permute-start.12 = (bf16[192,320]{1,0:T(8,128)(2,1)S(1)}, bf16[192,320]{1,0:T(8,128)(2,1)S(1)}, u32[]{:S(2)}, u32[]{:S(2)}) collective-permute-start(bf16[192,320]{1,0:T(8,128)(2,1)S(1)} %get-tuple-element.32), channel_id=1, source_target_pairs={{0,1},{1,0},{2,3},{3,2},{4,5},{5,4},{6,7},{7,6},{8,9},{9,8},{10,11... | collective-permute-start | bytes 368648 | tf_op jit(solution)/shard_map/ppermute | solution.py:390
